TPU v7x, 32 devices: a whole 2x2x4 slice. The times are simulated.
32 devices in a mesh: batch: 4 (over z), own: 8 (over y, x, core).
Axes of the slice: x: 2, y: 2, z: 4, core: 2. Of those that a mesh axis runs over, the one named last changes fastest.
Arguments:
- memory: float32 [8192, 172], P('own'), may hold values from -1.5 to 1.5
- last_update: int32 [8192], P('own'), may hold values from 0 to 999
- src_local: int32 [32768], P(('batch', 'own')), may hold values from 0 to 1023
- edge_feat: bfloat16 [32768, 172], P(('batch', 'own')), may hold values from -6 to 6
- event_time: int32 [32768], P(('batch', 'own')), may hold values from 1000 to 1999
- nbr_owner: int32 [32768, 4], P(('batch', 'own')), may hold values from 0 to 7, all different within a row; in each aligned block of 1024 rows (0 to 1023, 1024 to 2047, ...) at most 1024 rows name the same one
- nbr_ids: int32 [32768, 4, 5], P(('batch', 'own')), may hold values from 0 to 1023
- nbr_mask: int32 [32768, 4, 5], P(('batch', 'own')), may hold values from 0 to 1, as said below
- event_mask: int32 [32768], P(('batch', 'own')), may hold values from 0 to 1
- dest_local: int32 [16384], P(('batch', 'own')), may hold values from 0 to 1023
- target: int32 [32768], P(('batch', 'own')), may hold values from 0 to 4095
- w_msg: float32 [444, 172], replicated, may hold values from -0.25 to 0.25
- w_gru: float32 [2, 172, 516], replicated, may hold values from -0.4375 to 0.4375
- w_square: float32 [4, 172, 172], replicated, may hold values from -0.4375 to 0.4375
- w_key_value: float32 [272, 344], replicated, may hold values from -1.75 to 1.75
- w_output: float32 [344, 172], replicated, may hold values from -0.3125 to 0.3125
- mom_msg: float32 [444, 172], replicated, may hold values from -0.75 to 0.75
- mom_gru: float32 [2, 172, 516], replicated, may hold values from -0.75 to 0.75
- mom_square: float32 [4, 172, 172], replicated, may hold values from -0.75 to 0.75
- mom_key_value: float32 [272, 344], replicated, may hold values from -0.75 to 0.75
- mom_output: float32 [344, 172], replicated, may hold values from -0.75 to 0.75
- avg_msg: float32 [444, 172], replicated, may hold values from -0.25 to 0.25
- avg_gru: float32 [2, 172, 516], replicated, may hold values from -0.4375 to 0.4375
- avg_square: float32 [4, 172, 172], replicated, may hold values from -0.4375 to 0.4375
- avg_key_value: float32 [272, 344], replicated, may hold values from -1.75 to 1.75
- avg_output: float32 [344, 172], replicated, may hold values from -0.3125 to 0.3125
Outputs:
- loss_sum: float32 [], replicated
- positives: float32 [], replicated
- new_last: int32 [8192], P('own')
- new_mom_msg: float32 [444, 172], replicated
- new_mom_gru: float32 [2, 172, 516], replicated
- new_mom_square: float32 [4, 172, 172], replicated
- new_mom_key_value: float32 [272, 344], replicated
- new_mom_output: float32 [344, 172], replicated
- new_w_msg: float32 [444, 172], replicated
- new_w_gru: float32 [2, 172, 516], replicated
- new_w_square: float32 [4, 172, 172], replicated
- new_w_key_value: float32 [272, 344], replicated
- new_w_output: float32 [344, 172], replicated
- new_avg_msg: float32 [444, 172], replicated
- new_avg_gru: float32 [2, 172, 516], replicated
- new_avg_square: float32 [4, 172, 172], replicated
- new_avg_key_value: float32 [272, 344], replicated
- new_avg_output: float32 [344, 172], replicated
Inputs may be any that keep to these rules, and one draw needn't show every extreme that they name: `nbr_owner`: each row names 4 different owners; the rows of one device name one owner 1024 times at the most, and exactly 1024 times in some devices. `nbr_mask`: the first slot of the first owner of every event is live.
All inputs are finite; a program needn't handle non-finite values.
Results may differ from a plain program's by a relative error of at most 0.0018.
The roundings to bfloat16 on the way count: a program that leaves them out, or rounds other values in their place, can miss the bound.
Values may be sent and summed in bfloat16 or wider, within the bound.
A program may use at most 192 MiB of HBM per device.

v0:
```python
from functools import partial
import math

import jax
import jax.numpy as jnp
from jax import lax
from jax.sharding import PartitionSpec as P

HEADS = 2


mu_coef = 0.9
avg_coef = 0.1
rate_coef = 0.008
mask_fill = -1e30


def time_code(delta, time_width):
    frequency = 1.0 / 10.0 ** jnp.linspace(0.0, 9.0, time_width, dtype=jnp.float32)
    return jnp.cos(delta[..., None] * frequency)


def silu_grad(pre_act):
    sigmoid_val = jax.nn.sigmoid(pre_act)
    return sigmoid_val * (1.0 + pre_act * (1.0 - sigmoid_val))


def product(left_side, right_side):
    return jnp.dot(left_side, right_side, preferred_element_type=jnp.float32)


def product_left(left_side, right_side):
    return lax.dot_general(
        left_side, right_side, (((0,), (0,)), ((), ())), preferred_element_type=jnp.float32
    )


def product_right(left_side, right_side):
    return lax.dot_general(
        left_side, right_side, (((1,), (1,)), ((), ())), preferred_element_type=jnp.float32
    )


def nesterov(weight, gradient, moment, average, step_rate):
    new_moment = mu_coef * moment + gradient
    new_weight = weight - step_rate * (gradient + mu_coef * new_moment)
    return (new_moment, new_weight, (1.0 - avg_coef) * average + avg_coef * new_weight)


def bucket_slots(pair_owner, owners, capacity):
    onehot = (pair_owner[:, None] == jnp.arange(owners, dtype=jnp.int32)[None, :]).astype(jnp.int32)
    position = jnp.sum((jnp.cumsum(onehot, 0) - onehot) * onehot, 1)
    return pair_owner * capacity + position


def to_buckets(values, slot_index, owners, capacity, fill_value):
    buffer = jnp.full((owners * capacity,) + values.shape[1:], fill_value, values.dtype)
    return buffer.at[slot_index].set(values).reshape((owners, capacity) + values.shape[1:])


def from_buckets(buffer, slot_index):
    return buffer.reshape((-1,) + buffer.shape[2:])[slot_index]


def gru_gates(gate_in, gate_hid, mem_src):
    gate_width = mem_src.shape[1]
    reset_gate = jax.nn.sigmoid(gate_in[:, :gate_width] + gate_hid[:, :gate_width])
    update = jax.nn.sigmoid(
        gate_in[:, gate_width : 2 * gate_width] + gate_hid[:, gate_width : 2 * gate_width]
    )
    candidate = jnp.tanh(gate_in[:, 2 * gate_width :] + reset_gate * gate_hid[:, 2 * gate_width :])
    return (reset_gate, update, candidate, (1.0 - update) * candidate + update * mem_src)


def node_lookup(node_mem, node_last, safe_ids):
    table_rows = node_mem.shape[0]
    flat_ids = safe_ids.reshape(-1)
    selector = flat_ids[:, None] == jnp.arange(table_rows, dtype=jnp.int32)[None, :]
    mem_rows = product(selector.astype(jnp.bfloat16), node_mem.astype(jnp.bfloat16))
    last_rows = jnp.sum(jnp.where(selector, node_last[None, :], 0), 1)
    return (
        mem_rows.reshape(safe_ids.shape + (node_mem.shape[1],)),
        last_rows.reshape(safe_ids.shape),
    )


def key_parts(node_mem, node_last, low_kv, head_dim, block_data):
    block_query, block_ids, block_time = block_data
    row_count, slot_count = block_ids.shape
    feature_width = block_query.shape[-1]
    head_count = feature_width // head_dim
    is_valid = block_ids >= 0
    safe_ids = jnp.where(is_valid, block_ids, 0)
    mem_rows, last_rows = node_lookup(node_mem, node_last, safe_ids)
    delta_key = (block_time[:, None] - last_rows).astype(jnp.float32)
    time_width = low_kv.shape[0] - feature_width
    inputs = jnp.concatenate([mem_rows, time_code(delta_key, time_width)], -1).astype(jnp.bfloat16)
    pair_kv = jnp.einsum("rse,ef->rsf", inputs, low_kv, preferred_element_type=jnp.float32)
    key_rows = (
        pair_kv[..., :feature_width]
        .astype(jnp.bfloat16)
        .reshape(row_count, slot_count, head_count, head_dim)
    )
    value_rows = (
        pair_kv[..., feature_width:]
        .astype(jnp.bfloat16)
        .reshape(row_count, slot_count, head_count, head_dim)
    )
    query_heads = block_query.reshape(row_count, head_count, head_dim)
    scores = jnp.einsum(
        "rhd,rshd->rsh", query_heads, key_rows, preferred_element_type=jnp.float32
    ) * head_dim ** (-0.5)
    scores = jnp.where(is_valid[..., None], scores, mask_fill)
    return (inputs, is_valid, query_heads, key_rows, value_rows, scores)


def attention_forward(node_mem, node_last, low_kv, head_dim, block_data):
    inputs, is_valid, query_heads, key_rows, value_rows, scores = key_parts(
        node_mem, node_last, low_kv, head_dim, block_data
    )
    row_max = jnp.max(scores, 1)
    weights = jnp.where(is_valid[..., None], jnp.exp(scores - row_max[:, None]), 0.0)
    totals = jnp.sum(weights, 1)
    partial_sum = jnp.einsum("rsh,rshd->rhd", weights, value_rows.astype(jnp.float32))
    return (row_max, totals, partial_sum.reshape(partial_sum.shape[0], -1))


def attention_backward(node_mem, node_last, low_kv, head_dim, grad_kv, block_data):
    inputs, is_valid, query_heads, key_rows, value_rows, scores = key_parts(
        node_mem, node_last, low_kv, head_dim, block_data[:3]
    )
    block_grad, block_dot, block_lse = block_data[3:]
    row_count, slot_count = scores.shape[:2]
    probs = jnp.where(is_valid[..., None], jnp.exp(scores - block_lse[:, None, :]), 0.0)
    grad_heads = block_grad.reshape(query_heads.shape)
    grad_probs = jnp.einsum("rhd,rshd->rsh", grad_heads, value_rows.astype(jnp.float32))
    grad_scores = probs * (grad_probs - block_dot[:, None, :]) * head_dim ** (-0.5)
    grad_query = jnp.einsum("rsh,rshd->rhd", grad_scores, key_rows.astype(jnp.float32))
    grad_keys = grad_scores[..., None] * query_heads[:, None].astype(jnp.float32)
    grad_values = probs[..., None] * grad_heads[:, None]
    grad_pair = jnp.concatenate(
        [
            grad_keys.reshape(row_count, slot_count, -1),
            grad_values.reshape(row_count, slot_count, -1),
        ],
        -1,
    ).astype(jnp.bfloat16)
    grad_kv = grad_kv + jnp.einsum(
        "rse,rsf->ef", inputs, grad_pair, preferred_element_type=jnp.float32
    )
    return (grad_kv, grad_query.reshape(row_count, -1))


def local(
    memory,
    last_update,
    src_local,
    edge_feat,
    event_time,
    nbr_owner,
    nbr_ids,
    nbr_mask,
    event_mask,
    dest_local,
    target,
    w_msg,
    w_gru,
    w_square,
    w_key_value,
    w_output,
    mom_msg,
    mom_gru,
    mom_square,
    mom_key_value,
    mom_output,
    avg_msg,
    avg_gru,
    avg_square,
    avg_key_value,
    avg_output,
):
    owners = lax.axis_size("own")
    events = edge_feat.shape[0]
    feature_width = memory.shape[1]
    pick_count = nbr_ids.shape[1]
    slot_count = nbr_ids.shape[2]
    head_dim = feature_width // HEADS
    capacity = 8 * events // owners
    time_width = w_key_value.shape[0] - feature_width
    low_msg = w_msg.astype(jnp.bfloat16)
    low_gru = w_gru.astype(jnp.bfloat16)
    low_square = w_square.astype(jnp.bfloat16)
    low_kv = w_key_value.astype(jnp.bfloat16)
    low_output = w_output.astype(jnp.bfloat16)
    mask_float = event_mask.astype(jnp.float32)
    positives = jnp.maximum(lax.psum(jnp.sum(mask_float), ("batch", "own")), 1.0)
    new_last = lax.pmax(last_update.at[src_local].max(event_time), "batch")
    mem_src = memory[src_local]
    delta_src = (event_time - last_update[src_local]).astype(jnp.float32)
    x_msg = jnp.concatenate(
        [mem_src, edge_feat.astype(jnp.float32), time_code(delta_src, time_width)], 1
    ).astype(jnp.bfloat16)
    pre_msg = product(x_msg, low_msg)
    hidden = jax.nn.silu(pre_msg).astype(jnp.bfloat16)
    mem_low = mem_src.astype(jnp.bfloat16)
    gate_hid = product(mem_low, low_gru[1])
    reset_gate, update, candidate, fresh_mem = gru_gates(
        product(hidden, low_gru[0]), gate_hid, mem_src
    )
    fresh_low = fresh_mem.astype(jnp.bfloat16)
    queries = product(fresh_low, low_square[0]).astype(jnp.bfloat16)
    pair_slot = bucket_slots(nbr_owner.reshape(-1), owners, capacity)
    pair_ids = jnp.where(nbr_mask > 0, nbr_ids, -1).reshape(-1, slot_count)
    send_query = to_buckets(jnp.repeat(queries, pick_count, 0), pair_slot, owners, capacity, 0.0)
    send_ids = to_buckets(pair_ids, pair_slot, owners, capacity, -1)
    send_time = to_buckets(jnp.repeat(event_time, pick_count), pair_slot, owners, capacity, 0)
    got_query, got_ids, got_time = (
        lax.all_to_all(send_query, "own", split_axis=0, concat_axis=0, tiled=True),
        lax.all_to_all(send_ids, "own", split_axis=0, concat_axis=0, tiled=True),
        lax.all_to_all(send_time, "own", split_axis=0, concat_axis=0, tiled=True),
    )
    owner_blocks = (
        got_query.reshape(8, events, feature_width),
        got_ids.reshape(8, events, slot_count),
        got_time.reshape(8, events),
    )
    part_max, part_total, part_sum = lax.map(
        partial(attention_forward, memory, last_update, low_kv, head_dim), owner_blocks
    )
    back_max, back_total, back_sum = (
        lax.all_to_all(
            part_max.reshape(owners, capacity, HEADS),
            "own",
            split_axis=0,
            concat_axis=0,
            tiled=True,
        ),
        lax.all_to_all(
            part_total.reshape(owners, capacity, HEADS),
            "own",
            split_axis=0,
            concat_axis=0,
            tiled=True,
        ),
        lax.all_to_all(
            part_sum.reshape(owners, capacity, feature_width),
            "own",
            split_axis=0,
            concat_axis=0,
            tiled=True,
        ),
    )
    pair_max = from_buckets(back_max, pair_slot).reshape(events, pick_count, HEADS)
    pair_total = from_buckets(back_total, pair_slot).reshape(events, pick_count, HEADS)
    pair_sum = from_buckets(back_sum, pair_slot).reshape(events, pick_count, HEADS, head_dim)
    merged_max = jnp.max(pair_max, 1)
    factor = jnp.exp(pair_max - merged_max[:, None])
    merged_total = jnp.sum(pair_total * factor, 1)
    merged_sum = jnp.sum(pair_sum * factor[..., None], 1)
    attended = (merged_sum / merged_total[..., None]).reshape(events, feature_width)
    log_total = merged_max + jnp.log(merged_total)
    attended_low = attended.astype(jnp.bfloat16)
    x_out = jnp.concatenate([product(attended_low, low_square[1]), fresh_mem], 1).astype(
        jnp.bfloat16
    )
    pre_out = product(x_out, low_output)
    hidden_out = jax.nn.silu(pre_out).astype(jnp.bfloat16)
    embedding = product(hidden_out, low_square[2]).astype(jnp.bfloat16)
    dest_rows = memory[dest_local].astype(jnp.bfloat16)
    dest_emb = lax.all_gather(
        product(dest_rows, low_square[3]).astype(jnp.bfloat16), "own", axis=0, tiled=True
    )
    cand_total = dest_emb.shape[0]
    cand_block = min(cand_total, 4096)
    block_count = cand_total // cand_block
    dest_blocks = (
        dest_emb.reshape(block_count, cand_block, feature_width),
        jnp.arange(block_count, dtype=jnp.int32) * cand_block,
    )

    def lse_step(carry, block_data):
        run_max, run_total = carry
        logits = product_right(embedding, block_data[0])
        new_max = jnp.maximum(run_max, jnp.max(logits, 1))
        run_total = run_total * jnp.exp(run_max - new_max) + jnp.sum(
            jnp.exp(logits - new_max[:, None]), 1
        )
        return ((new_max, run_total), None)

    initial = (jnp.full((events,), mask_fill, jnp.float32), jnp.zeros((events,), jnp.float32))
    (run_max, run_total), unused = lax.scan(lse_step, initial, dest_blocks)
    log_sum = run_max + jnp.log(run_total)
    picked = jnp.sum(embedding.astype(jnp.float32) * dest_emb[target].astype(jnp.float32), 1)
    loss_local = jnp.sum(mask_float * (log_sum - picked))
    coeff_rows = mask_float / positives

    def loss_back(grad_embed, block_data):
        block_emb, block_start = block_data
        logits = product_right(embedding, block_emb)
        target_hit = (
            target[:, None] == block_start + jnp.arange(cand_block, dtype=jnp.int32)[None, :]
        ).astype(jnp.float32)
        grad_logits = (
            coeff_rows[:, None] * (jnp.exp(logits - log_sum[:, None]) - target_hit)
        ).astype(jnp.bfloat16)
        return (
            grad_embed + product(grad_logits, block_emb),
            product_left(grad_logits, embedding).astype(jnp.bfloat16),
        )

    grad_embed, grad_dest = lax.scan(
        loss_back, jnp.zeros((events, feature_width), jnp.float32), dest_blocks
    )
    grad_dest = grad_dest.reshape(cand_total, feature_width)
    dest_sum = lax.psum_scatter(
        grad_dest.astype(jnp.float32).astype(jnp.bfloat16), "own", scatter_dimension=0, tiled=True
    ).astype(jnp.float32)
    grad_w_dest = lax.dot_general(
        dest_rows.astype(jnp.float32),
        dest_sum,
        (((0,), (0,)), ((), ())),
        precision=lax.Precision.HIGHEST,
    )
    grad_embed_low = grad_embed.astype(jnp.bfloat16)
    grad_sq_embed = product_left(hidden_out, grad_embed_low)
    grad_pre_out = (product_right(grad_embed_low, low_square[2]) * silu_grad(pre_out)).astype(
        jnp.bfloat16
    )
    grad_out = product_left(x_out, grad_pre_out)
    grad_x_out = product_right(grad_pre_out, low_output)
    grad_mixed = grad_x_out[:, :feature_width].astype(jnp.bfloat16)
    grad_fresh = grad_x_out[:, feature_width:]
    grad_sq_mixed = product_left(attended_low, grad_mixed)
    grad_att = product_right(grad_mixed, low_square[1]).astype(jnp.bfloat16)
    grad_att_float = grad_att.astype(jnp.float32)
    att_dot = jnp.sum((grad_att_float * attended).reshape(events, HEADS, head_dim), 2)
    zeros_kv = jnp.zeros(w_key_value.shape, jnp.float32)
    send_grad = to_buckets(
        jnp.repeat(grad_att_float, pick_count, 0), pair_slot, owners, capacity, 0.0
    )
    send_dot = to_buckets(jnp.repeat(att_dot, pick_count, 0), pair_slot, owners, capacity, 0.0)
    send_lse = to_buckets(jnp.repeat(log_total, pick_count, 0), pair_slot, owners, capacity, 0.0)
    got_grad, got_dot, got_lse = (
        lax.all_to_all(
            send_grad.astype(jnp.bfloat16), "own", split_axis=0, concat_axis=0, tiled=True
        ).astype(send_grad.dtype),
        lax.all_to_all(
            send_dot.astype(jnp.bfloat16), "own", split_axis=0, concat_axis=0, tiled=True
        ).astype(send_dot.dtype),
        lax.all_to_all(
            send_lse.astype(jnp.bfloat16), "own", split_axis=0, concat_axis=0, tiled=True
        ).astype(send_lse.dtype),
    )
    grad_blocks = owner_blocks + (
        got_grad.reshape(8, events, feature_width),
        got_dot.reshape(8, events, HEADS),
        got_lse.reshape(8, events, HEADS),
    )
    grad_kv, owner_grads = lax.scan(
        partial(attention_backward, memory, last_update, low_kv, head_dim), zeros_kv, grad_blocks
    )
    back_query = lax.all_to_all(
        owner_grads.reshape(owners, capacity, feature_width).astype(jnp.bfloat16),
        "own",
        split_axis=0,
        concat_axis=0,
        tiled=True,
    ).astype(jnp.float32)
    grad_query = jnp.sum(
        from_buckets(back_query, pair_slot).reshape(events, pick_count, feature_width), 1
    )
    grad_query = grad_query.astype(jnp.bfloat16)
    grad_sq_query = product_left(fresh_low, grad_query)
    grad_fresh = grad_fresh + product_right(grad_query, low_square[0])
    grad_act = grad_fresh * (1.0 - update) * (1.0 - candidate * candidate)
    grad_reset_pre = grad_act * gate_hid[:, 2 * feature_width :] * reset_gate * (1.0 - reset_gate)
    grad_update_pre = grad_fresh * (mem_src - candidate) * update * (1.0 - update)
    grad_gate_in = jnp.concatenate([grad_reset_pre, grad_update_pre, grad_act], 1).astype(
        jnp.bfloat16
    )
    grad_gate_hid = jnp.concatenate(
        [grad_reset_pre, grad_update_pre, grad_act * reset_gate], 1
    ).astype(jnp.bfloat16)
    grad_gru = jnp.stack([product_left(hidden, grad_gate_in), product_left(mem_low, grad_gate_hid)])
    grad_pre_msg = (product_right(grad_gate_in, low_gru[0]) * silu_grad(pre_msg)).astype(
        jnp.bfloat16
    )
    grad_msg = product_left(x_msg, grad_pre_msg)
    grad_square = jnp.stack([grad_sq_query, grad_sq_mixed, grad_sq_embed, grad_w_dest])
    summed = lax.psum(
        (grad_msg, grad_gru, grad_square, grad_kv, grad_out, loss_local), ("batch", "own")
    )
    step_rate = rate_coef * math.sqrt(events * owners * lax.axis_size("batch"))
    params = (w_msg, w_gru, w_square, w_key_value, w_output)
    moments = (mom_msg, mom_gru, mom_square, mom_key_value, mom_output)
    averages = (avg_msg, avg_gru, avg_square, avg_key_value, avg_output)
    states = [
        nesterov(params[index], summed[index], moments[index], averages[index], step_rate)
        for index in range(5)
    ]
    return (
        summed[5],
        positives,
        new_last,
        states[0][0],
        states[1][0],
        states[2][0],
        states[3][0],
        states[4][0],
        states[0][1],
        states[1][1],
        states[2][1],
        states[3][1],
        states[4][1],
        states[0][2],
        states[1][2],
        states[2][2],
        states[3][2],
        states[4][2],
    )


def solution(mesh):
    placed = (
        P("own", None),
        P("own"),
        P(("batch", "own")),
        P(("batch", "own"), None),
        P(("batch", "own")),
        P(("batch", "own"), None),
        P(("batch", "own"), None, None),
        P(("batch", "own"), None, None),
        P(("batch", "own")),
        P(("batch", "own")),
        P(("batch", "own")),
        P(),
        P(),
        P(),
        P(),
        P(),
        P(),
        P(),
        P(),
        P(),
        P(),
        P(),
        P(),
        P(),
        P(),
        P(),
    )
    return jax.shard_map(
        local,
        mesh=mesh,
        in_specs=placed,
        out_specs=(
            P(),
            P(),
            P("own"),
            P(),
            P(),
            P(),
            P(),
            P(),
            P(),
            P(),
            P(),
            P(),
            P(),
            P(),
            P(),
            P(),
            P(),
            P(),
        ),
        check_vma=False,
    )
```

profile of v0, /device:TPU:0, one launch (start us, length us, event | category | flops | bytes accessed | tf_op | source)
XLA Modules:
  0.0 1774.9 jit_solution(9035706413077455453)
XLA Ops:
  14.4 16.1 scatter_custom_fusion.1
  58.1 12.9 scatter_custom_fusion
  85.6 20.9 %scatter_custom_fusion.2 = bf16[8192,172]{1,0:T(8,128)(2,1)} fusion(s32[4096]{0:T(1024)} %bitcast.293, bf16[4096,172]{1,0:T(8,128)(2,1)} %reshape.510, bf16[]{:T(256)} %constant.174.clone.1), kind=kCustom, calls=%fused_computation.103 | custom fusion | bytes 2818560 | tf_op jit(solution)/shard_map/scatter | solution.py:58
  118.0 34.3 %all-to-all-done.2 = bf16[8,1024,172]{1,2,0:T(8,128)(2,1)} async-done(((bf16[8,1024,172]{1,2,0:T(8,128)(2,1)}), bf16[8,1024,172]{1,2,0:T(8,128)(2,1)}, u32[]{:S(2)}, u32[]{:S(2)}) %all-to-all-start.2) | async-done | bytes 2818080 | tf_op jit(solution)/shard_map/all_to_all | solution.py:218
  152.3 384.4 %while.43 = (s32[]{:T(128)}, f32[8,1024,2]{1,2,0:T(2,128)}, f32[8,1024,2]{1,2,0:T(2,128)S(1)}, f32[8,1024,172]{1,2,0:T(8,128)}, s32[8,1024,5]{1,2,0:T(8,128)}, /...) while((s32[]{:T(128)}, f32[8,1024,2]{1,2,0:T(2,128)}, ...), condition=%wide.region_10.12_spmd.clone, body=%wide.region_6.11_spmd.sunk.clone | while | flops 2797267456 | bytes 48753192 | solution.py:227
  536.7 8.3 all_to_all.57
  560.1 43.7 %all-gather.2.cloned.1.call-done = bf16[4096,172]{0,1:T(8,128)(2,1)} async-done(((bf16[512,172]{0,1:T(8,128)(2,1)}), bf16[4096,172]{0,1:T(8,128)(2,1)}) %all-gather.2.cloned.1.call-update) | async-done | bytes 1409040 | tf_op jit(solution)/shard_map/all_gather | solution.py:270
  614.5 16.3 gather_fusion.4
  633.4 13.0 gather_fusion.3
  654.4 12.8 scatter_custom_fusion.4
  675.3 8.2 copy.389
  683.5 19.5 %gather_fusion.2 = f32[4096,172]{1,0:T(8,128)} fusion(f32[8192,172]{1,0:T(8,128)} %bitcast.273, s32[4096]{0:T(1024)S(1)} %broadcast_clamp_fusion), kind=kCustom, calls=%fused_computation.2 | custom fusion | bytes 5652480 | tf_op jit(solution)/shard_map/gather | solution.py:62
  709.1 13.1 multiply_reduce_fusion.5
  728.3 8.2 fusion.103
  736.5 8.1 exponential_reduce_fusion
  745.2 41.6 %all-reduce = (f32[]{:T(128)}, f32[]{:T(128)}) all-reduce(f32[]{:T(128)} %get-tuple-element.588, f32[]{:T(128)} %get-tuple-element.587), channel_id=1, replica_groups=mesh['batch'=4,'own'=8] {'batch','own'}, use_global_device_ids=true, to_apply=%region_18.20 | all-reduce | flops 2 | bytes 16 | tf_op jit(solution)/shard_map/psum | solution.py:390
  787.4 9.0 multiply_convert_fusion.2
  805.3 13.0 scatter_custom_fusion.6
  830.3 21.6 %scatter_custom_fusion.5 = f32[8192,172]{1,0:T(8,128)} fusion(s32[4096]{0:T(1024)S(1)} %bitcast.297, f32[4096,172]{1,0:T(8,128)} %reshape.534, f32[]{:T(128)} %constant.173.clone.1), kind=kCustom, calls=%fused_computation.92 | custom fusion | bytes 5636608 | tf_op jit(solution)/shard_map/scatter | solution.py:58
  876.9 32.2 %all-to-all-done.7 = bf16[8,1024,172]{1,2,0:T(8,128)(2,1)S(1)} async-done(((bf16[8,1024,172]{1,2,0:T(8,128)(2,1)}), bf16[8,1024,172]{1,2,0:T(8,128)(2,1)S(1)}, u32[]{:S(2)}, u32[]{:S(2)}) %all-to-all-start.7) | async-done | bytes 2818080 | tf_op jit(solution)/shard_map/all_to_all | solution.py:344
  912.4 590.1 %while.44 = (s32[]{:T(128)}, f32[272,344]{1,0:T(8,128)}, bf16[8,1024,172]{1,2,0:T(8,128)(2,1)}, s32[8,1024,5]{1,2,0:T(8,128)}, bf16[1024,172]{1,0:T(8,128)(2,1)}...) while((s32[]{:T(128)}, f32[272,344]{1,0:T(8,128)}, ...), condition=%wide.region_29.31_spmd.clone.clone, body=%wide.region_27.30_spmd.clone.sunk.clone | while | flops 3774530816 | bytes 122956576 | solution.py:359
  923.0 8.0 cosine_convert_fusion.8
  996.7 8.0 cosine_convert_fusion.8
  1070.4 8.0 cosine_convert_fusion.8
  1144.1 8.0 cosine_convert_fusion.8
  1217.8 8.0 cosine_convert_fusion.8
  1438.9 8.0 cosine_convert_fusion.8
  1519.2 35.3 %reduce-scatter.2.cloned.1.call-done = bf16[512,172]{0,1:T(8,128)(2,1)} async-done(((bf16[4096,172]{0,1:T(8,128)(2,1)}), bf16[512,172]{0,1:T(8,128)(2,1)}) %reduce-scatter.2.cloned.1.call-update) | async-done | bytes 176144 | tf_op jit(solution)/shard_map/reduce_scatter | solution.py:315
  1560.6 8.9 copy.463
  1569.5 19.5 %gather_fusion.7 = f32[4096,172]{1,0:T(8,128)} fusion(f32[8192,172]{1,0:T(8,128)} %bitcast.272, s32[4096]{0:T(1024)S(1)} %copy-done.61), kind=kCustom, calls=%fused_computation.7 | custom fusion | bytes 5652480 | tf_op jit(solution)/shard_map/gather | solution.py:62
  1622.7 9.1 pmax.7
  1631.8 121.7 %all-reduce.4.cloned.1.call-done = (f32[444,172]{0,1:T(8,128)}, f32[2,172,516]{2,1,0:T(8,128)}, f32[4,172,172]{2,1,0:T(8,128)}, f32[272,344]{1,0:T(8,128)}, f32[344,172]{0,1:T(8,128)}) async-done(((f32[444,172]{0,1:T(8,128)}, f32[2,172,516]{2,1,0:T(8,128)}, f32[4,172,172]{2,1,0:T(8,128)}, f32[272,344]{1,0:T(8,128)}, f32[344,172]{0,1:T(8,128)}), (f32[444,172]{0,1:T(8,128)}, f32[2,172,516]{2,1,0:T(8,128)}, ...) | async-done | bytes 2099792 | tf_op jit(solution)/shard_map/psum | solution.py:390
  (1079 shorter events, 1159.9 us)
Async XLA Ops:
  7.2 29.0 %copy-start.43 = (f32[1024,172]{0,1:T(8,128)S(1)}, f32[1024,172]{0,1:T(8,128)}, u32[]{:S(2)}) copy-start(f32[1024,172]{0,1:T(8,128)} %param.32) | copy-start | bytes 2113540
  7.2 28.4 %copy-start.85 = (s32[1024]{0:T(1024)S(1)}, s32[1024]{0:T(1024)}, u32[]{:S(2)}) copy-start(s32[1024]{0:T(1024)} %param.34) | copy-start | bytes 12292
  14.3 21.3 %copy-start.78 = (s32[4096,1]{0,1:T(1,128)}, s32[4096,1]{0,1:T(1,128)S(1)}, u32[]{:S(2)}) copy-start(s32[4096,1]{0,1:T(1,128)S(1)} %compare_select_fusion.2) | copy-start | bytes 49156
  30.4 44.1 %all-to-all-start.1 = ((s32[8,1,1024]{2,1,0:T(1,128)}), s32[8,1,1024]{2,1,0:T(1,128)S(1)}, u32[]{:S(2)}, u32[]{:S(2)}) async-start(s32[8,1,1024]{2,1,0:T(1,128)} %bitcast.19), calls=%async_computation.1 | async-start | bytes 65536 | tf_op jit(solution)/shard_map/all_to_all | solution.py:220
  36.6 80.7 %copy-start = (f32[1024,172]{1,0:T(8,128)}, f32[1024,172]{1,0:T(8,128)S(1)}, u32[]{:S(2)}) copy-start(f32[1024,172]{1,0:T(8,128)S(1)} %copy.380) | copy-start | bytes 2113540
  54.9 24.2 %copy-start.19 = (bf16[1024,172]{0,1:T(8,128)(2,1)}, bf16[1024,172]{0,1:T(8,128)(2,1)S(1)}, u32[]{:S(2)}) copy-start(bf16[1024,172]{0,1:T(8,128)(2,1)S(1)} %get-tuple-element.666) | copy-start | bytes 1056772
  74.6 38.1 %all-to-all-start = ((s32[8,1024,5]{1,2,0:T(8,128)}), s32[8,1024,5]{1,2,0:T(8,128)}, u32[]{:S(2)}, u32[]{:S(2)}) async-start(s32[8,1024,5]{1,2,0:T(8,128)} %copy.379), calls=%async_computation | async-start | bytes 524288 | tf_op jit(solution)/shard_map/all_to_all | solution.py:219
  112.6 39.7 %all-to-all-start.2 = ((bf16[8,1024,172]{1,2,0:T(8,128)(2,1)}), bf16[8,1024,172]{1,2,0:T(8,128)(2,1)}, u32[]{:S(2)}, u32[]{:S(2)}) async-start(bf16[8,1024,172]{1,2,0:T(8,128)(2,1)} %copy.388), calls=%async_computation.2 | async-start | bytes 5767168 | tf_op jit(solution)/shard_map/all_to_all | solution.py:218
  152.3 15.0 copy-start.50
  200.3 15.0 copy-start.50
  248.4 15.0 copy-start.50
  296.4 15.0 copy-start.50
  344.5 15.0 copy-start.50
  392.5 15.0 copy-start.50
  440.6 15.0 copy-start.50
  488.6 15.0 copy-start.50
  536.7 15.7 copy-start.75
  536.7 15.7 copy-start.52
  552.4 118.7 %all-to-all-start.3 = ((f32[8,1024,172]{1,2,0:T(8,128)}), f32[8,1024,172]{1,2,0:T(8,128)}, u32[]{:S(2)}, u32[]{:S(2)}) async-start(f32[8,1024,172]{1,2,0:T(8,128)} %get-tuple-element.315), calls=%async_computation.3 | async-start | bytes 11534336 | tf_op jit(solution)/shard_map/all_to_all | solution.py:245
  557.2 46.6 %all-gather.2.cloned.1.call-start = ((), (), s32[]{:S(2)}) async-start(), calls=%async_computation.11 | async-start | bytes 1622016 | tf_op jit(solution)/shard_map/all_gather | solution.py:270
  560.1 123.4 %copy-start.60 = (s32[4096]{0:T(1024)}, s32[4096]{0:T(1024)S(1)}, u32[]{:S(2)}) copy-start(s32[4096]{0:T(1024)S(1)} %broadcast_clamp_fusion) | copy-start | bytes 49156
  671.1 189.8 %all-to-all-start.6 = ((bf16[8,1024,2]{1,2,0:T(2,128)(2,1)}), bf16[8,1024,2]{1,2,0:T(2,128)(2,1)}, u32[]{:S(2)}, u32[]{:S(2)}) async-start(bf16[8,1024,2]{1,2,0:T(2,128)(2,1)} %bitcast.34), calls=%async_computation.6 | async-start | bytes 65536 | tf_op jit(solution)/shard_map/all_to_all | solution.py:350
  725.3 75.9 %copy-start.12 = (f32[1024,172]{0,1:T(8,128)}, f32[1024,172]{0,1:T(8,128)S(1)}, u32[]{:S(2)}) copy-start(f32[1024,172]{0,1:T(8,128)S(1)} %div.57) | copy-start | bytes 2113540
  860.9 9.0 all-to-all-start.8
  869.9 39.3 %all-to-all-start.7 = ((bf16[8,1024,172]{1,2,0:T(8,128)(2,1)}), bf16[8,1024,172]{1,2,0:T(8,128)(2,1)S(1)}, u32[]{:S(2)}, u32[]{:S(2)}) async-start(bf16[8,1024,172]{1,2,0:T(8,128)(2,1)} %copy.405), calls=%async_computation.7 | async-start | bytes 5767168 | tf_op jit(solution)/shard_map/all_to_all | solution.py:344
  1502.5 53.9 %all-to-all-start.9 = ((bf16[8,1024,172]{1,2,0:T(8,128)(2,1)}), bf16[8,1024,172]{1,2,0:T(8,128)(2,1)S(1)}, u32[]{:S(2)}, u32[]{:S(2)}) async-start(bf16[8,1024,172]{1,2,0:T(8,128)(2,1)} %get-tuple-element.318), calls=%async_computation.9 | async-start | bytes 5767168 | tf_op jit(solution)/shard_map/all_to_all | solution.py:362
  1506.3 48.3 %reduce-scatter.2.cloned.1.call-start = ((), (), s32[]{:S(2)}) async-start(), calls=%async_computation.12 | async-start | bytes 1622016 | tf_op jit(solution)/shard_map/reduce_scatter | solution.py:315
  1512.6 42.0 %copy-start.26 = (bf16[512,172]{1,0:T(8,128)(2,1)S(1)}, bf16[512,172]{1,0:T(8,128)(2,1)}, u32[]{:S(2)}) copy-start(bf16[512,172]{1,0:T(8,128)(2,1)} %copy-done.25) | copy-start | bytes 528388
  1512.6 240.9 %all-reduce.4.cloned.1.call-start = ((), (), s32[]{:S(2)}) async-start(), calls=%async_computation.13 | async-start | bytes 5341184 | tf_op jit(solution)/shard_map/psum | solution.py:390
  1615.0 138.5 %copy-start.24 = (f32[4,172,172]{2,0,1:T(4,128)S(1)}, f32[4,172,172]{2,0,1:T(4,128)}, u32[]{:S(2)}) copy-start(f32[4,172,172]{2,0,1:T(4,128)} %param.45) | copy-start | bytes 1420036
  1615.1 138.5 %copy-start.48 = (f32[4,172,172]{2,0,1:T(4,128)S(1)}, f32[4,172,172]{2,0,1:T(4,128)}, u32[]{:S(2)}) copy-start(f32[4,172,172]{2,0,1:T(4,128)} %param.55) | copy-start | bytes 1420036
  1615.1 138.5 %copy-start.49 = (f32[4,172,172]{2,0,1:T(4,128)S(1)}, f32[4,172,172]{2,0,1:T(4,128)}, u32[]{:S(2)}) copy-start(f32[4,172,172]{2,0,1:T(4,128)} %param.50) | copy-start | bytes 1420036
  (162 other events, 623.9 us)
Sparse Core Ops, SparseCore 0:
  560.5 43.2 all-gather.1
  1512.7 41.8 reduce-scatter.1
  1615.2 138.3 all-reduce.3
where the time goes:
time: 1790 us; the launch traced here: 1770 us
  local copies, waits for them, and re-layouts  759 us (42%)
  other arithmetic  406 us (23%)
  waiting for transfers between devices  267 us (15%)
  matrix products  221 us (12%)
  blocking collectives  66.3 us (4%)
  starting transfers between devices  35.4 us (2%)
    another operation x40, other arithmetic  177 us
    psum x1, waiting for transfers between devices, local(): lax.psum((grad_msg, grad_gru, grad_square, grad_kv, grad_out, loss_local)...  122 us
    dot_general x25, matrix products, product(): return jnp.dot(left_side, right_side, preferred_element_type=jnp.float32)  117 us
    reshape x32, local copies, waits for them, and re-layouts, node_lookup(): mem_rows.reshape(safe_ids.shape + (node_mem.shape[1],))  115 us
    scatter x7, local copies, waits for them, and re-layouts, to_buckets(): buffer.at[slot_index].set(values)  103 us
    mul x24, local copies, waits for them, and re-layouts, attention_backward(): grad_values = probs[..., None] * grad_heads[:, None]  69.1 us
    gather x4, local copies, waits for them, and re-layouts, from_buckets(): return buffer.reshape((-1,) + buffer.shape[2:])[slot_index]  68.2 us
    reduce_sum x16, other arithmetic, node_lookup(): last_rows = jnp.sum(jnp.where(selector, node_last[None, :], 0), 1)  60.9 us
  transfers between devices with their start and end apart: 11, of which 5 were waited for; matrix products, arithmetic and copies ran while one was open for 18% of the time, Pallas kernels for 0%

commit v1 on v0

v1 whole, which is shorter than its diff:
```python
from functools import partial
import math

import jax
import jax.numpy as jnp
import numpy as np
from jax import lax
from jax.experimental import pallas as pl
from jax.experimental.pallas import tpu as pltpu
from jax.sharding import PartitionSpec as P

HEADS = 2
LANES = 256
MESH = pl.DeviceIdType.MESH
f32 = jnp.float32
bf16 = jnp.bfloat16

mu_coef = 0.9
avg_coef = 0.1
rate_coef = 0.008
mask_fill = -1e30

COS_TERMS = (
    1.0,
    -19.73920440673828,
    64.93911743164062,
    -85.45011901855469,
    60.16745376586914,
    -25.966907501220703,
    6.527653217315674,
)


def pad_to(size, step):
    return -(-size // step) * step


def nn(a, b):
    return lax.dot_general(a, b, (((1,), (0,)), ((), ())), preferred_element_type=f32)


def nt(a, b):
    return lax.dot_general(a, b, (((1,), (1,)), ((), ())), preferred_element_type=f32)


def flip_bit(index, bit):
    size = 1 << bit
    return index + size * (1 - 2 * (lax.div(index, size) % 2))


def nesterov(weight, gradient, moment, average, step_rate):
    new_moment = mu_coef * moment + gradient
    new_weight = weight - step_rate * (gradient + mu_coef * new_moment)
    return (new_moment, new_weight, (1.0 - avg_coef) * average + avg_coef * new_weight)


def time_columns(time_width, rows):
    turns = 10.0 ** (-np.linspace(0.0, 9.0, time_width)) / (2.0 * np.pi)
    mant, expo = np.frexp(turns)
    high = np.ldexp(np.round(mant * 4096.0) / 4096.0, expo)
    out = np.zeros((rows, 128), np.float32)
    out[:time_width, 0] = high
    out[:time_width, 1] = turns - high
    return out


def cos_rows(delta, high, low):
    turns = delta * high
    rest = turns - jnp.floor(turns + 0.5) + delta * low
    square = rest * rest
    value = square * COS_TERMS[-1] + COS_TERMS[-2]
    for term in COS_TERMS[-3::-1]:
        value = value * square + term
    return value


class Heads:
    def __init__(self, head_dim, rows):
        self.low = head_dim // 8 * 8
        self.high = pad_to(head_dim, 8)
        self.cut = head_dim - self.low
        self.rows = rows

    def split(self, lanes):
        return lax.broadcasted_iota(jnp.int32, (8, lanes), 0) < self.cut

    def sums(self, x):
        lanes = x.shape[1]
        mid = x[self.low : self.high]
        first = self.split(lanes)
        a = jnp.sum(x[: self.low].reshape(self.low // 8, 8, lanes), 0)
        b = jnp.sum(x[self.high :].reshape((self.rows - self.high) // 8, 8, lanes), 0)
        a = a + jnp.where(first, mid, 0.0)
        b = b + jnp.where(first, 0.0, mid)
        return jnp.sum(a, 0, keepdims=True), jnp.sum(b, 0, keepdims=True)

    def scale(self, x, p0, p1):
        lanes = x.shape[1]
        mid = jnp.where(self.split(lanes), p0, p1)
        return jnp.concatenate(
            [x[: self.low] * p0, x[self.low : self.high] * mid, x[self.high :] * p1], 0
        )


def exchange_kernel(
    own, batch, shard_ref, cand_ref, event_ref, last_ref,
    table_ref, ids_ref, pos_ref, newest_ref,
    batch_buf, own_buf, local_sem, table_send, table_recv, batch_send, batch_recv, own_send, own_recv,
):
    me = lax.axis_index("own")
    group = lax.axis_index("batch")
    barrier = pltpu.get_barrier_semaphore()
    for step in range(1, own):
        pl.semaphore_signal(barrier, inc=1, device_id=(group, lax.rem(me + step, own)), device_id_type=MESH)
    for step in range(1, batch):
        pl.semaphore_signal(barrier, inc=1, device_id=(lax.rem(group + step, batch), me), device_id_type=MESH)
    pl.semaphore_wait(barrier, own + batch - 2)

    nodes = shard_ref.shape[0]
    half = nodes // 2
    bits = own.bit_length() - 1
    rest = list(range(1, bits))
    cut = len(rest) // 2
    orders = (rest + [0], rest[cut:] + rest[:cut] + [0])

    def shard_copy(stream, pattern, bit):
        peer = flip_bit(me, bit)
        source = me
        for b in range(bits):
            if pattern >> b & 1:
                source = flip_bit(source, b)
        rows = pl.ds(pl.multiple_of(source * nodes + stream * half, half), half)
        slot = pattern | 1 << bit
        src = shard_ref.at[pl.ds(stream * half, half)] if pattern == 0 else table_ref.at[rows]
        return pltpu.make_async_remote_copy(
            src_ref=src, dst_ref=table_ref.at[rows],
            send_sem=table_send.at[stream, slot], recv_sem=table_recv.at[stream, slot],
            device_id=(group, peer), device_id_type=MESH,
        )

    copies = [{}, {}]
    for step in range(bits):
        for stream in range(2):
            bit = orders[stream][step]
            copy = shard_copy(stream, 0, bit)
            copy.start()
            copies[stream][1 << bit] = copy
    mine = pltpu.make_async_copy(
        shard_ref, table_ref.at[pl.ds(pl.multiple_of(me * nodes, nodes), nodes)], local_sem
    )
    mine.start()

    events = event_ref.shape[1]
    time_row = event_ref[0:1, :].astype(f32)
    src_row = event_ref[2:3, :]
    best = []
    tile = 256
    for start in range(0, nodes, tile):
        node = lax.broadcasted_iota(jnp.int32, (tile, 128), 0) + start
        top = jnp.full((tile, 128), -1.0, f32)
        for lane in range(0, events, 128):
            hit = src_row[:, lane : lane + 128] == node
            top = jnp.maximum(top, jnp.where(hit, time_row[:, lane : lane + 128], -1.0))
        best.append(jnp.max(top.T, 0, keepdims=True))
    newest = jnp.concatenate(best, 1).astype(jnp.int32)
    newest = jnp.maximum(newest, last_ref[0:1, :])
    count = jnp.sum(event_ref[1:2, :].astype(f32), 1, keepdims=True).astype(jnp.int32)
    batch_buf[0, 0:1, :] = newest
    batch_buf[0, 1:2, :] = jnp.broadcast_to(count, (1, nodes))

    def peer_copy(step):
        return pltpu.make_async_remote_copy(
            src_ref=batch_buf.at[0], dst_ref=batch_buf.at[step],
            send_sem=batch_send.at[step], recv_sem=batch_recv.at[step],
            device_id=(lax.rem(group + step, batch), me), device_id_type=MESH,
        )

    peers = [peer_copy(step) for step in range(1, batch)]
    for copy in peers:
        copy.start()
    total = count
    for step, copy in enumerate(peers, 1):
        copy.wait_recv()
        newest = jnp.maximum(newest, batch_buf[step, 0:1, :])
        total = total + batch_buf[step, 1:2, 0:1]
    newest_ref[...] = newest

    width = cand_ref.shape[1]
    own_buf[0, 0:1, :] = cand_ref[...] + me * nodes
    own_buf[0, 1:2, :] = jnp.broadcast_to(total, (1, width))

    def owner_copy(step):
        return pltpu.make_async_remote_copy(
            src_ref=own_buf.at[0], dst_ref=own_buf.at[step],
            send_sem=own_send.at[step], recv_sem=own_recv.at[step],
            device_id=(group, lax.rem(me + step, own)), device_id_type=MESH,
        )

    owners = [owner_copy(step) for step in range(1, own)]
    for copy in owners:
        copy.start()

    for step in range(bits):
        for stream in range(2):
            order = orders[stream]
            held = [0]
            for bit in order[:step]:
                held = held + [p | 1 << bit for p in held]
            for pattern in held:
                slot = pattern | 1 << order[step]
                copies[stream][slot].wait_recv() if slot in copies[stream] else None
                for bit in order[step + 1 :]:
                    copy = shard_copy(stream, slot, bit)
                    copy.start()
                    copies[stream][slot | 1 << bit] = copy

    ids_ref[pl.ds(me, 1), :] = own_buf[0, 0:1, :]
    for step, copy in enumerate(owners, 1):
        copy.wait_recv()
        source = lax.rem(me - step + own, own)
        ids_ref[pl.ds(source, 1), :] = own_buf[step, 0:1, :]
        total = total + own_buf[step, 1:2, 0:1]
    pos_ref[...] = jnp.broadcast_to(jnp.maximum(total.astype(f32), 1.0), pos_ref.shape)
    mine.wait()
    for copy in peers + owners:
        copy.wait_send()
    for stream in range(2):
        for slot in copies[stream]:
            copies[stream][slot].wait_send()


def exchange(own, batch, shard, cand, event_rows, last):
    nodes = shard.shape[0]
    width = cand.shape[1]
    vmem = pl.BlockSpec(memory_space=pltpu.VMEM)
    hbm = pl.BlockSpec(memory_space=pl.ANY)
    return pl.pallas_call(
        partial(exchange_kernel, own, batch),
        out_shape=(
            jax.ShapeDtypeStruct((own * nodes, 2, 128), bf16),
            jax.ShapeDtypeStruct((own, width), jnp.int32),
            jax.ShapeDtypeStruct((8, 128), f32),
            jax.ShapeDtypeStruct((1, nodes), jnp.int32),
        ),
        in_specs=[hbm, vmem, vmem, vmem],
        out_specs=(hbm, vmem, vmem, vmem),
        scratch_shapes=[
            pltpu.VMEM((batch, 8, nodes), jnp.int32),
            pltpu.VMEM((own, 8, width), jnp.int32),
            pltpu.SemaphoreType.DMA,
            pltpu.SemaphoreType.DMA((2, own)),
            pltpu.SemaphoreType.DMA((2, own)),
            pltpu.SemaphoreType.DMA((batch,)),
            pltpu.SemaphoreType.DMA((batch,)),
            pltpu.SemaphoreType.DMA((own,)),
            pltpu.SemaphoreType.DMA((own,)),
        ],
        compiler_params=pltpu.CompilerParams(
            collective_id=1, has_side_effects=True, vmem_limit_bytes=32 * 2**20
        ),
        name="exchange",
    )(shard, cand, event_rows, last)


class Layout:
    def __init__(self, width, edge, time_width, fold):
        rows = pad_to(width, 16)
        times = pad_to(time_width, 16)
        edges = pad_to(edge, 16)
        assert width <= 192 and edges == rows
        names = ["msg_mem", "msg_edge"]
        names += [f"gru{i}{g}" for i in range(2) for g in range(3)]
        names += [f"square{i}" for i in range(4)]
        names += ["kv_mem_k", "kv_mem_v", "out_a", "out_b"]
        sizes = [(n, rows) for n in names] + [("kv_time_k", times), ("kv_time_v", times), ("msg_time", times)]
        self.at = {}
        row = 0
        for name, size in sizes:
            self.at[name] = [row, size, None, None]
            row += size
        for index, (name, size) in enumerate(sizes):
            if index % 2 == 0:
                self.at[name][2:] = [row, 0]
                row += size
            else:
                before = self.at[sizes[index - 1][0]]
                assert before[1] == size
                self.at[name][2:] = [before[2], 64]
        self.loss = row
        row += 8
        self.total = pad_to(row, fold)
        self.unused = row

    def put(self, ref, name, value):
        first, size, second, lane = self.at[name]
        ref[first : first + size, :] = value[:, :128]
        ref[second : second + size, lane : lane + value.shape[1] - 128] = value[:, 128:]

    def take(self, packed, name, rows, width):
        first, size, second, lane = self.at[name]
        return jnp.concatenate(
            [packed[first : first + rows, :128], packed[second : second + rows, lane : lane + width - 128]], 1
        )


def main_kernel(
    dims,
    ids_ref, cand_ref, pos_ref, table_ref, event_ref, valid_ref, mem3_ref, edge_ref,
    wsq_ref, wme_ref, wtime_ref, wkv1_ref, wkv2_ref, wd_ref, wdt_ref, eye_ref, freq_ref,
    grad_ref,
    xs, x_all, t_all, kv_all, score, dest_rows, slab,
    t_src, mem_low, hidden, fresh_low, att_low, mixed_low, hid_out, emb, emb_rows,
    mem_src, pre_msg, reset_gate, update, cand_act, gate_n, queries, attended, pre_out,
    acc_a, grad_att, gkv_m, gkv_t, rows_ref,
):
    width, head_dim, slots, keep_kv, layout = dims
    events = event_ref.shape[1]
    rows = pad_to(width, 16)
    times = t_src.shape[0]
    heads = Heads(head_dim, rows)
    scale = head_dim ** (-0.5)
    high, low = freq_ref[:, 0:1], freq_ref[:, 1:2]
    chunks = events // LANES
    owners, cand_width = cand_ref.shape
    W = {}
    order = ["wm_m", "g0r", "g0z", "g0n", "g1r", "g1z", "g1n", "s0t", "s1t", "s2t", "oat", "obt",
             "g0r_", "g0z_", "g0n_", "s0", "s1", "s2", "oa", "ob"]
    for index, name in enumerate(order):
        W[name] = index

    def w(name):
        return wsq_ref[W[name]]

    def gather(read_id, count):
        unroll = 64

        def body(i, unused):
            base = i * unroll
            got = [table_ref[read_id(base + k)] for k in range(unroll)]
            for k in range(unroll):
                xs[pl.ds(pl.multiple_of(2 * base, 2 * unroll) + 2 * k, 2), :] = got[k].astype(f32)
            return unused

        lax.fori_loop(0, count // unroll, body, 0)

    def gathered(start, count):
        base = pl.multiple_of(2 * start, 2 * count)
        return jnp.concatenate(
            [xs[pl.ds(base, count, stride=2), :], xs[pl.ds(base + 1, count, stride=2), :]], 1
        ).astype(bf16)

    grad_ref[...] = jnp.zeros_like(grad_ref)

    def cand_body(o, unused):
        gather(lambda i: cand_ref[o, i], cand_width)
        at = pl.multiple_of(o * cand_width, cand_width)
        dest_rows[pl.ds(at, cand_width), :] = gathered(0, cand_width)
        return unused

    lax.fori_loop(0, owners, cand_body, 0)

    def lanes(c, size=LANES):
        return pl.ds(pl.multiple_of(c * size, size), size)

    def gru_body(c, unused):
        cs = lanes(c)
        node = lax.broadcasted_iota(jnp.int32, (mem3_ref.shape[1], LANES), 0)
        onehot = (node == event_ref[2:3, cs]).astype(f32).astype(bf16)
        parts = nn(mem3_ref[...], onehot)
        mem = parts[:rows] + parts[rows : 2 * rows] + parts[2 * rows :]
        mem_src[:, cs] = mem
        delta = event_ref[0:1, cs].astype(f32) - mem[width : width + 1]
        t_low = cos_rows(delta, high, low).astype(bf16)
        t_src[:, cs] = t_low
        m_low = mem.astype(bf16)
        mem_low[:, cs] = m_low
        pre = nn(w("wm_m"), m_low) + nt(wme_ref[...], edge_ref[cs, :]) + nn(wtime_ref[...], t_low)
        pre_msg[:, cs] = pre
        hid = (pre * jax.nn.sigmoid(pre)).astype(bf16)
        hidden[:, cs] = hid
        r = jax.nn.sigmoid(nn(w("g0r"), hid) + nn(w("g1r"), m_low))
        reset_gate[:, cs] = r
        u = jax.nn.sigmoid(nn(w("g0z"), hid) + nn(w("g1z"), m_low))
        update[:, cs] = u
        gn = nn(w("g1n"), m_low)
        gate_n[:, cs] = gn
        cand = jnp.tanh(nn(w("g0n"), hid) + r * gn)
        cand_act[:, cs] = cand
        fresh = ((1.0 - u) * cand + u * mem).astype(bf16)
        fresh_low[:, cs] = fresh
        queries[:, cs] = nn(w("s0t"), fresh).astype(bf16)
        return unused

    lax.fori_loop(0, chunks, gru_body, 0)

    def slot_body(j, unused):
        gather(lambda i: ids_ref[j * events + i], events)

        def chunk_body(c, unused):
            cs = lanes(c)
            x = gathered(c * LANES, LANES)
            x_all[j, cs, :] = x
            kv = nt(wkv1_ref[...], x)
            delta = event_ref[0:1, cs].astype(f32) - kv[width : width + 1]
            t_low = cos_rows(delta, high, low).astype(bf16)
            t_all[j, :, cs] = t_low
            kv = (kv + nn(wkv2_ref[...], t_low)).astype(bf16)
            if keep_kv:
                kv_all[j, :, cs] = kv
            s0, s1 = heads.sums(kv[:rows].astype(f32) * queries[:, cs].astype(f32))
            live = valid_ref[j, :, cs] > 0
            score[j, 0:1, cs] = jnp.where(live, s0 * scale, mask_fill)
            score[j, 1:2, cs] = jnp.where(live, s1 * scale, mask_fill)
            return unused

        lax.fori_loop(0, chunks, chunk_body, 0)
        return unused

    lax.fori_loop(0, slots, slot_body, 0)

    def soft_body(c, unused):
        cs = lanes(c, 128)
        s = score[:, 0:2, cs]
        top = jnp.max(s, 0, keepdims=True)
        p = jnp.where(s > 0.5 * mask_fill, jnp.exp(s - top), 0.0)
        score[:, 0:2, cs] = p / jnp.sum(p, 0, keepdims=True)
        return unused

    lax.fori_loop(0, events // 128, soft_body, 0)

    def kv_of(j, cs, part):
        if keep_kv:
            return kv_all[j, part, cs]
        return (nt(wkv1_ref[part, :], x_all[j, cs, :]) + nn(wkv2_ref[part, :], t_all[j, :, cs])).astype(bf16)

    def att_body(c, unused):
        cs = lanes(c, 128)

        def add(j, total):
            v = kv_of(j, cs, slice(rows, 2 * rows)).astype(f32)
            return total + heads.scale(v, score[j, 0:1, cs], score[j, 1:2, cs])

        att = lax.fori_loop(0, slots, add, jnp.zeros((rows, 128), f32))
        attended[:, cs] = att
        att_low[:, cs] = att.astype(bf16)
        return unused

    lax.fori_loop(0, events // 128, att_body, 0)

    def out_body(c, unused):
        cs = lanes(c)
        mixed = nn(w("s1t"), att_low[:, cs]).astype(bf16)
        mixed_low[:, cs] = mixed
        pre = nn(w("oat"), mixed) + nn(w("obt"), fresh_low[:, cs])
        pre_out[:, cs] = pre
        hid = (pre * jax.nn.sigmoid(pre)).astype(bf16)
        hid_out[:, cs] = hid
        e = nn(w("s2t"), hid).astype(bf16)
        emb[:, cs] = e
        emb_rows[cs, :] = nt(eye_ref[...], e).astype(bf16)
        return unused

    lax.fori_loop(0, chunks, out_body, 0)

    def row_init(c, unused):
        cs = lanes(c)
        rows_ref[0:1, cs] = jnp.full((1, LANES), mask_fill, f32)
        rows_ref[1:3, cs] = jnp.zeros((2, LANES), f32)
        acc_a[:, cs] = jnp.zeros((rows, LANES), f32)
        return unused

    lax.fori_loop(0, chunks, row_init, 0)

    def dest_of(o):
        at = pl.multiple_of(o * cand_width, cand_width)
        return dest_rows[pl.ds(at, cand_width), :]

    def lse_block(o, unused):
        dest = nn(dest_of(o), wd_ref[...]).astype(bf16)

        def chunk(c, unused):
            cs = lanes(c)
            logits = nn(dest, emb[:, cs])
            old = rows_ref[0:1, cs]
            top = jnp.maximum(old, jnp.max(logits, 0, keepdims=True))
            rows_ref[0:1, cs] = top
            rows_ref[1:2, cs] = rows_ref[1:2, cs] * jnp.exp(old - top) + jnp.sum(
                jnp.exp(logits - top), 0, keepdims=True
            )
            hit = lax.broadcasted_iota(jnp.int32, logits.shape, 0) == event_ref[3:4, cs] - o * cand_width
            rows_ref[2:3, cs] = rows_ref[2:3, cs] + jnp.sum(jnp.where(hit, logits, 0.0), 0, keepdims=True)
            return unused

        lax.fori_loop(0, chunks, chunk, 0)
        return unused

    lax.fori_loop(0, owners, lse_block, 0)

    mask_row = event_ref[1:2, :].astype(f32)
    log_sum = rows_ref[0:1, :] + jnp.log(rows_ref[1:2, :])
    rows_ref[3:4, :] = log_sum
    rows_ref[4:5, :] = mask_row / jnp.broadcast_to(pos_ref[0:1, 0:1], mask_row.shape)
    loss = jnp.sum(mask_row * (log_sum - rows_ref[2:3, :]), 1, keepdims=True)
    grad_ref[layout.loss : layout.loss + 8, :] = jnp.broadcast_to(loss, (8, 128))

    def back_block(o, grad_dest_w):
        block = dest_of(o)
        dest = nn(block, wd_ref[...]).astype(bf16)
        dest_t = nt(wdt_ref[...], block).astype(bf16)
        block_t = nt(eye_ref[...], block).astype(bf16)

        def chunk(c, unused):
            cs = lanes(c)
            logits = nn(dest, emb[:, cs])
            coeff = rows_ref[4:5, cs]
            hit = lax.broadcasted_iota(jnp.int32, logits.shape, 0) == event_ref[3:4, cs] - o * cand_width
            grad = jnp.exp(logits - rows_ref[3:4, cs]) - jnp.where(hit, 1.0, 0.0)
            grad = (grad * coeff).astype(bf16)
            slab[0:cand_width, cs] = grad
            acc_a[:, cs] += nn(dest_t, grad)
            return unused

        lax.fori_loop(0, chunks, chunk, 0)
        grad_dest = nn(slab[0:cand_width, :], emb_rows[...]).astype(bf16)
        return grad_dest_w + nn(block_t, grad_dest)[:rows]

    grad_dest_w = lax.fori_loop(0, owners, back_block, jnp.zeros((rows, rows), f32))
    layout.put(grad_ref, "square3", grad_dest_w)

    r0, r1, r2 = slice(0, rows), slice(rows, 2 * rows), slice(2 * rows, 3 * rows)

    def out_back(c, unused):
        cs = lanes(c)
        ge = acc_a[:, cs].astype(bf16)
        slab[r0, cs] = ge
        pre = pre_out[:, cs]
        sig = jax.nn.sigmoid(pre)
        gp = (nn(w("s2"), ge) * (sig * (1.0 + pre * (1.0 - sig)))).astype(bf16)
        slab[r1, cs] = gp
        gm = nn(w("oa"), gp).astype(bf16)
        slab[r2, cs] = gm
        acc_a[:, cs] = nn(w("ob"), gp)
        ga = nn(w("s1"), gm).astype(bf16)
        grad_att[:, cs] = ga
        d0, d1 = heads.sums(ga.astype(f32) * attended[:, cs])
        rows_ref[5:6, cs] = d0
        rows_ref[6:7, cs] = d1
        return unused

    lax.fori_loop(0, chunks, out_back, 0)
    layout.put(grad_ref, "square2", nt(hid_out[...], slab[r0, :]))
    layout.put(grad_ref, "out_a", nt(mixed_low[...], slab[r1, :]))
    layout.put(grad_ref, "out_b", nt(fresh_low[...], slab[r1, :]))
    layout.put(grad_ref, "square1", nt(att_low[...], slab[r2, :]))

    attended[...] = jnp.zeros_like(attended)
    gkv_m[...] = jnp.zeros_like(gkv_m)
    gkv_t[...] = jnp.zeros_like(gkv_t)

    def slot_back(j, unused):
        def chunk(c, unused):
            cs = lanes(c, 128)
            kv = kv_of(j, cs, slice(0, 2 * rows)).astype(f32)
            ga = grad_att[:, cs].astype(f32)
            p0, p1 = score[j, 0:1, cs], score[j, 1:2, cs]
            g0, g1 = heads.sums(ga * kv[rows:])
            g0 = p0 * (g0 - rows_ref[5:6, cs]) * scale
            g1 = p1 * (g1 - rows_ref[6:7, cs]) * scale
            attended[:, cs] += heads.scale(kv[:rows], g0, g1)
            slab[r0, cs] = heads.scale(queries[:, cs].astype(f32), g0, g1).astype(bf16)
            slab[r1, cs] = heads.scale(ga, p0, p1).astype(bf16)
            return unused

        lax.fori_loop(0, events // 128, chunk, 0)
        both = slab[0 : 2 * rows, :]
        gkv_m[...] += nn(both, x_all[j])
        gkv_t[...] += nt(both, t_all[j])
        return unused

    lax.fori_loop(0, slots, slot_back, 0)
    gm = gkv_m[...].T
    layout.put(grad_ref, "kv_mem_k", gm[:rows, :rows])
    layout.put(grad_ref, "kv_mem_v", gm[:rows, rows:])
    gt = gkv_t[...].T
    layout.put(grad_ref, "kv_time_k", gt[:times, :rows])
    layout.put(grad_ref, "kv_time_v", gt[:times, rows:])

    def gru_back(c, unused):
        cs = lanes(c)
        gq = attended[:, cs].astype(bf16)
        slab[r0, cs] = gq
        gf = acc_a[:, cs] + nn(w("s0"), gq)
        u, cand, r = update[:, cs], cand_act[:, cs], reset_gate[:, cs]
        act = gf * (1.0 - u) * (1.0 - cand * cand)
        gr = (act * gate_n[:, cs] * r * (1.0 - r)).astype(bf16)
        gu = (gf * (mem_src[:, cs] - cand) * u * (1.0 - u)).astype(bf16)
        gn = act.astype(bf16)
        gh = (act * r).astype(bf16)
        slab[r1, cs] = gr
        slab[r2, cs] = gu
        mixed_low[:, cs] = gn
        hid_out[:, cs] = gh
        pre = pre_msg[:, cs]
        sig = jax.nn.sigmoid(pre)
        back = nn(w("g0r_"), gr) + nn(w("g0z_"), gu) + nn(w("g0n_"), gn)
        att_low[:, cs] = (back * (sig * (1.0 + pre * (1.0 - sig)))).astype(bf16)
        return unused

    lax.fori_loop(0, chunks, gru_back, 0)
    layout.put(grad_ref, "square0", nt(fresh_low[...], slab[r0, :]))
    for index, (left, last) in enumerate(((hidden, mixed_low), (mem_low, hid_out))):
        layout.put(grad_ref, f"gru{index}0", nt(left[...], slab[r1, :]))
        layout.put(grad_ref, f"gru{index}1", nt(left[...], slab[r2, :]))
        layout.put(grad_ref, f"gru{index}2", nt(left[...], last[...]))
    layout.put(grad_ref, "msg_mem", nt(mem_low[...], att_low[...]))
    layout.put(grad_ref, "msg_time", nt(t_src[...], att_low[...]))
    edge_back = nn(att_low[...], edge_ref[...])
    edge_back = jnp.concatenate([edge_back, jnp.zeros((rows, 256 - edge_back.shape[1]), f32)], 1)
    edge_back = jnp.concatenate([edge_back, jnp.zeros((256 - rows, 256), f32)], 0).T
    layout.put(grad_ref, "msg_edge", edge_back[:rows, :rows])


def main(layout, keep_kv, width, head_dim, slots, times, args):
    events = args[4].shape[1]
    rows = pad_to(width, 16)
    cands = args[1].shape[0] * args[1].shape[1]
    smem = pl.BlockSpec(memory_space=pltpu.SMEM)
    vmem = pl.BlockSpec(memory_space=pltpu.VMEM)
    low = lambda *shape: pltpu.VMEM(shape, bf16)
    full = lambda *shape: pltpu.VMEM(shape, f32)
    return pl.pallas_call(
        partial(main_kernel, (width, head_dim, slots, keep_kv, layout)),
        out_shape=jax.ShapeDtypeStruct((layout.total, 128), f32),
        in_specs=[smem, smem] + [vmem] * (len(args) - 2),
        out_specs=vmem,
        scratch_shapes=[
            full(2 * events, 128),
            low(slots, events, 256),
            low(slots, times, events),
            low(slots if keep_kv else 1, 2 * rows if keep_kv else 16, events),
            full(slots, 8, events),
            low(cands, 256),
            low(max(3 * rows, args[1].shape[1]), events),
            low(times, events),
        ]
        + [low(rows, events)] * 7
        + [low(events, rows)]
        + [full(rows, events)] * 6
        + [low(rows, events)]
        + [full(rows, events)] * 3
        + [low(rows, events), full(2 * rows, 256), full(2 * rows, times), full(8, events)],
        compiler_params=pltpu.CompilerParams(vmem_limit_bytes=63 * 2**20),
        name="train",
    )(*args)


def reduce_kernel(own, batch, streams, grad_ref, out_ref, acc, recv, send_sem, recv_sem):
    place = {"own": lax.axis_index("own"), "batch": lax.axis_index("batch")}

    def peer(axis, bit):
        moved = dict(place)
        moved[axis] = flip_bit(place[axis], bit)
        return (moved["batch"], moved["own"])

    barrier = pltpu.get_barrier_semaphore()
    steps = streams[0][2]
    for axis, bit in steps:
        pl.semaphore_signal(barrier, inc=1, device_id=peer(axis, bit), device_id_type=MESH)
    pl.semaphore_wait(barrier, len(steps))

    base = [start for start, size, order in streams]
    sizes = [size for start, size, order in streams]
    inner = [start for start, size, order in streams]
    sent = []
    for step in range(len(steps)):
        source = grad_ref if step == 0 else acc
        copies = []
        for s, (start, size, order) in enumerate(streams):
            axis, bit = order[step]
            half = sizes[s] // 2
            mine = lax.div(place[axis], 1 << bit) % 2
            away = pl.multiple_of(base[s] + (1 - mine) * half, 8)
            copy = pltpu.make_async_remote_copy(
                src_ref=source.at[pl.ds(away, half), :],
                dst_ref=recv.at[pl.ds(inner[s], half), :],
                send_sem=send_sem.at[s, step], recv_sem=recv_sem.at[s, step],
                device_id=peer(axis, bit), device_id_type=MESH,
            )
            copy.start()
            copies.append(copy)
            base[s] = pl.multiple_of(base[s] + mine * half, 8)
            sizes[s] = half
        last = step == len(steps) - 1
        target = out_ref if last else acc
        for s, copy in enumerate(copies):
            copy.wait_recv()
            part = pl.ds(base[s], sizes[s])
            target[part, :] = source[part, :] + recv[pl.ds(inner[s], sizes[s]), :]
            inner[s] += sizes[s]
        sent += copies
    for step in reversed(range(len(steps))):
        copies = []
        for s, (start, size, order) in enumerate(streams):
            axis, bit = order[step]
            part = pl.ds(base[s], sizes[s])
            copy = pltpu.make_async_remote_copy(
                src_ref=out_ref.at[part, :], dst_ref=out_ref.at[part, :],
                send_sem=send_sem.at[s, step + len(steps)], recv_sem=recv_sem.at[s, step + len(steps)],
                device_id=peer(axis, bit), device_id_type=MESH,
            )
            copy.start()
            copies.append(copy)
            mine = lax.div(place[axis], 1 << bit) % 2
            base[s] = pl.multiple_of(base[s] - mine * sizes[s], 8)
            sizes[s] *= 2
        for copy in copies:
            copy.wait_recv()
        sent += copies
    for copy in sent:
        copy.wait_send()


def reduce_all(own, batch, packed):
    total = packed.shape[0]
    own_bits = own.bit_length() - 1
    batch_bits = batch.bit_length() - 1
    fold = 8 << (own_bits + batch_bits)
    rest = [("own", b) for b in range(1, own_bits)]
    cut = len(rest) // 2
    tail = [("batch", b) for b in range(batch_bits)]
    blocks = total // fold
    first = (blocks + 1) // 2 * fold
    streams = (
        (0, first, [("own", 0)] + rest + tail),
        (first, total - first, [("own", 0)] + rest[cut:] + rest[:cut] + tail),
    )
    count = 2 * (own_bits + batch_bits)
    return pl.pallas_call(
        partial(reduce_kernel, own, batch, streams),
        out_shape=jax.ShapeDtypeStruct(packed.shape, f32),
        in_specs=[pl.BlockSpec(memory_space=pltpu.VMEM)],
        out_specs=pl.BlockSpec(memory_space=pltpu.VMEM),
        scratch_shapes=[
            pltpu.VMEM(packed.shape, f32),
            pltpu.VMEM(packed.shape, f32),
            pltpu.SemaphoreType.DMA((2, count)),
            pltpu.SemaphoreType.DMA((2, count)),
        ],
        compiler_params=pltpu.CompilerParams(
            collective_id=2, has_side_effects=True, vmem_limit_bytes=32 * 2**20
        ),
        name="reduce",
    )(packed)


def local(
    memory, last_update, src_local, edge_feat, event_time, nbr_owner, nbr_ids, nbr_mask, event_mask,
    dest_local, target, w_msg, w_gru, w_square, w_key_value, w_output,
    mom_msg, mom_gru, mom_square, mom_key_value, mom_output,
    avg_msg, avg_gru, avg_square, avg_key_value, avg_output,
):
    own = lax.axis_size("own")
    batch = lax.axis_size("batch")
    events, edge = edge_feat.shape
    nodes, width = memory.shape
    picks, per_pick = nbr_ids.shape[1:]
    slots = picks * per_pick
    head_dim = width // HEADS
    time_width = w_key_value.shape[0] - width
    rows = pad_to(width, 16)
    times = pad_to(time_width, 16)
    layout = Layout(width, edge, time_width, (8 * own * batch))

    mem_low = memory.astype(bf16)
    time_parts = jnp.stack([last_update // 8, last_update % 8], 1).astype(bf16)
    shard = jnp.pad(jnp.concatenate([mem_low, time_parts], 1), ((0, 0), (0, 256 - width - 2)))
    shard = shard.reshape(nodes, 2, 128)
    event_rows = jnp.stack([event_time, event_mask, src_local, target])
    event_rows = jnp.pad(event_rows, ((0, 4), (0, 0)))
    table, cand_ids, positives, newest = exchange(
        own, batch, shard, dest_local[None, :], event_rows, last_update[None, :]
    )

    flat_ids = (nbr_owner[:, :, None] * nodes + nbr_ids).reshape(events, slots).T.reshape(-1)
    valid = nbr_mask.reshape(events, slots).T.reshape(slots, 1, events)
    mem_t = jnp.pad(jnp.concatenate([memory, last_update.astype(f32)[:, None]], 1).T, ((0, rows - width - 1), (0, 0)))
    part0 = mem_t.astype(bf16)
    part1 = (mem_t - part0.astype(f32)).astype(bf16)
    part2 = (mem_t - part0.astype(f32) - part1.astype(f32)).astype(bf16)
    mem3 = jnp.concatenate([part0, part1, part2], 0)

    def square(weight):
        weight = weight.astype(bf16)
        return jnp.pad(weight, ((0, rows - weight.shape[0]), (0, rows - weight.shape[1])))

    g0 = [w_gru[0, :, i * width : (i + 1) * width] for i in range(3)]
    g1 = [w_gru[1, :, i * width : (i + 1) * width] for i in range(3)]
    sq = [w_square[i] for i in range(3)]
    out = [w_output[:width], w_output[width:]]
    wsq = jnp.stack(
        [square(m.T) for m in [w_msg[:width]] + g0 + g1 + sq + out] + [square(m) for m in g0 + sq + out]
    )
    w_edge = jnp.pad(w_msg[width : width + edge].T.astype(bf16), ((0, rows - width), (0, 0)))
    w_time = jnp.pad(w_msg[width + edge :].T.astype(bf16), ((0, rows - width), (0, times - time_width)))
    kv_t = w_key_value.T.astype(bf16)
    pick_last = jnp.zeros((rows - width, 256), bf16).at[0, width].set(8.0).at[0, width + 1].set(1.0)

    def kv_rows(part, first):
        mem_part = jnp.pad(part[:, :width], ((0, 0), (0, 256 - width)))
        return jnp.concatenate([mem_part, pick_last if first else jnp.zeros_like(pick_last)], 0)

    wkv1 = jnp.concatenate([kv_rows(kv_t[:width], True), kv_rows(kv_t[width:], False)], 0)
    pad_time = lambda part: jnp.pad(part[:, width:], ((0, rows - width), (0, times - time_width)))
    wkv2 = jnp.concatenate([pad_time(kv_t[:width]), pad_time(kv_t[width:])], 0)
    wd = jnp.pad(w_square[3].astype(bf16), ((0, 256 - width), (0, rows - width)))
    eye = jnp.eye(256, dtype=bf16)
    freq = jnp.asarray(time_columns(time_width, times))

    packed = main(
        layout, own * nodes <= 16384, width, head_dim, slots, times,
        (flat_ids, cand_ids, positives, table, event_rows, valid, mem3, edge_feat,
         wsq, w_edge, w_time, wkv1, wkv2, wd, wd.T, eye, freq),
    )
    summed = reduce_all(own, batch, packed)

    take = partial(layout.take, summed)
    grads = (
        jnp.concatenate(
            [take("msg_mem", width, width), take("msg_edge", edge, width), take("msg_time", time_width, width)], 0
        ),
        jnp.stack([jnp.concatenate([take(f"gru{i}{g}", width, width) for g in range(3)], 1) for i in range(2)]),
        jnp.stack([take(f"square{i}", width, width) for i in range(4)]),
        jnp.concatenate(
            [
                jnp.concatenate([take("kv_mem_k", width, width), take("kv_time_k", time_width, width)], 0),
                jnp.concatenate([take("kv_mem_v", width, width), take("kv_time_v", time_width, width)], 0),
            ],
            1,
        ),
        jnp.concatenate([take("out_a", width, width), take("out_b", width, width)], 0),
    )
    step_rate = rate_coef * math.sqrt(events * own * batch)
    params = (w_msg, w_gru, w_square, w_key_value, w_output)
    moments = (mom_msg, mom_gru, mom_square, mom_key_value, mom_output)
    averages = (avg_msg, avg_gru, avg_square, avg_key_value, avg_output)
    states = [nesterov(params[i], grads[i], moments[i], averages[i], step_rate) for i in range(5)]
    return (
        (summed[layout.loss, 0], positives[0, 0], newest.reshape(-1))
        + tuple(s[0] for s in states)
        + tuple(s[1] for s in states)
        + tuple(s[2] for s in states)
    )


def solution(mesh):
    row = P(("batch", "own"))
    placed = (
        (P("own", None), P("own"), row, P(("batch", "own"), None), row, P(("batch", "own"), None))
        + (P(("batch", "own"), None, None),) * 2
        + (row,) * 3
        + (P(),) * 15
    )
    return jax.shard_map(
        local,
        mesh=mesh,
        in_specs=placed,
        out_specs=(P(), P(), P("own")) + (P(),) * 15,
        check_vma=False,
    )
```

time: 1790 us -> 333 us (0.19)
  local copies, waits for them, and re-layouts: 759 us -> 73.9 us
  other arithmetic: 406 us -> 14.4 us
  waiting for transfers between devices: 267 us -> 0 us
  Pallas kernels: 0 us -> 240 us
  matrix products: 221 us -> 0 us
  blocking collectives: 66.3 us -> 0 us
  starting transfers between devices: 35.4 us -> 0 us
    pallas_call x0 -> x3, Pallas kernels: none -> 240 us  [the longest x1 161 us: main(): pl.pallas_call(partial(main_kernel, (width, head_dim, slots, keep_kv, lay...]
    reshape x130 -> x5, local copies, waits for them, and re-layouts: 236 us -> 1.79 us  [the longest x2 0.71 us: local(): valid = nbr_mask.reshape(events, slots).T.reshape(slots, 1, events)]
    dot_general x63 -> x0, matrix products: 221 us -> none  [the longest x25 117 us: product(): return jnp.dot(left_side, right_side, preferred_element_type=jnp.float32)]
    another operation x43 -> x9, other arithmetic: 186 us -> 0.76 us
    psum x1 -> x0, waiting for transfers between devices: 122 us -> none  [local(): lax.psum((grad_msg, grad_gru, grad_square, grad_kv, grad_out, loss_local)...]
    mul x42 -> x0, local copies, waits for them, and re-layouts: 122 us -> none  [the longest x24 69.1 us: attention_backward(): grad_values = probs[..., None] * grad_heads[:, None]]
    scatter x7 -> x2, local copies, waits for them, and re-layouts: 103 us -> 2.82 us  [local(): jnp.zeros((rows - width, 256), bf16).at[0, width].set(8.0).at[0, width + 1]]
    reduce_sum x23 -> x0, other arithmetic: 93 us -> none  [the longest x16 60.9 us: node_lookup(): last_rows = jnp.sum(jnp.where(selector, node_last[None, :], 0), 1)]
  transfers between devices with their start and end apart: 11 -> 0, of which waited for: 5 -> 0; matrix products, arithmetic and copies ran while one was open for 18% -> 0% of each run, Pallas kernels for 0% -> 0%
where the time goes in v1:
time: 333 us; the launch traced here: 332 us
  Pallas kernels  240 us (72%)
  local copies, waits for them, and re-layouts  73.9 us (22%)
  other arithmetic  14.4 us (4%)
    pallas_call x1, Pallas kernels, main(): pl.pallas_call(partial(main_kernel, (width, head_dim, slots, keep_kv, lay...  161 us
    pallas_call x1, Pallas kernels, reduce_all(): pl.pallas_call(partial(reduce_kernel, own, batch, streams), out_shape=jax...  51.4 us
    unnamed x125, local copies, waits for them, and re-layouts  50.4 us
    pallas_call x1, Pallas kernels, exchange(): pl.pallas_call(partial(exchange_kernel, own, batch), out_shape=(jax.Shape...  27.7 us
    add x5, other arithmetic, nesterov(): (1.0 - avg_coef) * average + avg_coef * new_weight  10.2 us

profile of v1, /device:TPU:0, one launch (start us, length us, event | category | flops | bytes accessed | tf_op | source)
XLA Modules:
  0.0 332.0 jit_solution(11121199145022105876)
XLA Ops:
  0.7 1.3 copy.143
  13.5 1.6 constant_dynamic-update-slice_fusion
  17.1 1.5 bitcast_dynamic-update-slice_fusion.4
  23.1 1.4 scatter.6
  25.1 1.9 dynamic-slice.16
  28.3 1.4 scatter.9
  32.8 27.7 %exchange.1 = (bf16[8192,2,128]{2,1,0:T(2,128)(2,1)S(1)}, s32[8,512]{1,0:T(8,128)S(1)}, f32[8,128]{1,0:T(8,128)S(1)}, s32[1,1024]{1,0:T(1,128)S(1)}) custom-call(bf16[1024,2,128]{2,1,0:T(2,128)(2,1)S(1)} %copy.188.shard_ref, s32[1,512]{1,0:T(1,128)S(1)} %bitcast.131, s32[8,1024]{1,0:T(8,128)S(1)} %pad.107.event_ref, s32[1,1024]{1,0:T(1,128)S(1)} %bitcast.129), custom_call_target="tpu_custom_call" | custom-call | tf_op jit(solution)/shard_map/exchange/pallas_call | solution.py:237
  60.6 2.0 copy-done.1
  70.9 161.3 %train.1.grad_ref = f32[4864,128]{1,0:T(8,128)} custom-call(s32[20480]{0:T(1024)} %reshape.148.ids_ref, s32[8,512]{1,0:T(8,128)} %copy-done.3, f32[8,128]{1,0:T(8,128)} %copy-done.5, bf16[8192,2,128]{2,1,0:T(2,128)(2,1)} %copy-done.1, s32[8,1024]{1,0:T(8,128)} %copy-done.2, s32[20,1,1024]{2,1,0:T(1,128)} %reshape.151.valid_ref, ...), custom_call_target="tpu_custom_call" | custom-call | tf_op jit(solution)/shard_map/train/pallas_call | solution.py:631
  232.2 1.7 copy-done
  233.9 51.4 %reduce.17 = f32[4864,128]{1,0:T(8,128)S(1)} custom-call(f32[4864,128]{1,0:T(8,128)S(1)} %copy-done), custom_call_target="tpu_custom_call" | custom-call | tf_op jit(solution)/shard_map/reduce/pallas_call | solution.py:738
  287.6 1.8 copy.167
  289.4 1.8 copy.175
  291.3 2.4 multiply_add_fusion.4
  293.6 1.8 copy.179
  295.5 1.8 copy.183
  297.3 1.8 copy.187
  299.9 2.8 multiply_add_fusion.2
  303.4 1.3 copy.178
  304.7 1.3 copy.182
  306.0 1.3 copy.186
  307.3 2.0 concatenate.89
  309.3 2.0 concatenate.90
  311.4 2.1 fusion.3
  313.5 1.4 copy.177
  314.8 1.4 copy.181
  316.2 1.4 copy.185
  317.6 1.9 copy.164
  320.5 1.9 copy.172
  322.5 2.4 multiply_add_fusion
  324.9 1.9 copy.176
  326.8 1.9 copy.180
  (176 shorter events, 36.8 us)
Async XLA Ops:
  0.7 1.7 copy-start.13
  1.9 3.9 %copy-start.7 = (f32[2,172,516]{2,0,1:T(2,128)S(1)}, f32[2,172,516]{2,0,1:T(2,128)}, u32[]{:S(2)}) copy-start(f32[2,172,516]{2,0,1:T(2,128)} %param.43) | copy-start | bytes 2130052
  2.4 6.2 %copy-start.8 = (f32[4,172,172]{2,0,1:T(4,128)S(1)}, f32[4,172,172]{2,0,1:T(4,128)}, u32[]{:S(2)}) copy-start(f32[4,172,172]{2,0,1:T(4,128)} %param.44) | copy-start | bytes 1420036
  8.6 3.1 copy-start.30
  11.8 9.4 %copy-start.39 = (s32[2]{0:T(128)S(1)}, s32[2]{0:T(128)}, u32[]{:S(2)}) copy-start(s32[2]{0:T(128)} %constant.101.clone.1) | copy-start | bytes 28
  11.8 17.9 %copy-start.12 = (f32[272,344]{1,0:T(8,128)S(1)}, f32[272,344]{1,0:T(8,128)}, u32[]{:S(2)}) copy-start(f32[272,344]{1,0:T(8,128)} %param.45) | copy-start | bytes 1122820
  12.8 17.9 %copy-start.4 = (s32[1024]{0:T(1024)S(1)}, s32[1024]{0:T(1024)}, u32[]{:S(2)}) copy-start(s32[1024]{0:T(1024)} %param.32) | copy-start | bytes 12292
  13.5 17.2 %copy-start.10 = (f32[1024,172]{0,1:T(8,128)S(1)}, f32[1024,172]{0,1:T(8,128)}, u32[]{:S(2)}) copy-start(f32[1024,172]{0,1:T(8,128)} %param.31) | copy-start | bytes 2113540
  32.1 32.4 %copy-start.29 = (bf16[172,172]{1,0:T(8,128)(2,1)S(1)}, bf16[172,172]{1,0:T(8,128)(2,1)}, u32[]{:S(2)}) copy-start(bf16[172,172]{1,0:T(8,128)(2,1)} %get-tuple-element.182) | copy-start | bytes 177508
  32.6 35.0 %copy-start.28 = (bf16[1024,172]{0,1:T(8,128)(2,1)S(1)}, bf16[1024,172]{0,1:T(8,128)(2,1)}, u32[]{:S(2)}) copy-start(bf16[1024,172]{0,1:T(8,128)(2,1)} %param.34) | copy-start | bytes 1056772
  32.6 36.0 %copy-start.34 = (s32[1024,4]{0,1:T(4,128)S(1)}, s32[1024,4]{0,1:T(4,128)}, u32[]{:S(2)}) copy-start(s32[1024,4]{0,1:T(4,128)} %param.36) | copy-start | bytes 49156
  32.6 36.0 %copy-start.32 = (s32[1024,4,5]{0,1,2:T(4,128)S(1)}, s32[1024,4,5]{0,1,2:T(4,128)}, u32[]{:S(2)}) copy-start(s32[1024,4,5]{0,1,2:T(4,128)} %param.37) | copy-start | bytes 245764
  32.8 36.0 %copy-start.2 = (s32[8,1024]{1,0:T(8,128)}, s32[8,1024]{1,0:T(8,128)S(1)}, u32[]{:S(2)}) copy-start(s32[8,1024]{1,0:T(8,128)S(1)} %pad.107.event_ref) | copy-start | bytes 98308
  60.5 2.0 copy-start.1
  63.7 5.7 %copy-start.33 = (s32[1024,4,5]{0,1,2:T(4,128)S(1)}, s32[1024,4,5]{0,1,2:T(4,128)}, u32[]{:S(2)}) copy-start(s32[1024,4,5]{0,1,2:T(4,128)} %param.38) | copy-start | bytes 245764
  232.2 1.7 copy-start
  299.1 3.5 %copy-start.23 = (f32[172,128]{1,0:T(8,128)S(1)}, f32[172,128]{1,0:T(8,128)}, u32[]{:S(2)}) copy-start(f32[172,128]{1,0:T(8,128)} %get-tuple-element.124) | copy-start | bytes 264196
  299.1 3.5 %copy-start.27 = (f32[172,44]{1,0:T(8,128)S(1)}, f32[172,44]{1,0:T(8,128)}, u32[]{:S(2)}) copy-start(f32[172,44]{1,0:T(8,128)} %get-tuple-element.140) | copy-start | bytes 90820
  299.8 2.9 copy-start.22
  299.8 2.9 copy-start.26
  299.8 2.9 copy-start.21
  299.8 2.9 copy-start.25
  299.8 3.0 copy-start.20
  299.8 3.0 copy-start.24
  299.8 3.0 copy-start.9
  299.8 3.0 copy-start.15
  299.9 3.0 copy-start.16
  314.8 4.7 %copy-start.14 = (f32[444,172]{0,1:T(8,128)S(1)}, f32[444,172]{0,1:T(8,128)}, u32[]{:S(2)}) copy-start(f32[444,172]{0,1:T(8,128)} %param.42) | copy-start | bytes 916420
  316.2 6.3 %copy-start.17 = (f32[172,128]{1,0:T(8,128)S(1)}, f32[172,128]{1,0:T(8,128)}, u32[]{:S(2)}) copy-start(f32[172,128]{1,0:T(8,128)} %get-tuple-element.132) | copy-start | bytes 264196
  316.2 6.3 %copy-start.18 = (f32[172,44]{1,0:T(8,128)S(1)}, f32[172,44]{1,0:T(8,128)}, u32[]{:S(2)}) copy-start(f32[172,44]{1,0:T(8,128)} %get-tuple-element.147) | copy-start | bytes 90820
  316.2 6.3 %copy-start.19 = (f32[172,44]{1,0:T(8,128)S(1)}, f32[172,44]{1,0:T(8,128)}, u32[]{:S(2)}) copy-start(f32[172,44]{1,0:T(8,128)} %get-tuple-element.148) | copy-start | bytes 90820
  316.2 6.3 %copy-start.31 = (f32[100,44]{1,0:T(8,128)S(1)}, f32[100,44]{1,0:T(8,128)}, u32[]{:S(2)}) copy-start(f32[100,44]{1,0:T(8,128)} %get-tuple-element.154) | copy-start | bytes 52804
  (8 other events, 5.6 us)

commit v2 on v1

--- a/solution.py
+++ b/solution.py
@@ -48,12 +48,6 @@
     return index + size * (1 - 2 * (lax.div(index, size) % 2))
 
 
-def nesterov(weight, gradient, moment, average, step_rate):
-    new_moment = mu_coef * moment + gradient
-    new_weight = weight - step_rate * (gradient + mu_coef * new_moment)
-    return (new_moment, new_weight, (1.0 - avg_coef) * average + avg_coef * new_weight)
-
-
 def time_columns(time_width, rows):
     turns = 10.0 ** (-np.linspace(0.0, 9.0, time_width)) / (2.0 * np.pi)
     mant, expo = np.frexp(turns)
@@ -102,10 +96,19 @@
         )
 
 
+SQUARES = (
+    "g0r g0z g0n g1r g1z g1n s0t s1t s2t g0r_back g0z_back g0n_back s0 s1 s2 oa ob".split()
+)
+
+
 def exchange_kernel(
-    own, batch, shard_ref, cand_ref, event_ref, last_ref,
-    table_ref, ids_ref, pos_ref, newest_ref,
-    batch_buf, own_buf, local_sem, table_send, table_recv, batch_send, batch_recv, own_send, own_recv,
+    own, batch,
+    mem_ref, last_ref, cand_ref, time_ref, mask_ref, src_ref, owner_ref, nbr_ref,
+    msg_ref, gru_ref, square_ref, kv_ref, outw_ref,
+    table_ref, ids_ref, flat_ref, pos_ref, newest_ref, mem3_ref,
+    wsq_ref, wmsg_ref, wout_ref, wkv1_ref, wkv2_ref, wd_ref, wdt_ref,
+    shard, ext, pairs, square_pad, wide_pad, kv_pad, batch_buf, own_buf,
+    local_sem, table_send, table_recv, batch_send, batch_recv, own_send, own_recv,
 ):
     me = lax.axis_index("own")
     group = lax.axis_index("batch")
@@ -114,9 +117,33 @@
         pl.semaphore_signal(barrier, inc=1, device_id=(group, lax.rem(me + step, own)), device_id_type=MESH)
     for step in range(1, batch):
         pl.semaphore_signal(barrier, inc=1, device_id=(lax.rem(group + step, batch), me), device_id_type=MESH)
+
+    width, nodes = mem_ref.shape
+    rows = pad_to(width, 16)
+    ext[...] = jnp.zeros_like(ext)
+    ext[0:width, :] = mem_ref[...]
+    last = last_ref[...]
+    ext[width : width + 1, :] = lax.div(last, 8).astype(f32)
+    ext[width + 1 : width + 2, :] = lax.rem(last, 8).astype(f32)
+
+    def turn(i, unused):
+        block = ext[:, pl.ds(pl.multiple_of(i * 128, 128), 128)].T
+        base = pl.multiple_of(i * 256, 256)
+        pairs[pl.ds(base, 128, stride=2), :] = block[:, :128]
+        pairs[pl.ds(base + 1, 128, stride=2), :] = block[:, 128:]
+        return unused
+
+    lax.fori_loop(0, nodes // 128, turn, 0)
+
+    def pack(i, unused):
+        got = [pairs[pl.ds(pl.multiple_of(i * 128, 128) + 2 * k, 2), :] for k in range(64)]
+        for k in range(64):
+            shard[i * 64 + k] = got[k].astype(bf16)
+        return unused
+
+    lax.fori_loop(0, nodes // 64, pack, 0)
     pl.semaphore_wait(barrier, own + batch - 2)
 
-    nodes = shard_ref.shape[0]
     half = nodes // 2
     bits = own.bit_length() - 1
     rest = list(range(1, bits))
@@ -129,11 +156,11 @@
         for b in range(bits):
             if pattern >> b & 1:
                 source = flip_bit(source, b)
-        rows = pl.ds(pl.multiple_of(source * nodes + stream * half, half), half)
+        part = pl.ds(pl.multiple_of(source * nodes + stream * half, half), half)
         slot = pattern | 1 << bit
-        src = shard_ref.at[pl.ds(stream * half, half)] if pattern == 0 else table_ref.at[rows]
+        src = shard.at[pl.ds(stream * half, half)] if pattern == 0 else table_ref.at[part]
         return pltpu.make_async_remote_copy(
-            src_ref=src, dst_ref=table_ref.at[rows],
+            src_ref=src, dst_ref=table_ref.at[part],
             send_sem=table_send.at[stream, slot], recv_sem=table_recv.at[stream, slot],
             device_id=(group, peer), device_id_type=MESH,
         )
@@ -146,13 +173,13 @@
             copy.start()
             copies[stream][1 << bit] = copy
     mine = pltpu.make_async_copy(
-        shard_ref, table_ref.at[pl.ds(pl.multiple_of(me * nodes, nodes), nodes)], local_sem
+        shard, table_ref.at[pl.ds(pl.multiple_of(me * nodes, nodes), nodes)], local_sem
     )
     mine.start()
 
-    events = event_ref.shape[1]
-    time_row = event_ref[0:1, :].astype(f32)
-    src_row = event_ref[2:3, :]
+    events = src_ref.shape[1]
+    time_row = time_ref[...].astype(f32)
+    src_row = src_ref[...]
     best = []
     tile = 256
     for start in range(0, nodes, tile):
@@ -163,8 +190,8 @@
             top = jnp.maximum(top, jnp.where(hit, time_row[:, lane : lane + 128], -1.0))
         best.append(jnp.max(top.T, 0, keepdims=True))
     newest = jnp.concatenate(best, 1).astype(jnp.int32)
-    newest = jnp.maximum(newest, last_ref[0:1, :])
-    count = jnp.sum(event_ref[1:2, :].astype(f32), 1, keepdims=True).astype(jnp.int32)
+    newest = jnp.maximum(newest, last)
+    count = jnp.sum(mask_ref[...].astype(f32), 1, keepdims=True).astype(jnp.int32)
     batch_buf[0, 0:1, :] = newest
     batch_buf[0, 1:2, :] = jnp.broadcast_to(count, (1, nodes))
 
@@ -178,6 +205,65 @@
     peers = [peer_copy(step) for step in range(1, batch)]
     for copy in peers:
         copy.start()
+
+    picks = owner_ref.shape[0]
+    per_pick = nbr_ref.shape[0]
+    for s in range(per_pick):
+        flat = owner_ref[...] * nodes + nbr_ref[s]
+        for block in range(events // 128):
+            at = (s * (events // 128) + block) * picks
+            flat_ref[at : at + picks, :] = flat[:, block * 128 : block * 128 + 128]
+    whole = ext[0:rows, :]
+    part0 = whole.astype(bf16)
+    whole = whole - part0.astype(f32)
+    part1 = whole.astype(bf16)
+    mem3_ref[0:rows, :] = part0
+    mem3_ref[rows : 2 * rows, :] = part1
+    mem3_ref[2 * rows :, :] = (whole - part1.astype(f32)).astype(bf16)
+
+    square_pad[...] = jnp.zeros_like(square_pad)
+
+    def put(name, value):
+        square_pad[0:width, 0:width] = value
+        wsq_ref[SQUARES.index(name)] = square_pad[...].astype(bf16)
+
+    for index in range(2):
+        for gate, letter in enumerate("rzn"):
+            value = gru_ref[:, index, gate * width : gate * width + width]
+            put(f"g{index}{letter}", value.T)
+            if index == 0:
+                put(f"g0{letter}_back", value)
+    for index in range(3):
+        value = square_ref[:, index, :]
+        put(f"s{index}", value)
+        put(f"s{index}t", value.T)
+    put("oa", outw_ref[:, 0:width].T)
+    put("ob", outw_ref[:, width : 2 * width].T)
+    wide_pad[...] = jnp.zeros_like(wide_pad)
+    wide_pad[0:width, 0 : 2 * width] = outw_ref[...]
+    wout_ref[...] = wide_pad[:, 0 : wout_ref.shape[1]].astype(bf16)
+    wide_pad[0:width, 0 : msg_ref.shape[1]] = msg_ref[...]
+    wmsg_ref[...] = wide_pad[...].astype(bf16)
+    last_square = square_ref[:, 3, :]
+    kv_pad[...] = jnp.zeros_like(kv_pad)
+    kv_pad[0:width, 0:width] = last_square
+    wd_ref[...] = kv_pad[0 : wd_ref.shape[0], 0 : wd_ref.shape[1]].astype(bf16)
+    kv_pad[0:width, 0:width] = last_square.T
+    wdt_ref[...] = kv_pad[0 : wdt_ref.shape[0], 0 : wdt_ref.shape[1]].astype(bf16)
+    times = wkv2_ref.shape[1]
+    time_width = kv_ref.shape[0] - width
+    lane = lax.broadcasted_iota(jnp.int32, (1, 256), 1)
+    for index in range(2):
+        part = kv_ref[:, index * width : index * width + width]
+        kv_pad[index * rows : index * rows + width, 0:width] = part[0:width].T
+    kv_pad[width : width + 1, :] = jnp.where(lane == width, 8.0, jnp.where(lane == width + 1, 1.0, 0.0))
+    wkv1_ref[...] = kv_pad[...].astype(bf16)
+    kv_pad[...] = jnp.zeros_like(kv_pad)
+    for index in range(2):
+        part = kv_ref[:, index * width : index * width + width]
+        kv_pad[index * rows : index * rows + width, 0:time_width] = part[width:].T
+    wkv2_ref[...] = kv_pad[:, 0:times].astype(bf16)
+
     total = count
     for step, copy in enumerate(peers, 1):
         copy.wait_recv()
@@ -185,9 +271,9 @@
         total = total + batch_buf[step, 1:2, 0:1]
     newest_ref[...] = newest
 
-    width = cand_ref.shape[1]
+    cands = cand_ref.shape[1]
     own_buf[0, 0:1, :] = cand_ref[...] + me * nodes
-    own_buf[0, 1:2, :] = jnp.broadcast_to(total, (1, width))
+    own_buf[0, 1:2, :] = jnp.broadcast_to(total, (1, cands))
 
     def owner_copy(step):
         return pltpu.make_async_remote_copy(
@@ -208,18 +294,21 @@
                 held = held + [p | 1 << bit for p in held]
             for pattern in held:
                 slot = pattern | 1 << order[step]
-                copies[stream][slot].wait_recv() if slot in copies[stream] else None
+                copies[stream][slot].wait_recv()
                 for bit in order[step + 1 :]:
                     copy = shard_copy(stream, slot, bit)
                     copy.start()
                     copies[stream][slot | 1 << bit] = copy
 
-    ids_ref[pl.ds(me, 1), :] = own_buf[0, 0:1, :]
-    for step, copy in enumerate(owners, 1):
-        copy.wait_recv()
+    for step in range(own):
+        if step:
+            owners[step - 1].wait_recv()
+            total = total + own_buf[step, 1:2, 0:1]
         source = lax.rem(me - step + own, own)
-        ids_ref[pl.ds(source, 1), :] = own_buf[step, 0:1, :]
-        total = total + own_buf[step, 1:2, 0:1]
+        for block in range(cands // 128):
+            ids_ref[pl.ds(source * (cands // 128) + block, 1), :] = own_buf[
+                step, 0:1, block * 128 : block * 128 + 128
+            ]
     pos_ref[...] = jnp.broadcast_to(jnp.maximum(total.astype(f32), 1.0), pos_ref.shape)
     mine.wait()
     for copy in peers + owners:
@@ -229,24 +318,46 @@
             copies[stream][slot].wait_send()
 
 
-def exchange(own, batch, shard, cand, event_rows, last):
-    nodes = shard.shape[0]
-    width = cand.shape[1]
+def exchange(own, batch, args):
+    mem, last, cand, time, mask, src, owner, nbr, msg, gru, square, kv, outw = args
+    width, nodes = mem.shape
+    events = src.shape[1]
+    cands = cand.shape[1]
+    rows = pad_to(width, 16)
+    times = pad_to(kv.shape[0] - width, 16)
+    wide = pad_to(msg.shape[1], 16)
     vmem = pl.BlockSpec(memory_space=pltpu.VMEM)
     hbm = pl.BlockSpec(memory_space=pl.ANY)
+    low = lambda *shape: jax.ShapeDtypeStruct(shape, bf16)
+    whole = lambda *shape: jax.ShapeDtypeStruct(shape, jnp.int32)
     return pl.pallas_call(
         partial(exchange_kernel, own, batch),
         out_shape=(
-            jax.ShapeDtypeStruct((own * nodes, 2, 128), bf16),
-            jax.ShapeDtypeStruct((own, width), jnp.int32),
+            low(own * nodes, 2, 128),
+            whole(own * cands // 128, 128),
+            whole(nbr.shape[0] * nbr.shape[1] * events // 128, 128),
             jax.ShapeDtypeStruct((8, 128), f32),
-            jax.ShapeDtypeStruct((1, nodes), jnp.int32),
+            whole(1, nodes),
+            low(3 * rows, nodes),
+            low(len(SQUARES), rows, rows),
+            low(rows, wide),
+            low(rows, 2 * rows),
+            low(2 * rows, 256),
+            low(2 * rows, times),
+            low(256, rows),
+            low(rows, 256),
         ),
-        in_specs=[hbm, vmem, vmem, vmem],
-        out_specs=(hbm, vmem, vmem, vmem),
+        in_specs=[vmem] * len(args),
+        out_specs=(hbm,) + (vmem,) * 12,
         scratch_shapes=[
+            pltpu.VMEM((nodes, 2, 128), bf16),
+            pltpu.VMEM((256, nodes), f32),
+            pltpu.VMEM((2 * nodes, 128), f32),
+            pltpu.VMEM((rows, rows), f32),
+            pltpu.VMEM((rows, wide), f32),
+            pltpu.VMEM((2 * rows, 256), f32),
             pltpu.VMEM((batch, 8, nodes), jnp.int32),
-            pltpu.VMEM((own, 8, width), jnp.int32),
+            pltpu.VMEM((own, 8, cands), jnp.int32),
             pltpu.SemaphoreType.DMA,
             pltpu.SemaphoreType.DMA((2, own)),
             pltpu.SemaphoreType.DMA((2, own)),
@@ -256,87 +367,102 @@
             pltpu.SemaphoreType.DMA((own,)),
         ],
         compiler_params=pltpu.CompilerParams(
-            collective_id=1, has_side_effects=True, vmem_limit_bytes=32 * 2**20
+            collective_id=1, has_side_effects=True, vmem_limit_bytes=63 * 2**20
         ),
         name="exchange",
-    )(shard, cand, event_rows, last)
+    )(*args)
 
 
 class Layout:
-    def __init__(self, width, edge, time_width, fold):
-        rows = pad_to(width, 16)
-        times = pad_to(time_width, 16)
-        edges = pad_to(edge, 16)
-        assert width <= 192 and edges == rows
-        names = ["msg_mem", "msg_edge"]
-        names += [f"gru{i}{g}" for i in range(2) for g in range(3)]
-        names += [f"square{i}" for i in range(4)]
-        names += ["kv_mem_k", "kv_mem_v", "out_a", "out_b"]
-        sizes = [(n, rows) for n in names] + [("kv_time_k", times), ("kv_time_v", times), ("msg_time", times)]
-        self.at = {}
+    def __init__(self, width, wide, deep, gates, kv_rows, kv_cols, fold):
+        rows = pad_to(width, 8)
+        self.width = width
+        self.pieces = {}
         row = 0
-        for name, size in sizes:
-            self.at[name] = [row, size, None, None]
-            row += size
-        for index, (name, size) in enumerate(sizes):
-            if index % 2 == 0:
-                self.at[name][2:] = [row, 0]
-                row += size
-            else:
-                before = self.at[sizes[index - 1][0]]
-                assert before[1] == size
-                self.at[name][2:] = [before[2], 64]
+        for name, depth, columns in (
+            ("msg", width, wide),
+            ("out", width, deep),
+            ("kv", kv_rows, kv_cols),
+            ("gru0", width, gates),
+            ("gru1", width, gates),
+            ("square0", width, width),
+            ("square1", width, width),
+            ("square2", width, width),
+            ("square3", width, width),
+        ):
+            tiles = []
+            for column in range(0, columns, 128):
+                size = min(128, columns - column)
+                if size < 128 and name[:3] in ("gru", "squ"):
+                    tiles.append([column, size, None, None])
+                else:
+                    tiles.append([column, size, row, 0])
+                    row += pad_to(depth, 8)
+            self.pieces[name] = (depth, tiles)
+        host = self.pieces["msg"][1][-1]
+        lane = pad_to(host[1], 8)
+        for name in ("gru0", "gru1"):
+            tile = self.pieces[name][1][-1]
+            if tile[2] is None:
+                assert lane + tile[1] <= 128
+                tile[2:] = [host[2], lane]
+                lane += tile[1]
+        for pair in range(2):
+            for side in range(2):
+                tile = self.pieces[f"square{2 * pair + side}"][1][-1]
+                assert tile[1] <= 64
+                tile[2:] = [row, 64 * side]
+            row += rows
         self.loss = row
         row += 8
         self.total = pad_to(row, fold)
-        self.unused = row
 
     def put(self, ref, name, value):
-        first, size, second, lane = self.at[name]
-        ref[first : first + size, :] = value[:, :128]
-        ref[second : second + size, lane : lane + value.shape[1] - 128] = value[:, 128:]
-
-    def take(self, packed, name, rows, width):
-        first, size, second, lane = self.at[name]
-        return jnp.concatenate(
-            [packed[first : first + rows, :128], packed[second : second + rows, lane : lane + width - 128]], 1
-        )
+        depth, tiles = self.pieces[name]
+        for column, size, row, lane in tiles:
+            ref[row : row + depth, lane : lane + size] = value[:depth, column : column + size]
+
+    def tiles(self, ref, name):
+        depth, tiles = self.pieces[name]
+        for column, size, row, lane in tiles:
+            yield slice(column, column + size), ref[row : row + depth, lane : lane + size]
 
 
 def main_kernel(
     dims,
-    ids_ref, cand_ref, pos_ref, table_ref, event_ref, valid_ref, mem3_ref, edge_ref,
-    wsq_ref, wme_ref, wtime_ref, wkv1_ref, wkv2_ref, wd_ref, wdt_ref, eye_ref, freq_ref,
+    ids_ref, cand_ref, pos_ref, table_ref, time_ref, mask_ref, src_ref, target_ref, valid_ref, mem3_ref, edge_ref,
+    wsq_ref, wmsg_ref, wout_ref, wkv1_ref, wkv2_ref, wd_ref, wdt_ref, freq_ref,
     grad_ref,
-    xs, x_all, t_all, kv_all, score, dest_rows, slab,
-    t_src, mem_low, hidden, fresh_low, att_low, mixed_low, hid_out, emb, emb_rows,
+    xs, x_all, t_all, kv_all, score, dest_rows, slab, eye_ref, stage,
+    x_msg, mem_low, hidden, fresh_low, att_low, x_out, hid_out, emb, emb_rows,
     mem_src, pre_msg, reset_gate, update, cand_act, gate_n, queries, attended, pre_out,
     acc_a, grad_att, gkv_m, gkv_t, rows_ref,
 ):
-    width, head_dim, slots, keep_kv, layout = dims
-    events = event_ref.shape[1]
+    width, head_dim, keep_kv, cand_width, layout = dims
+    events = time_ref.shape[1]
+    per_pick, picks = valid_ref.shape[:2]
+    slots = per_pick * picks
     rows = pad_to(width, 16)
-    times = t_src.shape[0]
+    times = wkv2_ref.shape[1]
+    wide = wmsg_ref.shape[1]
+    time_width = layout.pieces["kv"][0] - width
+    edge = edge_ref.shape[0]
     heads = Heads(head_dim, rows)
     scale = head_dim ** (-0.5)
     high, low = freq_ref[:, 0:1], freq_ref[:, 1:2]
     chunks = events // LANES
-    owners, cand_width = cand_ref.shape
-    W = {}
-    order = ["wm_m", "g0r", "g0z", "g0n", "g1r", "g1z", "g1n", "s0t", "s1t", "s2t", "oat", "obt",
-             "g0r_", "g0z_", "g0n_", "s0", "s1", "s2", "oa", "ob"]
-    for index, name in enumerate(order):
-        W[name] = index
+    owners = cand_ref.shape[0] // cand_width
 
     def w(name):
-        return wsq_ref[W[name]]
+        return wsq_ref[SQUARES.index(name)]
 
     def gather(read_id, count):
-        unroll = 64
+        unroll = 128
 
         def body(i, unused):
             base = i * unroll
-            got = [table_ref[read_id(base + k)] for k in range(unroll)]
+            first = read_id(i)
+            got = [table_ref[first(k)] for k in range(unroll)]
             for k in range(unroll):
                 xs[pl.ds(pl.multiple_of(2 * base, 2 * unroll) + 2 * k, 2), :] = got[k].astype(f32)
             return unused
@@ -349,10 +475,15 @@
             [xs[pl.ds(base, count, stride=2), :], xs[pl.ds(base + 1, count, stride=2), :]], 1
         ).astype(bf16)
 
-    grad_ref[...] = jnp.zeros_like(grad_ref)
+    grad_ref[layout.loss :, :] = jnp.zeros_like(grad_ref[layout.loss :, :])
+    host = layout.pieces["msg"][1][-1][2]
+    grad_ref[host : host + rows, :] = jnp.zeros((rows, 128), f32)
+    eye = lax.broadcasted_iota(jnp.int32, (256, 256), 0) == lax.broadcasted_iota(jnp.int32, (256, 256), 1)
+    eye_ref[...] = eye.astype(f32).astype(bf16)
+    stage[...] = jnp.zeros_like(stage)
 
     def cand_body(o, unused):
-        gather(lambda i: cand_ref[o, i], cand_width)
+        gather(lambda i: lambda k: cand_ref[o * cand_width + i * 128 + k], cand_width)
         at = pl.multiple_of(o * cand_width, cand_width)
         dest_rows[pl.ds(at, cand_width), :] = gathered(0, cand_width)
         return unused
@@ -365,16 +496,19 @@
     def gru_body(c, unused):
         cs = lanes(c)
         node = lax.broadcasted_iota(jnp.int32, (mem3_ref.shape[1], LANES), 0)
-        onehot = (node == event_ref[2:3, cs]).astype(f32).astype(bf16)
+        onehot = (node == src_ref[:, cs]).astype(f32).astype(bf16)
         parts = nn(mem3_ref[...], onehot)
         mem = parts[:rows] + parts[rows : 2 * rows] + parts[2 * rows :]
         mem_src[:, cs] = mem
-        delta = event_ref[0:1, cs].astype(f32) - mem[width : width + 1]
-        t_low = cos_rows(delta, high, low).astype(bf16)
-        t_src[:, cs] = t_low
+        delta = time_ref[:, cs].astype(f32) - 8.0 * mem[width : width + 1] - mem[width + 1 : width + 2]
+        stage[0:width, :] = mem[0:width]
+        stage[width : width + edge, :] = edge_ref[:, cs].astype(f32)
+        stage[width + edge : width + edge + time_width, :] = cos_rows(delta, high, low)[0:time_width]
+        x = stage[...].astype(bf16)
+        x_msg[:, cs] = x
         m_low = mem.astype(bf16)
         mem_low[:, cs] = m_low
-        pre = nn(w("wm_m"), m_low) + nt(wme_ref[...], edge_ref[cs, :]) + nn(wtime_ref[...], t_low)
+        pre = nn(wmsg_ref[...], x)
         pre_msg[:, cs] = pre
         hid = (pre * jax.nn.sigmoid(pre)).astype(bf16)
         hidden[:, cs] = hid
@@ -394,26 +528,33 @@
     lax.fori_loop(0, chunks, gru_body, 0)
 
     def slot_body(j, unused):
-        gather(lambda i: ids_ref[j * events + i], events)
+        pick = lax.rem(j, picks)
+        round_ = lax.div(j, picks)
+
+        def first(i):
+            base = ((round_ * (events // 128) + i) * picks + pick) * 128
+            return lambda k: ids_ref[base + k]
+
+        gather(first, events)
 
         def chunk_body(c, unused):
             cs = lanes(c)
             x = gathered(c * LANES, LANES)
             x_all[j, cs, :] = x
             kv = nt(wkv1_ref[...], x)
-            delta = event_ref[0:1, cs].astype(f32) - kv[width : width + 1]
+            delta = time_ref[:, cs].astype(f32) - kv[width : width + 1]
             t_low = cos_rows(delta, high, low).astype(bf16)
             t_all[j, :, cs] = t_low
             kv = (kv + nn(wkv2_ref[...], t_low)).astype(bf16)
             if keep_kv:
                 kv_all[j, :, cs] = kv
             s0, s1 = heads.sums(kv[:rows].astype(f32) * queries[:, cs].astype(f32))
-            live = valid_ref[j, :, cs] > 0
+            live = valid_ref[round_, pl.ds(pick, 1), cs] > 0
             score[j, 0:1, cs] = jnp.where(live, s0 * scale, mask_fill)
             score[j, 1:2, cs] = jnp.where(live, s1 * scale, mask_fill)
             return unused
 
-        lax.fori_loop(0, chunks, chunk_body, 0)
+        lax.fori_loop(0, chunks, chunk_body, 0, unroll=True)
         return unused
 
     lax.fori_loop(0, slots, slot_body, 0)
@@ -449,9 +590,11 @@
 
     def out_body(c, unused):
         cs = lanes(c)
-        mixed = nn(w("s1t"), att_low[:, cs]).astype(bf16)
-        mixed_low[:, cs] = mixed
-        pre = nn(w("oat"), mixed) + nn(w("obt"), fresh_low[:, cs])
+        stage[0:width, :] = nn(w("s1t"), att_low[:, cs])[0:width]
+        stage[width : 2 * width, :] = fresh_low[:, cs].astype(f32)[0:width]
+        x = stage[0 : 2 * rows, :].astype(bf16)
+        x_out[:, cs] = x
+        pre = nn(wout_ref[...], x)
         pre_out[:, cs] = pre
         hid = (pre * jax.nn.sigmoid(pre)).astype(bf16)
         hid_out[:, cs] = hid
@@ -487,16 +630,16 @@
             rows_ref[1:2, cs] = rows_ref[1:2, cs] * jnp.exp(old - top) + jnp.sum(
                 jnp.exp(logits - top), 0, keepdims=True
             )
-            hit = lax.broadcasted_iota(jnp.int32, logits.shape, 0) == event_ref[3:4, cs] - o * cand_width
+            hit = lax.broadcasted_iota(jnp.int32, logits.shape, 0) == target_ref[:, cs] - o * cand_width
             rows_ref[2:3, cs] = rows_ref[2:3, cs] + jnp.sum(jnp.where(hit, logits, 0.0), 0, keepdims=True)
             return unused
 
-        lax.fori_loop(0, chunks, chunk, 0)
+        lax.fori_loop(0, chunks, chunk, 0, unroll=True)
         return unused
 
     lax.fori_loop(0, owners, lse_block, 0)
 
-    mask_row = event_ref[1:2, :].astype(f32)
+    mask_row = mask_ref[...].astype(f32)
     log_sum = rows_ref[0:1, :] + jnp.log(rows_ref[1:2, :])
     rows_ref[3:4, :] = log_sum
     rows_ref[4:5, :] = mask_row / jnp.broadcast_to(pos_ref[0:1, 0:1], mask_row.shape)
@@ -513,14 +656,14 @@
             cs = lanes(c)
             logits = nn(dest, emb[:, cs])
             coeff = rows_ref[4:5, cs]
-            hit = lax.broadcasted_iota(jnp.int32, logits.shape, 0) == event_ref[3:4, cs] - o * cand_width
+            hit = lax.broadcasted_iota(jnp.int32, logits.shape, 0) == target_ref[:, cs] - o * cand_width
             grad = jnp.exp(logits - rows_ref[3:4, cs]) - jnp.where(hit, 1.0, 0.0)
             grad = (grad * coeff).astype(bf16)
             slab[0:cand_width, cs] = grad
             acc_a[:, cs] += nn(dest_t, grad)
             return unused
 
-        lax.fori_loop(0, chunks, chunk, 0)
+        lax.fori_loop(0, chunks, chunk, 0, unroll=True)
         grad_dest = nn(slab[0:cand_width, :], emb_rows[...]).astype(bf16)
         return grad_dest_w + nn(block_t, grad_dest)[:rows]
 
@@ -549,8 +692,7 @@
 
     lax.fori_loop(0, chunks, out_back, 0)
     layout.put(grad_ref, "square2", nt(hid_out[...], slab[r0, :]))
-    layout.put(grad_ref, "out_a", nt(mixed_low[...], slab[r1, :]))
-    layout.put(grad_ref, "out_b", nt(fresh_low[...], slab[r1, :]))
+    layout.put(grad_ref, "out", nt(slab[r1, :], x_out[...]))
     layout.put(grad_ref, "square1", nt(att_low[...], slab[r2, :]))
 
     attended[...] = jnp.zeros_like(attended)
@@ -579,11 +721,10 @@
 
     lax.fori_loop(0, slots, slot_back, 0)
     gm = gkv_m[...].T
-    layout.put(grad_ref, "kv_mem_k", gm[:rows, :rows])
-    layout.put(grad_ref, "kv_mem_v", gm[:rows, rows:])
     gt = gkv_t[...].T
-    layout.put(grad_ref, "kv_time_k", gt[:times, :rows])
-    layout.put(grad_ref, "kv_time_v", gt[:times, rows:])
+    both = [jnp.concatenate([g[:depth, :width], g[:depth, rows : rows + width]], 1)
+            for g, depth in ((gm, width), (gt, time_width))]
+    layout.put(grad_ref, "kv", jnp.concatenate(both, 0))
 
     def gru_back(c, unused):
         cs = lanes(c)
@@ -598,38 +739,36 @@
         gh = (act * r).astype(bf16)
         slab[r1, cs] = gr
         slab[r2, cs] = gu
-        mixed_low[:, cs] = gn
+        x_out[0:rows, cs] = gn
         hid_out[:, cs] = gh
         pre = pre_msg[:, cs]
         sig = jax.nn.sigmoid(pre)
-        back = nn(w("g0r_"), gr) + nn(w("g0z_"), gu) + nn(w("g0n_"), gn)
+        back = nn(w("g0r_back"), gr) + nn(w("g0z_back"), gu) + nn(w("g0n_back"), gn)
         att_low[:, cs] = (back * (sig * (1.0 + pre * (1.0 - sig)))).astype(bf16)
         return unused
 
     lax.fori_loop(0, chunks, gru_back, 0)
     layout.put(grad_ref, "square0", nt(fresh_low[...], slab[r0, :]))
-    for index, (left, last) in enumerate(((hidden, mixed_low), (mem_low, hid_out))):
-        layout.put(grad_ref, f"gru{index}0", nt(left[...], slab[r1, :]))
-        layout.put(grad_ref, f"gru{index}1", nt(left[...], slab[r2, :]))
-        layout.put(grad_ref, f"gru{index}2", nt(left[...], last[...]))
-    layout.put(grad_ref, "msg_mem", nt(mem_low[...], att_low[...]))
-    layout.put(grad_ref, "msg_time", nt(t_src[...], att_low[...]))
-    edge_back = nn(att_low[...], edge_ref[...])
-    edge_back = jnp.concatenate([edge_back, jnp.zeros((rows, 256 - edge_back.shape[1]), f32)], 1)
-    edge_back = jnp.concatenate([edge_back, jnp.zeros((256 - rows, 256), f32)], 0).T
-    layout.put(grad_ref, "msg_edge", edge_back[:rows, :rows])
-
-
-def main(layout, keep_kv, width, head_dim, slots, times, args):
+    for index, (left, last) in enumerate(((hidden, x_out[0:rows, :]), (mem_low, hid_out[...]))):
+        left = left[...]
+        parts = [nt(left, slab[r1, :]), nt(left, slab[r2, :]), nt(left, last)]
+        layout.put(grad_ref, f"gru{index}", jnp.concatenate([p[:, :width] for p in parts], 1))
+    layout.put(grad_ref, "msg", nt(att_low[...], x_msg[...]))
+
+
+def main(layout, keep_kv, width, head_dim, cand_width, args):
     events = args[4].shape[1]
+    slots = args[8].shape[0] * args[8].shape[1]
+    wide = args[12].shape[1]
+    times = args[15].shape[1]
     rows = pad_to(width, 16)
-    cands = args[1].shape[0] * args[1].shape[1]
+    cands = args[1].shape[0]
     smem = pl.BlockSpec(memory_space=pltpu.SMEM)
     vmem = pl.BlockSpec(memory_space=pltpu.VMEM)
     low = lambda *shape: pltpu.VMEM(shape, bf16)
     full = lambda *shape: pltpu.VMEM(shape, f32)
     return pl.pallas_call(
-        partial(main_kernel, (width, head_dim, slots, keep_kv, layout)),
+        partial(main_kernel, (width, head_dim, keep_kv, cand_width, layout)),
         out_shape=jax.ShapeDtypeStruct((layout.total, 128), f32),
         in_specs=[smem, smem] + [vmem] * (len(args) - 2),
         out_specs=vmem,
@@ -640,10 +779,14 @@
             low(slots if keep_kv else 1, 2 * rows if keep_kv else 16, events),
             full(slots, 8, events),
             low(cands, 256),
-            low(max(3 * rows, args[1].shape[1]), events),
-            low(times, events),
+            low(max(3 * rows, cand_width), events),
+            low(256, 256),
+            full(wide, LANES),
+            low(wide, events),
         ]
-        + [low(rows, events)] * 7
+        + [low(rows, events)] * 4
+        + [low(2 * rows, events)]
+        + [low(rows, events)] * 2
         + [low(events, rows)]
         + [full(rows, events)] * 6
         + [low(rows, events)]
@@ -747,10 +890,49 @@
             pltpu.SemaphoreType.DMA((2, count)),
         ],
         compiler_params=pltpu.CompilerParams(
-            collective_id=2, has_side_effects=True, vmem_limit_bytes=32 * 2**20
+            collective_id=2, has_side_effects=True, vmem_limit_bytes=63 * 2**20
         ),
         name="reduce",
     )(packed)
+
+
+def update_kernel(layout, step_rate, grad_ref, *refs):
+    weights, moments, averages, new_moments, new_weights, new_averages = (refs[5 * i : 5 * i + 5] for i in range(6))
+
+    def step(index, at, gradient):
+        moment = mu_coef * moments[index][at] + gradient
+        weight = weights[index][at] - step_rate * (gradient + mu_coef * moment)
+        new_moments[index][at] = moment
+        new_weights[index][at] = weight
+        new_averages[index][at] = (1.0 - avg_coef) * averages[index][at] + avg_coef * weight
+
+    for index, name in ((0, "msg"), (3, "kv"), (4, "out")):
+        for columns, gradient in layout.tiles(grad_ref, name):
+            step(index, (slice(None), columns), gradient)
+    for part in range(2):
+        for columns, gradient in layout.tiles(grad_ref, f"gru{part}"):
+            step(1, (slice(None), part, columns), gradient)
+    for part in range(4):
+        for columns, gradient in layout.tiles(grad_ref, f"square{part}"):
+            step(2, (slice(None), part, columns), gradient)
+
+
+def update_all(layout, step_rate, packed, params):
+    vmem = pl.BlockSpec(memory_space=pltpu.VMEM)
+    shapes = tuple(jax.ShapeDtypeStruct(p.shape, f32) for p in params)
+    return pl.pallas_call(
+        partial(update_kernel, layout, step_rate),
+        out_shape=shapes,
+        in_specs=[vmem] * (len(params) + 1),
+        out_specs=(vmem,) * len(params),
+        compiler_params=pltpu.CompilerParams(vmem_limit_bytes=63 * 2**20),
+        name="update",
+    )(packed, *params)
+
+
+def turned(arrays):
+    msg, gru, square, kv, out = arrays
+    return (msg.T, gru.transpose(1, 0, 2), square.transpose(1, 0, 2), kv, out.T)
 
 
 def local(
@@ -763,93 +945,34 @@
     batch = lax.axis_size("batch")
     events, edge = edge_feat.shape
     nodes, width = memory.shape
-    picks, per_pick = nbr_ids.shape[1:]
-    slots = picks * per_pick
     head_dim = width // HEADS
     time_width = w_key_value.shape[0] - width
-    rows = pad_to(width, 16)
     times = pad_to(time_width, 16)
-    layout = Layout(width, edge, time_width, (8 * own * batch))
-
-    mem_low = memory.astype(bf16)
-    time_parts = jnp.stack([last_update // 8, last_update % 8], 1).astype(bf16)
-    shard = jnp.pad(jnp.concatenate([mem_low, time_parts], 1), ((0, 0), (0, 256 - width - 2)))
-    shard = shard.reshape(nodes, 2, 128)
-    event_rows = jnp.stack([event_time, event_mask, src_local, target])
-    event_rows = jnp.pad(event_rows, ((0, 4), (0, 0)))
-    table, cand_ids, positives, newest = exchange(
-        own, batch, shard, dest_local[None, :], event_rows, last_update[None, :]
+    layout = Layout(
+        width, w_msg.shape[0], w_output.shape[0], w_gru.shape[2], *w_key_value.shape, 8 * own * batch
     )
-
-    flat_ids = (nbr_owner[:, :, None] * nodes + nbr_ids).reshape(events, slots).T.reshape(-1)
-    valid = nbr_mask.reshape(events, slots).T.reshape(slots, 1, events)
-    mem_t = jnp.pad(jnp.concatenate([memory, last_update.astype(f32)[:, None]], 1).T, ((0, rows - width - 1), (0, 0)))
-    part0 = mem_t.astype(bf16)
-    part1 = (mem_t - part0.astype(f32)).astype(bf16)
-    part2 = (mem_t - part0.astype(f32) - part1.astype(f32)).astype(bf16)
-    mem3 = jnp.concatenate([part0, part1, part2], 0)
-
-    def square(weight):
-        weight = weight.astype(bf16)
-        return jnp.pad(weight, ((0, rows - weight.shape[0]), (0, rows - weight.shape[1])))
-
-    g0 = [w_gru[0, :, i * width : (i + 1) * width] for i in range(3)]
-    g1 = [w_gru[1, :, i * width : (i + 1) * width] for i in range(3)]
-    sq = [w_square[i] for i in range(3)]
-    out = [w_output[:width], w_output[width:]]
-    wsq = jnp.stack(
-        [square(m.T) for m in [w_msg[:width]] + g0 + g1 + sq + out] + [square(m) for m in g0 + sq + out]
+    weights = turned((w_msg, w_gru, w_square, w_key_value, w_output))
+    time_row, mask_row, src_row, target_row = (x[None, :] for x in (event_time, event_mask, src_local, target))
+    table, cand_ids, flat_ids, positives, newest, mem3, *low_weights = exchange(
+        own, batch,
+        (memory.T, last_update[None, :], dest_local[None, :], time_row, mask_row, src_row,
+         nbr_owner.T, nbr_ids.transpose(2, 1, 0)) + weights,
     )
-    w_edge = jnp.pad(w_msg[width : width + edge].T.astype(bf16), ((0, rows - width), (0, 0)))
-    w_time = jnp.pad(w_msg[width + edge :].T.astype(bf16), ((0, rows - width), (0, times - time_width)))
-    kv_t = w_key_value.T.astype(bf16)
-    pick_last = jnp.zeros((rows - width, 256), bf16).at[0, width].set(8.0).at[0, width + 1].set(1.0)
-
-    def kv_rows(part, first):
-        mem_part = jnp.pad(part[:, :width], ((0, 0), (0, 256 - width)))
-        return jnp.concatenate([mem_part, pick_last if first else jnp.zeros_like(pick_last)], 0)
-
-    wkv1 = jnp.concatenate([kv_rows(kv_t[:width], True), kv_rows(kv_t[width:], False)], 0)
-    pad_time = lambda part: jnp.pad(part[:, width:], ((0, rows - width), (0, times - time_width)))
-    wkv2 = jnp.concatenate([pad_time(kv_t[:width]), pad_time(kv_t[width:])], 0)
-    wd = jnp.pad(w_square[3].astype(bf16), ((0, 256 - width), (0, rows - width)))
-    eye = jnp.eye(256, dtype=bf16)
-    freq = jnp.asarray(time_columns(time_width, times))
-
     packed = main(
-        layout, own * nodes <= 16384, width, head_dim, slots, times,
-        (flat_ids, cand_ids, positives, table, event_rows, valid, mem3, edge_feat,
-         wsq, w_edge, w_time, wkv1, wkv2, wd, wd.T, eye, freq),
+        layout, own * nodes <= 16384, width, head_dim, dest_local.shape[0],
+        (flat_ids.reshape(-1), cand_ids.reshape(-1), positives, table, time_row, mask_row, src_row, target_row,
+         nbr_mask.transpose(2, 1, 0), mem3, edge_feat.T, *low_weights, jnp.asarray(time_columns(time_width, times))),
     )
     summed = reduce_all(own, batch, packed)
-
-    take = partial(layout.take, summed)
-    grads = (
-        jnp.concatenate(
-            [take("msg_mem", width, width), take("msg_edge", edge, width), take("msg_time", time_width, width)], 0
-        ),
-        jnp.stack([jnp.concatenate([take(f"gru{i}{g}", width, width) for g in range(3)], 1) for i in range(2)]),
-        jnp.stack([take(f"square{i}", width, width) for i in range(4)]),
-        jnp.concatenate(
-            [
-                jnp.concatenate([take("kv_mem_k", width, width), take("kv_time_k", time_width, width)], 0),
-                jnp.concatenate([take("kv_mem_v", width, width), take("kv_time_v", time_width, width)], 0),
-            ],
-            1,
-        ),
-        jnp.concatenate([take("out_a", width, width), take("out_b", width, width)], 0),
+    step_rate = rate_coef * math.sqrt(events * own * batch)
+    states = update_all(
+        layout, step_rate, summed,
+        weights
+        + turned((mom_msg, mom_gru, mom_square, mom_key_value, mom_output))
+        + turned((avg_msg, avg_gru, avg_square, avg_key_value, avg_output)),
     )
-    step_rate = rate_coef * math.sqrt(events * own * batch)
-    params = (w_msg, w_gru, w_square, w_key_value, w_output)
-    moments = (mom_msg, mom_gru, mom_square, mom_key_value, mom_output)
-    averages = (avg_msg, avg_gru, avg_square, avg_key_value, avg_output)
-    states = [nesterov(params[i], grads[i], moments[i], averages[i], step_rate) for i in range(5)]
-    return (
-        (summed[layout.loss, 0], positives[0, 0], newest.reshape(-1))
-        + tuple(s[0] for s in states)
-        + tuple(s[1] for s in states)
-        + tuple(s[2] for s in states)
-    )
+    states = [x for i in range(3) for x in turned(states[5 * i : 5 * i + 5])]
+    return (summed[layout.loss, 0], positives[0, 0], newest.reshape(-1), *states)
 
 
 def solution(mesh):

time: 333 us -> 222 us (0.67)
  local copies, waits for them, and re-layouts: 73.9 us -> 2.98 us
  Pallas kernels: 240 us -> 218 us
  other arithmetic: 14.4 us -> 0 us
    unnamed x125 -> x3, local copies, waits for them, and re-layouts: 50.4 us -> 0.6 us
    pallas_call x2 -> x3, Pallas kernels: 189 us -> 166 us  [the longest x1 118 us: main(): pl.pallas_call(partial(main_kernel, (width, head_dim, keep_kv, cand_width...]
    add x6 -> x0, other arithmetic: 10.2 us -> none  [the longest x5 10.2 us: nesterov(): (1.0 - avg_coef) * average + avg_coef * new_weight]
    another operation x22 -> x0, local copies, waits for them, and re-layouts: 5.26 us -> none
    concatenate x2 -> x0, local copies, waits for them, and re-layouts: 4.08 us -> none  [local(): jnp.concatenate([take(f'gru{i}{g}', width, width) for g in range(3)], 1)]
where the time goes in v2:
time: 222 us; the launch traced here: 221 us
  Pallas kernels  218 us (98%)
  local copies, waits for them, and re-layouts  2.98 us (1%)
    pallas_call x1, Pallas kernels, main(): pl.pallas_call(partial(main_kernel, (width, head_dim, keep_kv, cand_width...  118 us
    pallas_call x1, Pallas kernels, reduce_all(): pl.pallas_call(partial(reduce_kernel, own, batch, streams), out_shape=jax...  52 us
    pallas_call x1, Pallas kernels, exchange(): pl.pallas_call(partial(exchange_kernel, own, batch), out_shape=(low(own *...  32 us
    pallas_call x1, Pallas kernels, update_all(): pl.pallas_call(partial(update_kernel, layout, step_rate), out_shape=shape...  15.8 us

profile of v2, /device:TPU:0, one launch (start us, length us, event | category | flops | bytes accessed | tf_op | source)
XLA Modules:
  0.0 221.3 jit_solution(4445883782591606610)
XLA Ops:
  0.7 32.0 %exchange.1 = (bf16[8192,2,128]{2,1,0:T(2,128)(2,1)}, s32[32,128]{1,0:T(8,128)}, s32[160,128]{1,0:T(8,128)}, f32[8,128]{1,0:T(8,128)}, s32[1,1024]{1,0:T(1,128)}...) custom-call(f32[172,1024]{1,0:T(8,128)} %bitcast.50, ...), custom_call_target="tpu_custom_call" | custom-call | tf_op jit(solution)/shard_map/exchange/pallas_call | solution.py:333
  32.7 1.2 slice.7
  33.8 117.8 %train.1.grad_ref = f32[4608,128]{1,0:T(8,128)} custom-call(s32[20480]{0:T(1024)} %bitcast.59, s32[4096]{0:T(1024)} %bitcast.62, f32[8,128]{1,0:T(8,128)} %get-tuple-element.48.pos_ref, bf16[8192,2,128]{2,1,0:T(2,128)(2,1)} %get-tuple-element.49.table_ref, s32[1,1024]{1,0:T(1,128)} %bitcast.64, s32[1,1024]{1,0:T(1,128)} %bitcast.66, s32[1,1024]{1,0:T(1,128)} %bitcast.68, ...), custom_call_target="tpu_custom_call" | custom-call | tf_op jit(solution)/shard_map/train/pallas_call | solution.py:770
  151.7 52.0 %reduce.1.grad_ref = f32[4608,128]{1,0:T(8,128)} custom-call(f32[4608,128]{1,0:T(8,128)} %train.1.grad_ref), custom_call_target="tpu_custom_call" | custom-call | tf_op jit(solution)/shard_map/reduce/pallas_call | solution.py:881
  203.7 1.2 slice.6
  204.9 0.0 copy-start
  204.9 15.8 %update.1 = (f32[172,444]{1,0:T(8,128)}, f32[172,2,516]{2,1,0:T(2,128)}, f32[172,4,172]{2,1,0:T(4,128)}, f32[272,344]{1,0:T(8,128)}, f32[172,344]{1,0:T(8,128)},...) custom-call(f32[4608,128]{1,0:T(8,128)} %reduce.1.grad_ref, ...), custom_call_target="tpu_custom_call" | custom-call | tf_op jit(solution)/shard_map/update/pallas_call | solution.py:923
  220.7 0.0 copy-done
  220.8 0.6 copy.46
Async XLA Ops:
  204.9 15.8 %copy-start = (s32[1,1024]{1,0:T(1,128)S(1)}, s32[1,1024]{1,0:T(1,128)}, u32[]{:S(2)}) copy-start(s32[1,1024]{1,0:T(1,128)} %get-tuple-element.58) | copy-start | bytes 12292

commit v3 on v2

--- a/solution.py
+++ b/solution.py
@@ -97,7 +97,9 @@
 
 
 SQUARES = (
-    "g0r g0z g0n g1r g1z g1n s0t s1t s2t g0r_back g0z_back g0n_back s0 s1 s2 oa ob".split()
+    "g0r", "g0z", "g0n", "g1r", "g1z", "g1n",
+    "s0t", "s1t", "s2t", "g0r_back", "g0z_back", "g0n_back",
+    "s0", "s1", "s2", "oa", "ob",
 )
 
 
@@ -433,7 +435,7 @@
     ids_ref, cand_ref, pos_ref, table_ref, time_ref, mask_ref, src_ref, target_ref, valid_ref, mem3_ref, edge_ref,
     wsq_ref, wmsg_ref, wout_ref, wkv1_ref, wkv2_ref, wd_ref, wdt_ref, freq_ref,
     grad_ref,
-    xs, x_all, t_all, kv_all, score, dest_rows, slab, eye_ref, stage,
+    xs, xs2, x_all, t_all, kv_all, score, dest_rows, slab, eye_ref, gslab, stage,
     x_msg, mem_low, hidden, fresh_low, att_low, x_out, hid_out, emb, emb_rows,
     mem_src, pre_msg, reset_gate, update, cand_act, gate_n, queries, attended, pre_out,
     acc_a, grad_att, gkv_m, gkv_t, rows_ref,
@@ -456,23 +458,15 @@
     def w(name):
         return wsq_ref[SQUARES.index(name)]
 
-    def gather(read_id, count):
-        unroll = 128
-
-        def body(i, unused):
-            base = i * unroll
-            first = read_id(i)
-            got = [table_ref[first(k)] for k in range(unroll)]
-            for k in range(unroll):
-                xs[pl.ds(pl.multiple_of(2 * base, 2 * unroll) + 2 * k, 2), :] = got[k].astype(f32)
-            return unused
-
-        lax.fori_loop(0, count // unroll, body, 0)
-
-    def gathered(start, count):
+    def gather(buf, read_id, at):
+        got = [table_ref[read_id(k)] for k in range(128)]
+        for k in range(128):
+            buf[pl.ds(pl.multiple_of(2 * at, 256) + 2 * k, 2), :] = got[k].astype(f32)
+
+    def gathered(buf, start, count):
         base = pl.multiple_of(2 * start, 2 * count)
         return jnp.concatenate(
-            [xs[pl.ds(base, count, stride=2), :], xs[pl.ds(base + 1, count, stride=2), :]], 1
+            [buf[pl.ds(base, count, stride=2), :], buf[pl.ds(base + 1, count, stride=2), :]], 1
         ).astype(bf16)
 
     grad_ref[layout.loss :, :] = jnp.zeros_like(grad_ref[layout.loss :, :])
@@ -483,9 +477,13 @@
     stage[...] = jnp.zeros_like(stage)
 
     def cand_body(o, unused):
-        gather(lambda i: lambda k: cand_ref[o * cand_width + i * 128 + k], cand_width)
+        def fill(i, unused):
+            gather(xs, lambda k: cand_ref[o * cand_width + i * 128 + k], i * 128)
+            return unused
+
+        lax.fori_loop(0, cand_width // 128, fill, 0)
         at = pl.multiple_of(o * cand_width, cand_width)
-        dest_rows[pl.ds(at, cand_width), :] = gathered(0, cand_width)
+        dest_rows[pl.ds(at, cand_width), :] = gathered(xs, 0, cand_width)
         return unused
 
     lax.fori_loop(0, owners, cand_body, 0)
@@ -527,37 +525,43 @@
 
     lax.fori_loop(0, chunks, gru_body, 0)
 
-    def slot_body(j, unused):
-        pick = lax.rem(j, picks)
-        round_ = lax.div(j, picks)
-
-        def first(i):
-            base = ((round_ * (events // 128) + i) * picks + pick) * 128
-            return lambda k: ids_ref[base + k]
-
-        gather(first, events)
-
-        def chunk_body(c, unused):
-            cs = lanes(c)
-            x = gathered(c * LANES, LANES)
-            x_all[j, cs, :] = x
-            kv = nt(wkv1_ref[...], x)
-            delta = time_ref[:, cs].astype(f32) - kv[width : width + 1]
-            t_low = cos_rows(delta, high, low).astype(bf16)
-            t_all[j, :, cs] = t_low
-            kv = (kv + nn(wkv2_ref[...], t_low)).astype(bf16)
-            if keep_kv:
-                kv_all[j, :, cs] = kv
-            s0, s1 = heads.sums(kv[:rows].astype(f32) * queries[:, cs].astype(f32))
-            live = valid_ref[round_, pl.ds(pick, 1), cs] > 0
-            score[j, 0:1, cs] = jnp.where(live, s0 * scale, mask_fill)
-            score[j, 1:2, cs] = jnp.where(live, s1 * scale, mask_fill)
-            return unused
-
-        lax.fori_loop(0, chunks, chunk_body, 0, unroll=True)
-        return unused
-
-    lax.fori_loop(0, slots, slot_body, 0)
+    def fetch(buf, j, i):
+        base = ((lax.div(j, picks) * (events // 128) + i) * picks + lax.rem(j, picks)) * 128
+        gather(buf, lambda k: ids_ref[base + k], i * 128)
+
+    def slot_chunk(buf, j, c):
+        cs = lanes(c)
+        x = gathered(buf, c * LANES, LANES)
+        x_all[j, cs, :] = x
+        kv = nt(wkv1_ref[...], x)
+        delta = time_ref[:, cs].astype(f32) - kv[width : width + 1]
+        t_low = cos_rows(delta, high, low).astype(bf16)
+        t_all[j, :, cs] = t_low
+        kv = (kv + nn(wkv2_ref[...], t_low)).astype(bf16)
+        if keep_kv:
+            kv_all[j, :, cs] = kv
+        s0, s1 = heads.sums(kv[:rows].astype(f32) * queries[:, cs].astype(f32))
+        live = valid_ref[lax.div(j, picks), pl.ds(lax.rem(j, picks), 1), cs] > 0
+        score[j, 0:1, cs] = jnp.where(live, s0 * scale, mask_fill)
+        score[j, 1:2, cs] = jnp.where(live, s1 * scale, mask_fill)
+
+    def first_slot(i, unused):
+        fetch(xs, 0, i)
+        return unused
+
+    lax.fori_loop(0, events // 128, first_slot, 0)
+
+    def slot_pair(i, unused):
+        for side, (now, later) in enumerate(((xs, xs2), (xs2, xs))):
+            j = 2 * i + side
+            ahead = jnp.minimum(j + 1, slots - 1)
+            for c in range(chunks):
+                for block in range(LANES // 128):
+                    fetch(later, ahead, c * (LANES // 128) + block)
+                slot_chunk(now, j, c)
+        return unused
+
+    lax.fori_loop(0, slots // 2, slot_pair, 0)
 
     def soft_body(c, unused):
         cs = lanes(c, 128)
@@ -576,14 +580,12 @@
 
     def att_body(c, unused):
         cs = lanes(c, 128)
-
-        def add(j, total):
+        total = jnp.zeros((rows, 128), f32)
+        for j in range(slots):
             v = kv_of(j, cs, slice(rows, 2 * rows)).astype(f32)
-            return total + heads.scale(v, score[j, 0:1, cs], score[j, 1:2, cs])
-
-        att = lax.fori_loop(0, slots, add, jnp.zeros((rows, 128), f32))
-        attended[:, cs] = att
-        att_low[:, cs] = att.astype(bf16)
+            total = total + heads.scale(v, score[j, 0:1, cs], score[j, 1:2, cs])
+        attended[:, cs] = total
+        att_low[:, cs] = total.astype(bf16)
         return unused
 
     lax.fori_loop(0, events // 128, att_body, 0)
@@ -603,7 +605,7 @@
         emb_rows[cs, :] = nt(eye_ref[...], e).astype(bf16)
         return unused
 
-    lax.fori_loop(0, chunks, out_body, 0)
+    lax.fori_loop(0, chunks, out_body, 0, unroll=2)
 
     def row_init(c, unused):
         cs = lanes(c)
@@ -618,26 +620,24 @@
         at = pl.multiple_of(o * cand_width, cand_width)
         return dest_rows[pl.ds(at, cand_width), :]
 
-    def lse_block(o, unused):
-        dest = nn(dest_of(o), wd_ref[...]).astype(bf16)
-
-        def chunk(c, unused):
-            cs = lanes(c)
-            logits = nn(dest, emb[:, cs])
-            old = rows_ref[0:1, cs]
-            top = jnp.maximum(old, jnp.max(logits, 0, keepdims=True))
-            rows_ref[0:1, cs] = top
-            rows_ref[1:2, cs] = rows_ref[1:2, cs] * jnp.exp(old - top) + jnp.sum(
-                jnp.exp(logits - top), 0, keepdims=True
-            )
-            hit = lax.broadcasted_iota(jnp.int32, logits.shape, 0) == target_ref[:, cs] - o * cand_width
-            rows_ref[2:3, cs] = rows_ref[2:3, cs] + jnp.sum(jnp.where(hit, logits, 0.0), 0, keepdims=True)
-            return unused
-
-        lax.fori_loop(0, chunks, chunk, 0, unroll=True)
-        return unused
-
-    lax.fori_loop(0, owners, lse_block, 0)
+    def lse_block(i, unused):
+        for side in range(2):
+            o = 2 * i + side
+            dest = nn(dest_of(o), wd_ref[...]).astype(bf16)
+            for c in range(chunks):
+                cs = lanes(c)
+                logits = nn(dest, emb[:, cs])
+                old = rows_ref[0:1, cs]
+                top = jnp.maximum(old, jnp.max(logits, 0, keepdims=True))
+                rows_ref[0:1, cs] = top
+                rows_ref[1:2, cs] = rows_ref[1:2, cs] * jnp.exp(old - top) + jnp.sum(
+                    jnp.exp(logits - top), 0, keepdims=True
+                )
+                hit = lax.broadcasted_iota(jnp.int32, logits.shape, 0) == target_ref[:, cs] - o * cand_width
+                rows_ref[2:3, cs] = rows_ref[2:3, cs] + jnp.sum(jnp.where(hit, logits, 0.0), 0, keepdims=True)
+        return unused
+
+    lax.fori_loop(0, owners // 2, lse_block, 0)
 
     mask_row = mask_ref[...].astype(f32)
     log_sum = rows_ref[0:1, :] + jnp.log(rows_ref[1:2, :])
@@ -660,10 +660,10 @@
             grad = jnp.exp(logits - rows_ref[3:4, cs]) - jnp.where(hit, 1.0, 0.0)
             grad = (grad * coeff).astype(bf16)
             slab[0:cand_width, cs] = grad
-            acc_a[:, cs] += nn(dest_t, grad)
             return unused
 
         lax.fori_loop(0, chunks, chunk, 0, unroll=True)
+        acc_a[...] += nn(dest_t, slab[0:cand_width, :])
         grad_dest = nn(slab[0:cand_width, :], emb_rows[...]).astype(bf16)
         return grad_dest_w + nn(block_t, grad_dest)[:rows]
 
@@ -690,7 +690,7 @@
         rows_ref[6:7, cs] = d1
         return unused
 
-    lax.fori_loop(0, chunks, out_back, 0)
+    lax.fori_loop(0, chunks, out_back, 0, unroll=2)
     layout.put(grad_ref, "square2", nt(hid_out[...], slab[r0, :]))
     layout.put(grad_ref, "out", nt(slab[r1, :], x_out[...]))
     layout.put(grad_ref, "square1", nt(att_low[...], slab[r2, :]))
@@ -699,27 +699,26 @@
     gkv_m[...] = jnp.zeros_like(gkv_m)
     gkv_t[...] = jnp.zeros_like(gkv_t)
 
-    def slot_back(j, unused):
-        def chunk(c, unused):
-            cs = lanes(c, 128)
-            kv = kv_of(j, cs, slice(0, 2 * rows)).astype(f32)
-            ga = grad_att[:, cs].astype(f32)
-            p0, p1 = score[j, 0:1, cs], score[j, 1:2, cs]
-            g0, g1 = heads.sums(ga * kv[rows:])
-            g0 = p0 * (g0 - rows_ref[5:6, cs]) * scale
-            g1 = p1 * (g1 - rows_ref[6:7, cs]) * scale
-            attended[:, cs] += heads.scale(kv[:rows], g0, g1)
-            slab[r0, cs] = heads.scale(queries[:, cs].astype(f32), g0, g1).astype(bf16)
-            slab[r1, cs] = heads.scale(ga, p0, p1).astype(bf16)
-            return unused
-
-        lax.fori_loop(0, events // 128, chunk, 0)
-        both = slab[0 : 2 * rows, :]
-        gkv_m[...] += nn(both, x_all[j])
-        gkv_t[...] += nt(both, t_all[j])
-        return unused
-
-    lax.fori_loop(0, slots, slot_back, 0)
+    def slot_back(i, unused):
+        for side in range(2):
+            j = 2 * i + side
+            for c in range(events // 256):
+                cs = lanes(c, 256)
+                kv = kv_of(j, cs, slice(0, 2 * rows)).astype(f32)
+                ga = grad_att[:, cs].astype(f32)
+                p0, p1 = score[j, 0:1, cs], score[j, 1:2, cs]
+                g0, g1 = heads.sums(ga * kv[rows:])
+                g0 = p0 * (g0 - rows_ref[5:6, cs]) * scale
+                g1 = p1 * (g1 - rows_ref[6:7, cs]) * scale
+                attended[:, cs] += heads.scale(kv[:rows], g0, g1)
+                gslab[side, 0:rows, cs] = heads.scale(queries[:, cs].astype(f32), g0, g1).astype(bf16)
+                gslab[side, rows:2*rows, cs] = heads.scale(ga, p0, p1).astype(bf16)
+            both = gslab[side, 0 : 2 * rows, :]
+            gkv_m[...] += nn(both, x_all[j])
+            gkv_t[...] += nt(both, t_all[j])
+        return unused
+
+    lax.fori_loop(0, slots // 2, slot_back, 0)
     gm = gkv_m[...].T
     gt = gkv_t[...].T
     both = [jnp.concatenate([g[:depth, :width], g[:depth, rows : rows + width]], 1)
@@ -747,7 +746,7 @@
         att_low[:, cs] = (back * (sig * (1.0 + pre * (1.0 - sig)))).astype(bf16)
         return unused
 
-    lax.fori_loop(0, chunks, gru_back, 0)
+    lax.fori_loop(0, chunks, gru_back, 0, unroll=2)
     layout.put(grad_ref, "square0", nt(fresh_low[...], slab[r0, :]))
     for index, (left, last) in enumerate(((hidden, x_out[0:rows, :]), (mem_low, hid_out[...]))):
         left = left[...]
@@ -774,6 +773,7 @@
         out_specs=vmem,
         scratch_shapes=[
             full(2 * events, 128),
+            full(2 * events, 128),
             low(slots, events, 256),
             low(slots, times, events),
             low(slots if keep_kv else 1, 2 * rows if keep_kv else 16, events),
@@ -781,6 +781,7 @@
             low(cands, 256),
             low(max(3 * rows, cand_width), events),
             low(256, 256),
+            low(2, cand_width, events),
             full(wide, LANES),
             low(wide, events),
         ]
@@ -799,66 +800,95 @@
 
 def reduce_kernel(own, batch, streams, grad_ref, out_ref, acc, recv, send_sem, recv_sem):
     place = {"own": lax.axis_index("own"), "batch": lax.axis_index("batch")}
-
-    def peer(axis, bit):
-        moved = dict(place)
-        moved[axis] = flip_bit(place[axis], bit)
-        return (moved["batch"], moved["own"])
+    rounds = len(streams[0][2])
+
+    def peers(axis, bit):
+        if axis == "own":
+            return [(place["batch"], flip_bit(place["own"], bit))]
+        return [(lax.rem(place["batch"] + d, batch), place["own"]) for d in range(1, batch)]
 
     barrier = pltpu.get_barrier_semaphore()
-    steps = streams[0][2]
-    for axis, bit in steps:
-        pl.semaphore_signal(barrier, inc=1, device_id=peer(axis, bit), device_id_type=MESH)
-    pl.semaphore_wait(barrier, len(steps))
-
-    base = [start for start, size, order in streams]
-    sizes = [size for start, size, order in streams]
-    inner = [start for start, size, order in streams]
+    signals = 0
+    for axis, bit in streams[0][2]:
+        for peer in peers(axis, bit):
+            pl.semaphore_signal(barrier, inc=1, device_id=peer, device_id_type=MESH)
+            signals += 1
+    pl.semaphore_wait(barrier, signals)
+
     sent = []
-    for step in range(len(steps)):
-        source = grad_ref if step == 0 else acc
-        copies = []
-        for s, (start, size, order) in enumerate(streams):
-            axis, bit = order[step]
-            half = sizes[s] // 2
-            mine = lax.div(place[axis], 1 << bit) % 2
-            away = pl.multiple_of(base[s] + (1 - mine) * half, 8)
+
+    class Stream:
+        def __init__(self, index, start, size, order):
+            self.index, self.base, self.size, self.inner, self.order = index, start, size, start, order
+            self.copies = []
+
+        def copy(self, source, target, peer, slot):
             copy = pltpu.make_async_remote_copy(
-                src_ref=source.at[pl.ds(away, half), :],
-                dst_ref=recv.at[pl.ds(inner[s], half), :],
-                send_sem=send_sem.at[s, step], recv_sem=recv_sem.at[s, step],
-                device_id=peer(axis, bit), device_id_type=MESH,
+                src_ref=source, dst_ref=target,
+                send_sem=send_sem.at[self.index, slot], recv_sem=recv_sem.at[self.index, slot],
+                device_id=peer, device_id_type=MESH,
             )
             copy.start()
-            copies.append(copy)
-            base[s] = pl.multiple_of(base[s] + mine * half, 8)
-            sizes[s] = half
-        last = step == len(steps) - 1
-        target = out_ref if last else acc
-        for s, copy in enumerate(copies):
-            copy.wait_recv()
-            part = pl.ds(base[s], sizes[s])
-            target[part, :] = source[part, :] + recv[pl.ds(inner[s], sizes[s]), :]
-            inner[s] += sizes[s]
-        sent += copies
-    for step in reversed(range(len(steps))):
-        copies = []
-        for s, (start, size, order) in enumerate(streams):
-            axis, bit = order[step]
-            part = pl.ds(base[s], sizes[s])
-            copy = pltpu.make_async_remote_copy(
-                src_ref=out_ref.at[part, :], dst_ref=out_ref.at[part, :],
-                send_sem=send_sem.at[s, step + len(steps)], recv_sem=recv_sem.at[s, step + len(steps)],
-                device_id=peer(axis, bit), device_id_type=MESH,
-            )
-            copy.start()
-            copies.append(copy)
-            mine = lax.div(place[axis], 1 << bit) % 2
-            base[s] = pl.multiple_of(base[s] - mine * sizes[s], 8)
-            sizes[s] *= 2
-        for copy in copies:
-            copy.wait_recv()
-        sent += copies
+            self.copies.append(copy)
+            sent.append(copy)
+
+        def parts(self, axis, bit):
+            if axis == "own":
+                return 2, lax.div(place["own"], 1 << bit) % 2
+            return batch, place["batch"]
+
+        def scatter(self, step):
+            axis, bit = self.order[step]
+            count, mine = self.parts(axis, bit)
+            piece = self.size // count
+            source = grad_ref if step == 0 else acc
+            for d, peer in enumerate(peers(axis, bit), 1):
+                theirs = 1 - mine if axis == "own" else peer[0]
+                away = pl.multiple_of(self.base + theirs * piece, 8)
+                self.copy(
+                    source.at[pl.ds(away, piece), :], recv.at[pl.ds(self.inner + (d - 1) * piece, piece), :],
+                    peer, step * (batch - 1) + d - 1,
+                )
+            self.base = pl.multiple_of(self.base + mine * piece, 8)
+            self.size = piece
+
+        def add(self, step):
+            source = grad_ref if step == 0 else acc
+            target = out_ref if step == rounds - 1 else acc
+            part = pl.ds(self.base, self.size)
+            total = source[part, :]
+            for copy in self.copies:
+                copy.wait_recv()
+                total = total + recv[pl.ds(self.inner, self.size), :]
+                self.inner += self.size
+            target[part, :] = total
+            self.copies = []
+
+        def gather(self, step):
+            axis, bit = self.order[step]
+            count, mine = self.parts(axis, bit)
+            part = pl.ds(self.base, self.size)
+            for d, peer in enumerate(peers(axis, bit), 1):
+                self.copy(out_ref.at[part, :], out_ref.at[part, :], peer, (rounds + step) * (batch - 1) + d - 1)
+            self.base = pl.multiple_of(self.base - mine * self.size, 8)
+            self.size *= count
+
+        def gathered(self):
+            for copy in self.copies:
+                copy.wait_recv()
+            self.copies = []
+
+    flows = [Stream(index, *stream) for index, stream in enumerate(streams)]
+    for step in range(2 * rounds + 1):
+        for flow in flows:
+            if 0 < step <= rounds:
+                flow.add(step - 1)
+            elif step > rounds:
+                flow.gathered()
+            if step < rounds:
+                flow.scatter(step)
+            elif step < 2 * rounds:
+                flow.gather(2 * rounds - 1 - step)
     for copy in sent:
         copy.wait_send()
 
@@ -866,18 +896,22 @@
 def reduce_all(own, batch, packed):
     total = packed.shape[0]
     own_bits = own.bit_length() - 1
-    batch_bits = batch.bit_length() - 1
-    fold = 8 << (own_bits + batch_bits)
+    fold = 8 * own * batch
     rest = [("own", b) for b in range(1, own_bits)]
     cut = len(rest) // 2
-    tail = [("batch", b) for b in range(batch_bits)]
+    axes = [rest[:cut], rest[cut:], [("batch", 0)]]
     blocks = total // fold
-    first = (blocks + 1) // 2 * fold
-    streams = (
-        (0, first, [("own", 0)] + rest + tail),
-        (first, total - first, [("own", 0)] + rest[cut:] + rest[:cut] + tail),
-    )
-    count = 2 * (own_bits + batch_bits)
+    halves = 1
+    streams = []
+    start = 0
+    for index in range(3 * halves):
+        size = (blocks + 3 * halves - 1 - index) // (3 * halves) * fold
+        turn = index % 3
+        order = [("own", 0)] + [bit for part in axes[turn:] + axes[:turn] for bit in part]
+        if size:
+            streams.append((start, size, order))
+            start += size
+    count = 2 * len(streams[0][2]) * (batch - 1)
     return pl.pallas_call(
         partial(reduce_kernel, own, batch, streams),
         out_shape=jax.ShapeDtypeStruct(packed.shape, f32),
@@ -886,8 +920,8 @@
         scratch_shapes=[
             pltpu.VMEM(packed.shape, f32),
             pltpu.VMEM(packed.shape, f32),
-            pltpu.SemaphoreType.DMA((2, count)),
-            pltpu.SemaphoreType.DMA((2, count)),
+            pltpu.SemaphoreType.DMA((len(streams), count)),
+            pltpu.SemaphoreType.DMA((len(streams), count)),
         ],
         compiler_params=pltpu.CompilerParams(
             collective_id=2, has_side_effects=True, vmem_limit_bytes=63 * 2**20
@@ -897,34 +931,52 @@
 
 
 def update_kernel(layout, step_rate, grad_ref, *refs):
-    weights, moments, averages, new_moments, new_weights, new_averages = (refs[5 * i : 5 * i + 5] for i in range(6))
+    sources, targets, held, laid = refs[:15], refs[15:30], refs[30:45], refs[45:47]
+    in_sem, out_sem = refs[47:]
+    arrive = [pltpu.make_async_copy(sources[i], held[i], in_sem.at[i]) for i in range(15)]
+    leave = [pltpu.make_async_copy(held[i], targets[(i + 5) % 10 if i < 10 else i], out_sem.at[i]) for i in range(15)]
+    order = (1, 2, 0, 3, 4)
+    for index in order:
+        for kind in range(3):
+            arrive[5 * kind + index].start()
+
+    for ref, name, parts in ((laid[0], "gru", 2), (laid[1], "square", 4)):
+        for part in range(parts):
+            for columns, gradient in layout.tiles(grad_ref, f"{name}{part}"):
+                ref[:, part, columns] = gradient
 
     def step(index, at, gradient):
-        moment = mu_coef * moments[index][at] + gradient
-        weight = weights[index][at] - step_rate * (gradient + mu_coef * moment)
-        new_moments[index][at] = moment
-        new_weights[index][at] = weight
-        new_averages[index][at] = (1.0 - avg_coef) * averages[index][at] + avg_coef * weight
-
-    for index, name in ((0, "msg"), (3, "kv"), (4, "out")):
-        for columns, gradient in layout.tiles(grad_ref, name):
-            step(index, (slice(None), columns), gradient)
-    for part in range(2):
-        for columns, gradient in layout.tiles(grad_ref, f"gru{part}"):
-            step(1, (slice(None), part, columns), gradient)
-    for part in range(4):
-        for columns, gradient in layout.tiles(grad_ref, f"square{part}"):
-            step(2, (slice(None), part, columns), gradient)
+        weights, moments, averages = (held[5 * kind + index] for kind in range(3))
+        moment = mu_coef * moments[at] + gradient
+        weight = weights[at] - step_rate * (gradient + mu_coef * moment)
+        moments[at] = moment
+        weights[at] = weight
+        averages[at] = (1.0 - avg_coef) * averages[at] + avg_coef * weight
+
+    for index in order:
+        for kind in range(3):
+            arrive[5 * kind + index].wait()
+        if index in (1, 2):
+            step(index, slice(None), laid[index - 1][...])
+        else:
+            for columns, gradient in layout.tiles(grad_ref, ("msg", "", "", "kv", "out")[index]):
+                step(index, (slice(None), columns), gradient)
+        for kind in range(3):
+            leave[5 * kind + index].start()
+    for copy in leave:
+        copy.wait()
 
 
 def update_all(layout, step_rate, packed, params):
     vmem = pl.BlockSpec(memory_space=pltpu.VMEM)
-    shapes = tuple(jax.ShapeDtypeStruct(p.shape, f32) for p in params)
+    hbm = pl.BlockSpec(memory_space=pl.ANY)
+    buffers = [pltpu.VMEM(p.shape, f32) for p in params]
     return pl.pallas_call(
         partial(update_kernel, layout, step_rate),
-        out_shape=shapes,
-        in_specs=[vmem] * (len(params) + 1),
-        out_specs=(vmem,) * len(params),
+        out_shape=tuple(jax.ShapeDtypeStruct(p.shape, f32) for p in params[5:10] + params[:5] + params[10:]),
+        in_specs=[vmem] + [hbm] * 15,
+        out_specs=(hbm,) * 15,
+        scratch_shapes=buffers + buffers[1:3] + [pltpu.SemaphoreType.DMA((15,))] * 2,
         compiler_params=pltpu.CompilerParams(vmem_limit_bytes=63 * 2**20),
         name="update",
     )(packed, *params)

time: 222 us -> 175 us (0.79)
  Pallas kernels: 218 us -> 171 us
    pallas_call x1, Pallas kernels: 118 us -> 87.9 us  [main(): pl.pallas_call(partial(main_kernel, (width, head_dim, keep_kv, cand_width...]
    pallas_call x1, Pallas kernels: 15.8 us -> 7.21 us  [update_all(): pl.pallas_call(partial(update_kernel, layout, step_rate), out_shape=tuple...]
    pallas_call x1, Pallas kernels: 52 us -> 44 us  [reduce_all(): pl.pallas_call(partial(reduce_kernel, own, batch, streams), out_shape=jax...]
where the time goes in v3:
time: 175 us
  Pallas kernels  171 us (98%)
  local copies, waits for them, and re-layouts  2.98 us (2%)
    pallas_call x1, Pallas kernels, main(): pl.pallas_call(partial(main_kernel, (width, head_dim, keep_kv, cand_width...  87.9 us
    pallas_call x1, Pallas kernels, reduce_all(): pl.pallas_call(partial(reduce_kernel, own, batch, streams), out_shape=jax...  44 us
    pallas_call x1, Pallas kernels, exchange(): pl.pallas_call(partial(exchange_kernel, own, batch), out_shape=(low(own *...  32 us
    pallas_call x1, Pallas kernels, update_all(): pl.pallas_call(partial(update_kernel, layout, step_rate), out_shape=tuple...  7.21 us

profile of v3, /device:TPU:0, one launch (start us, length us, event | category | flops | bytes accessed | tf_op | source)
XLA Modules:
  0.0 174.7 jit_solution(11686239168274661075)
XLA Ops:
  0.7 32.0 %exchange.1 = (bf16[8192,2,128]{2,1,0:T(2,128)(2,1)}, s32[32,128]{1,0:T(8,128)}, s32[160,128]{1,0:T(8,128)}, f32[8,128]{1,0:T(8,128)}, s32[1,1024]{1,0:T(1,128)}...) custom-call(f32[172,1024]{1,0:T(8,128)} %bitcast.50, ...), custom_call_target="tpu_custom_call" | custom-call | tf_op jit(solution)/shard_map/exchange/pallas_call | solution.py:335
  32.7 1.2 slice.7
  33.8 87.9 %train.1.grad_ref = f32[4608,128]{1,0:T(8,128)} custom-call(s32[20480]{0:T(1024)} %bitcast.59, s32[4096]{0:T(1024)} %bitcast.62, f32[8,128]{1,0:T(8,128)} %get-tuple-element.48.pos_ref, bf16[8192,2,128]{2,1,0:T(2,128)(2,1)} %get-tuple-element.49.table_ref, s32[1,1024]{1,0:T(1,128)} %bitcast.64, s32[1,1024]{1,0:T(1,128)} %bitcast.66, s32[1,1024]{1,0:T(1,128)} %bitcast.68, ...), custom_call_target="tpu_custom_call" | custom-call | tf_op jit(solution)/shard_map/train/pallas_call | solution.py:769
  121.7 44.0 %reduce.1.grad_ref = f32[4608,128]{1,0:T(8,128)} custom-call(f32[4608,128]{1,0:T(8,128)} %train.1.grad_ref), custom_call_target="tpu_custom_call" | custom-call | tf_op jit(solution)/shard_map/reduce/pallas_call | solution.py:915
  165.7 1.2 slice.6
  166.9 0.0 copy-start
  166.9 7.2 %update.1 = (f32[172,444]{1,0:T(8,128)}, f32[172,2,516]{2,1,0:T(2,128)}, f32[172,4,172]{2,1,0:T(4,128)}, f32[272,344]{1,0:T(8,128)}, f32[172,344]{1,0:T(8,128)},...) custom-call(f32[4608,128]{1,0:T(8,128)} %reduce.1.grad_ref, ...), custom_call_target="tpu_custom_call" | custom-call | tf_op jit(solution)/shard_map/update/pallas_call | solution.py:974
  174.1 0.0 copy-done
  174.1 0.6 copy.46
Async XLA Ops:
  166.9 7.2 %copy-start = (s32[1,1024]{1,0:T(1,128)S(1)}, s32[1,1024]{1,0:T(1,128)}, u32[]{:S(2)}) copy-start(s32[1,1024]{1,0:T(1,128)} %get-tuple-element.58) | copy-start | bytes 12292

commit v4 on v3

--- a/solution.py
+++ b/solution.py
@@ -96,22 +96,37 @@
         )
 
 
-SQUARES = (
-    "g0r", "g0z", "g0n", "g1r", "g1z", "g1n",
-    "s0t", "s1t", "s2t", "g0r_back", "g0z_back", "g0n_back",
-    "s0", "s1", "s2", "oa", "ob",
-)
+GATES = ("g0r", "g0z", "g0n", "g1r", "g1z", "g1n", "s0t")
+SQUARES = ("s1t", "s2t", "g0r_back", "g0z_back", "g0n_back", "s0", "s1", "s2", "oa", "ob")
+LOW_STATE = ("queries", "fresh_low", "x_msg", "mem_low", "hidden")
+STATE = ("mem_src", "pre_msg", "reset_gate", "update", "cand_act", "gate_n")
 
 
 def exchange_kernel(
     own, batch,
-    mem_ref, last_ref, cand_ref, time_ref, mask_ref, src_ref, owner_ref, nbr_ref,
-    msg_ref, gru_ref, square_ref, kv_ref, outw_ref,
-    table_ref, ids_ref, flat_ref, pos_ref, newest_ref, mem3_ref,
-    wsq_ref, wmsg_ref, wout_ref, wkv1_ref, wkv2_ref, wd_ref, wdt_ref,
-    shard, ext, pairs, square_pad, wide_pad, kv_pad, batch_buf, own_buf,
-    local_sem, table_send, table_recv, batch_send, batch_recv, own_send, own_recv,
+    mem_ref, last_ref, cand_ref, time_ref, mask_ref, src_ref, owner_ref, nbr_ref, freq_ref,
+    msg_hbm, gru_hbm, square_hbm, kv_hbm, outw_hbm, edge_hbm,
+    table_ref, ids_ref, flat_ref, pos_ref, newest_ref, *rest,
 ):
+    handed = rest[: 5 + len(LOW_STATE) + len(STATE)]
+    rest = rest[len(handed) :]
+    staged = rest[: len(handed)]
+    wsq_ref, wout_ref, wkv_ref, wd_ref, wdt_ref = staged[:5]
+    state = dict(zip(LOW_STATE + STATE, staged[5:]))
+    (msg_ref, gru_ref, square_ref, kv_ref, outw_ref, edge_ref, gates_ref, wmsg_ref, mem3_ref, stage,
+     shard, ext, pairs, square_pad, wide_pad, kv_pad, batch_buf, own_buf,
+     local_sem, load_sem, hand_sem,
+     table_send, table_recv, batch_send, batch_recv, own_send, own_recv) = rest[len(handed) :]
+    loads = [
+        pltpu.make_async_copy(source, target, load_sem.at[i])
+        for i, (source, target) in enumerate((
+            (gru_hbm, gru_ref), (square_hbm, square_ref), (outw_hbm, outw_ref),
+            (msg_hbm, msg_ref), (kv_hbm, kv_ref), (edge_hbm, edge_ref),
+        ))
+    ]
+    for copy in loads:
+        copy.start()
+    hands = [pltpu.make_async_copy(staged[i], handed[i], hand_sem.at[i]) for i in range(len(handed))]
     me = lax.axis_index("own")
     group = lax.axis_index("batch")
     barrier = pltpu.get_barrier_semaphore()
@@ -148,9 +163,9 @@
 
     half = nodes // 2
     bits = own.bit_length() - 1
-    rest = list(range(1, bits))
-    cut = len(rest) // 2
-    orders = (rest + [0], rest[cut:] + rest[:cut] + [0])
+    others = list(range(1, bits))
+    cut = len(others) // 2
+    orders = (others + [0], others[cut:] + others[:cut] + [0])
 
     def shard_copy(stream, pattern, bit):
         peer = flip_bit(me, bit)
@@ -224,10 +239,15 @@
     mem3_ref[2 * rows :, :] = (whole - part1.astype(f32)).astype(bf16)
 
     square_pad[...] = jnp.zeros_like(square_pad)
+    for copy in loads:
+        copy.wait()
 
     def put(name, value):
         square_pad[0:width, 0:width] = value
-        wsq_ref[SQUARES.index(name)] = square_pad[...].astype(bf16)
+        if name in GATES:
+            gates_ref[GATES.index(name)] = square_pad[...].astype(bf16)
+        else:
+            wsq_ref[SQUARES.index(name)] = square_pad[...].astype(bf16)
 
     for index in range(2):
         for gate, letter in enumerate("rzn"):
@@ -252,43 +272,17 @@
     wd_ref[...] = kv_pad[0 : wd_ref.shape[0], 0 : wd_ref.shape[1]].astype(bf16)
     kv_pad[0:width, 0:width] = last_square.T
     wdt_ref[...] = kv_pad[0 : wdt_ref.shape[0], 0 : wdt_ref.shape[1]].astype(bf16)
-    times = wkv2_ref.shape[1]
     time_width = kv_ref.shape[0] - width
-    lane = lax.broadcasted_iota(jnp.int32, (1, 256), 1)
+    kv_pad[...] = jnp.zeros_like(kv_pad)
     for index in range(2):
         part = kv_ref[:, index * width : index * width + width]
         kv_pad[index * rows : index * rows + width, 0:width] = part[0:width].T
-    kv_pad[width : width + 1, :] = jnp.where(lane == width, 8.0, jnp.where(lane == width + 1, 1.0, 0.0))
-    wkv1_ref[...] = kv_pad[...].astype(bf16)
-    kv_pad[...] = jnp.zeros_like(kv_pad)
-    for index in range(2):
-        part = kv_ref[:, index * width : index * width + width]
-        kv_pad[index * rows : index * rows + width, 0:time_width] = part[width:].T
-    wkv2_ref[...] = kv_pad[:, 0:times].astype(bf16)
-
-    total = count
-    for step, copy in enumerate(peers, 1):
-        copy.wait_recv()
-        newest = jnp.maximum(newest, batch_buf[step, 0:1, :])
-        total = total + batch_buf[step, 1:2, 0:1]
-    newest_ref[...] = newest
-
-    cands = cand_ref.shape[1]
-    own_buf[0, 0:1, :] = cand_ref[...] + me * nodes
-    own_buf[0, 1:2, :] = jnp.broadcast_to(total, (1, cands))
-
-    def owner_copy(step):
-        return pltpu.make_async_remote_copy(
-            src_ref=own_buf.at[0], dst_ref=own_buf.at[step],
-            send_sem=own_send.at[step], recv_sem=own_recv.at[step],
-            device_id=(group, lax.rem(me + step, own)), device_id_type=MESH,
-        )
-
-    owners = [owner_copy(step) for step in range(1, own)]
-    for copy in owners:
+        kv_pad[index * rows : index * rows + width, 256 : 256 + time_width] = part[width:].T
+    wkv_ref[...] = kv_pad[...].astype(bf16)
+    for copy in hands[:5]:
         copy.start()
 
-    for step in range(bits):
+    def forward(step):
         for stream in range(2):
             order = orders[stream]
             held = [0]
@@ -302,6 +296,74 @@
                     copy.start()
                     copies[stream][slot | 1 << bit] = copy
 
+    forward(0)
+    total = count
+    for step, copy in enumerate(peers, 1):
+        copy.wait_recv()
+        newest = jnp.maximum(newest, batch_buf[step, 0:1, :])
+        total = total + batch_buf[step, 1:2, 0:1]
+    newest_ref[...] = newest
+
+    cands = cand_ref.shape[1]
+    own_buf[0, 0:1, :] = cand_ref[...] + me * nodes
+    own_buf[0, 1:2, :] = jnp.broadcast_to(total, (1, cands))
+
+    def owner_copy(step):
+        return pltpu.make_async_remote_copy(
+            src_ref=own_buf.at[0], dst_ref=own_buf.at[step],
+            send_sem=own_send.at[step], recv_sem=own_recv.at[step],
+            device_id=(group, lax.rem(me + step, own)), device_id_type=MESH,
+        )
+
+    owners = [owner_copy(step) for step in range(1, own)]
+    for copy in owners:
+        copy.start()
+
+    edge = edge_ref.shape[0]
+    high, low = freq_ref[:, 0:1], freq_ref[:, 1:2]
+    stage[...] = jnp.zeros_like(stage)
+
+    def w(name):
+        return gates_ref[GATES.index(name)]
+
+    def gru_body(c, unused):
+        cs = pl.ds(pl.multiple_of(c * LANES, LANES), LANES)
+        node = lax.broadcasted_iota(jnp.int32, (nodes, LANES), 0)
+        onehot = (node == src_ref[:, cs]).astype(f32).astype(bf16)
+        parts = nn(mem3_ref[...], onehot)
+        mem = parts[:rows] + parts[rows : 2 * rows] + parts[2 * rows :]
+        state["mem_src"][:, cs] = mem
+        delta = time_ref[:, cs].astype(f32) - 8.0 * mem[width : width + 1] - mem[width + 1 : width + 2]
+        stage[0:width, :] = mem[0:width]
+        stage[width : width + edge, :] = edge_ref[:, cs].astype(f32)
+        stage[width + edge : width + edge + time_width, :] = cos_rows(delta, high, low)[0:time_width]
+        x = stage[...].astype(bf16)
+        state["x_msg"][:, cs] = x
+        m_low = mem.astype(bf16)
+        state["mem_low"][:, cs] = m_low
+        pre = nn(wmsg_ref[...], x)
+        state["pre_msg"][:, cs] = pre
+        hid = (pre * jax.nn.sigmoid(pre)).astype(bf16)
+        state["hidden"][:, cs] = hid
+        r = jax.nn.sigmoid(nn(w("g0r"), hid) + nn(w("g1r"), m_low))
+        state["reset_gate"][:, cs] = r
+        u = jax.nn.sigmoid(nn(w("g0z"), hid) + nn(w("g1z"), m_low))
+        state["update"][:, cs] = u
+        gn = nn(w("g1n"), m_low)
+        state["gate_n"][:, cs] = gn
+        cand = jnp.tanh(nn(w("g0n"), hid) + r * gn)
+        state["cand_act"][:, cs] = cand
+        fresh = ((1.0 - u) * cand + u * mem).astype(bf16)
+        state["fresh_low"][:, cs] = fresh
+        state["queries"][:, cs] = nn(w("s0t"), fresh).astype(bf16)
+        return unused
+
+    lax.fori_loop(0, events // LANES, gru_body, 0)
+    for copy in hands[5:]:
+        copy.start()
+    for step in range(1, bits):
+        forward(step)
+
     for step in range(own):
         if step:
             owners[step - 1].wait_recv()
@@ -313,6 +375,8 @@
             ]
     pos_ref[...] = jnp.broadcast_to(jnp.maximum(total.astype(f32), 1.0), pos_ref.shape)
     mine.wait()
+    for copy in hands:
+        copy.wait()
     for copy in peers + owners:
         copy.wait_send()
     for stream in range(2):
@@ -321,46 +385,54 @@
 
 
 def exchange(own, batch, args):
-    mem, last, cand, time, mask, src, owner, nbr, msg, gru, square, kv, outw = args
+    mem, last, cand, time, mask, src, owner, nbr, freq, msg, gru, square, kv, outw, edge = args
     width, nodes = mem.shape
     events = src.shape[1]
     cands = cand.shape[1]
     rows = pad_to(width, 16)
-    times = pad_to(kv.shape[0] - width, 16)
     wide = pad_to(msg.shape[1], 16)
     vmem = pl.BlockSpec(memory_space=pltpu.VMEM)
     hbm = pl.BlockSpec(memory_space=pl.ANY)
-    low = lambda *shape: jax.ShapeDtypeStruct(shape, bf16)
     whole = lambda *shape: jax.ShapeDtypeStruct(shape, jnp.int32)
+    handed = [
+        ((len(SQUARES), rows, rows), bf16),
+        ((rows, 2 * rows), bf16),
+        ((2 * rows, 384), bf16),
+        ((256, rows), bf16),
+        ((rows, 256), bf16),
+    ]
+    handed += [((wide if name == "x_msg" else rows, events), bf16) for name in LOW_STATE]
+    handed += [((rows, events), f32) for name in STATE]
     return pl.pallas_call(
         partial(exchange_kernel, own, batch),
         out_shape=(
-            low(own * nodes, 2, 128),
+            jax.ShapeDtypeStruct((own * nodes, 2, 128), bf16),
             whole(own * cands // 128, 128),
             whole(nbr.shape[0] * nbr.shape[1] * events // 128, 128),
             jax.ShapeDtypeStruct((8, 128), f32),
             whole(1, nodes),
-            low(3 * rows, nodes),
-            low(len(SQUARES), rows, rows),
-            low(rows, wide),
-            low(rows, 2 * rows),
-            low(2 * rows, 256),
-            low(2 * rows, times),
-            low(256, rows),
-            low(rows, 256),
-        ),
-        in_specs=[vmem] * len(args),
-        out_specs=(hbm,) + (vmem,) * 12,
-        scratch_shapes=[
+        )
+        + tuple(jax.ShapeDtypeStruct(*h) for h in handed),
+        in_specs=[vmem] * 9 + [hbm] * 6,
+        out_specs=(hbm,) + (vmem,) * 4 + (hbm,) * len(handed),
+        scratch_shapes=[pltpu.VMEM(*h) for h in handed]
+        + [pltpu.VMEM(x.shape, x.dtype) for x in (msg, gru, square, kv, outw, edge)]
+        + [
+            pltpu.VMEM((len(GATES), rows, rows), bf16),
+            pltpu.VMEM((rows, wide), bf16),
+            pltpu.VMEM((3 * rows, nodes), bf16),
+            pltpu.VMEM((wide, LANES), f32),
             pltpu.VMEM((nodes, 2, 128), bf16),
             pltpu.VMEM((256, nodes), f32),
             pltpu.VMEM((2 * nodes, 128), f32),
             pltpu.VMEM((rows, rows), f32),
             pltpu.VMEM((rows, wide), f32),
-            pltpu.VMEM((2 * rows, 256), f32),
+            pltpu.VMEM((2 * rows, 384), f32),
             pltpu.VMEM((batch, 8, nodes), jnp.int32),
             pltpu.VMEM((own, 8, cands), jnp.int32),
             pltpu.SemaphoreType.DMA,
+            pltpu.SemaphoreType.DMA((6,)),
+            pltpu.SemaphoreType.DMA((len(handed),)),
             pltpu.SemaphoreType.DMA((2, own)),
             pltpu.SemaphoreType.DMA((2, own)),
             pltpu.SemaphoreType.DMA((batch,)),
@@ -432,26 +504,30 @@
 
 def main_kernel(
     dims,
-    ids_ref, cand_ref, pos_ref, table_ref, time_ref, mask_ref, src_ref, target_ref, valid_ref, mem3_ref, edge_ref,
-    wsq_ref, wmsg_ref, wout_ref, wkv1_ref, wkv2_ref, wd_ref, wdt_ref, freq_ref,
-    grad_ref,
-    xs, xs2, x_all, t_all, kv_all, score, dest_rows, slab, eye_ref, gslab, stage,
-    x_msg, mem_low, hidden, fresh_low, att_low, x_out, hid_out, emb, emb_rows,
-    mem_src, pre_msg, reset_gate, update, cand_act, gate_n, queries, attended, pre_out,
-    acc_a, grad_att, gkv_m, gkv_t, rows_ref,
+    ids_ref, cand_ref, pos_ref, table_ref, time_ref, mask_ref, target_ref, valid_ref,
+    wsq_ref, wout_ref, wkv_ref, wd_ref, wdt_ref, freq_row_ref, queries, fresh_low, *rest,
 ):
+    late = rest[: len(LOW_STATE) + len(STATE) - 2]
+    grad_ref, load_sem = rest[len(late)], rest[-1]
+    held = rest[len(late) + 1 : 2 * len(late) + 1]
+    x_msg, mem_low, hidden, mem_src, pre_msg, reset_gate, update, cand_act, gate_n = held
+    (
+        xs, xs2, x_all, time_all, kv_all, score, dest_rows, slab, eye_ref, gslab, stage,
+        att_low, x_out, hid_out, emb, emb_rows, attended, pre_out,
+        acc_a, grad_att, gkv_m, pick_last, rows_ref,
+    ) = rest[2 * len(late) + 1 : -1]
+    loads = [pltpu.make_async_copy(late[i], held[i], load_sem.at[i]) for i in range(len(late))]
+    for copy in loads:
+        copy.start()
     width, head_dim, keep_kv, cand_width, layout = dims
     events = time_ref.shape[1]
     per_pick, picks = valid_ref.shape[:2]
     slots = per_pick * picks
     rows = pad_to(width, 16)
-    times = wkv2_ref.shape[1]
-    wide = wmsg_ref.shape[1]
     time_width = layout.pieces["kv"][0] - width
-    edge = edge_ref.shape[0]
     heads = Heads(head_dim, rows)
     scale = head_dim ** (-0.5)
-    high, low = freq_ref[:, 0:1], freq_ref[:, 1:2]
+    high_row, low_row = freq_row_ref[0:1, :], freq_row_ref[1:2, :]
     chunks = events // LANES
     owners = cand_ref.shape[0] // cand_width
 
@@ -475,6 +551,12 @@
     eye = lax.broadcasted_iota(jnp.int32, (256, 256), 0) == lax.broadcasted_iota(jnp.int32, (256, 256), 1)
     eye_ref[...] = eye.astype(f32).astype(bf16)
     stage[...] = jnp.zeros_like(stage)
+    lane = lax.broadcasted_iota(jnp.int32, (256, 128), 0)
+    pick_last[...] = jnp.where(lane == width, 8.0, jnp.where(lane == width + 1, 1.0, 0.0)).astype(bf16)
+    for start in range(0, events, 128):
+        time_all[start : start + 128, :] = jnp.broadcast_to(
+            time_ref[:, start : start + 128].astype(f32), (128, 128)
+        ).T
 
     def cand_body(o, unused):
         def fill(i, unused):
@@ -491,40 +573,6 @@
     def lanes(c, size=LANES):
         return pl.ds(pl.multiple_of(c * size, size), size)
 
-    def gru_body(c, unused):
-        cs = lanes(c)
-        node = lax.broadcasted_iota(jnp.int32, (mem3_ref.shape[1], LANES), 0)
-        onehot = (node == src_ref[:, cs]).astype(f32).astype(bf16)
-        parts = nn(mem3_ref[...], onehot)
-        mem = parts[:rows] + parts[rows : 2 * rows] + parts[2 * rows :]
-        mem_src[:, cs] = mem
-        delta = time_ref[:, cs].astype(f32) - 8.0 * mem[width : width + 1] - mem[width + 1 : width + 2]
-        stage[0:width, :] = mem[0:width]
-        stage[width : width + edge, :] = edge_ref[:, cs].astype(f32)
-        stage[width + edge : width + edge + time_width, :] = cos_rows(delta, high, low)[0:time_width]
-        x = stage[...].astype(bf16)
-        x_msg[:, cs] = x
-        m_low = mem.astype(bf16)
-        mem_low[:, cs] = m_low
-        pre = nn(wmsg_ref[...], x)
-        pre_msg[:, cs] = pre
-        hid = (pre * jax.nn.sigmoid(pre)).astype(bf16)
-        hidden[:, cs] = hid
-        r = jax.nn.sigmoid(nn(w("g0r"), hid) + nn(w("g1r"), m_low))
-        reset_gate[:, cs] = r
-        u = jax.nn.sigmoid(nn(w("g0z"), hid) + nn(w("g1z"), m_low))
-        update[:, cs] = u
-        gn = nn(w("g1n"), m_low)
-        gate_n[:, cs] = gn
-        cand = jnp.tanh(nn(w("g0n"), hid) + r * gn)
-        cand_act[:, cs] = cand
-        fresh = ((1.0 - u) * cand + u * mem).astype(bf16)
-        fresh_low[:, cs] = fresh
-        queries[:, cs] = nn(w("s0t"), fresh).astype(bf16)
-        return unused
-
-    lax.fori_loop(0, chunks, gru_body, 0)
-
     def fetch(buf, j, i):
         base = ((lax.div(j, picks) * (events // 128) + i) * picks + lax.rem(j, picks)) * 128
         gather(buf, lambda k: ids_ref[base + k], i * 128)
@@ -532,12 +580,10 @@
     def slot_chunk(buf, j, c):
         cs = lanes(c)
         x = gathered(buf, c * LANES, LANES)
+        delta = time_all[cs, :] - nn(x, pick_last[...])
+        x = jnp.concatenate([x, cos_rows(delta, high_row, low_row).astype(bf16)], 1)
         x_all[j, cs, :] = x
-        kv = nt(wkv1_ref[...], x)
-        delta = time_ref[:, cs].astype(f32) - kv[width : width + 1]
-        t_low = cos_rows(delta, high, low).astype(bf16)
-        t_all[j, :, cs] = t_low
-        kv = (kv + nn(wkv2_ref[...], t_low)).astype(bf16)
+        kv = nt(wkv_ref[...], x).astype(bf16)
         if keep_kv:
             kv_all[j, :, cs] = kv
         s0, s1 = heads.sums(kv[:rows].astype(f32) * queries[:, cs].astype(f32))
@@ -576,7 +622,7 @@
     def kv_of(j, cs, part):
         if keep_kv:
             return kv_all[j, part, cs]
-        return (nt(wkv1_ref[part, :], x_all[j, cs, :]) + nn(wkv2_ref[part, :], t_all[j, :, cs])).astype(bf16)
+        return nt(wkv_ref[part, :], x_all[j, cs, :]).astype(bf16)
 
     def att_body(c, unused):
         cs = lanes(c, 128)
@@ -697,7 +743,6 @@
 
     attended[...] = jnp.zeros_like(attended)
     gkv_m[...] = jnp.zeros_like(gkv_m)
-    gkv_t[...] = jnp.zeros_like(gkv_t)
 
     def slot_back(i, unused):
         for side in range(2):
@@ -715,16 +760,16 @@
                 gslab[side, rows:2*rows, cs] = heads.scale(ga, p0, p1).astype(bf16)
             both = gslab[side, 0 : 2 * rows, :]
             gkv_m[...] += nn(both, x_all[j])
-            gkv_t[...] += nt(both, t_all[j])
         return unused
 
     lax.fori_loop(0, slots // 2, slot_back, 0)
-    gm = gkv_m[...].T
-    gt = gkv_t[...].T
-    both = [jnp.concatenate([g[:depth, :width], g[:depth, rows : rows + width]], 1)
-            for g, depth in ((gm, width), (gt, time_width))]
+    gkv = gkv_m[...].T
+    both = [jnp.concatenate([g[:, :width], g[:, rows : rows + width]], 1)
+            for g in (gkv[:width], gkv[256 : 256 + time_width])]
     layout.put(grad_ref, "kv", jnp.concatenate(both, 0))
 
+    for copy in loads:
+        copy.wait()
     def gru_back(c, unused):
         cs = lanes(c)
         gq = attended[:, cs].astype(bf16)
@@ -757,42 +802,47 @@
 
 def main(layout, keep_kv, width, head_dim, cand_width, args):
     events = args[4].shape[1]
-    slots = args[8].shape[0] * args[8].shape[1]
-    wide = args[12].shape[1]
-    times = args[15].shape[1]
+    slots = args[7].shape[0] * args[7].shape[1]
+    late = args[16:]
     rows = pad_to(width, 16)
     cands = args[1].shape[0]
     smem = pl.BlockSpec(memory_space=pltpu.SMEM)
     vmem = pl.BlockSpec(memory_space=pltpu.VMEM)
+    hbm = pl.BlockSpec(memory_space=pl.ANY)
     low = lambda *shape: pltpu.VMEM(shape, bf16)
     full = lambda *shape: pltpu.VMEM(shape, f32)
     return pl.pallas_call(
         partial(main_kernel, (width, head_dim, keep_kv, cand_width, layout)),
         out_shape=jax.ShapeDtypeStruct((layout.total, 128), f32),
-        in_specs=[smem, smem] + [vmem] * (len(args) - 2),
+        in_specs=[smem, smem] + [vmem] * 14 + [hbm] * len(late),
         out_specs=vmem,
-        scratch_shapes=[
+        scratch_shapes=[pltpu.VMEM(x.shape, x.dtype) for x in late]
+        + [
             full(2 * events, 128),
             full(2 * events, 128),
-            low(slots, events, 256),
-            low(slots, times, events),
+            low(slots, events, 384),
+            full(events, 128),
             low(slots if keep_kv else 1, 2 * rows if keep_kv else 16, events),
             full(slots, 8, events),
             low(cands, 256),
             low(max(3 * rows, cand_width), events),
             low(256, 256),
-            low(2, cand_width, events),
-            full(wide, LANES),
-            low(wide, events),
-        ]
-        + [low(rows, events)] * 4
-        + [low(2 * rows, events)]
-        + [low(rows, events)] * 2
-        + [low(events, rows)]
-        + [full(rows, events)] * 6
-        + [low(rows, events)]
-        + [full(rows, events)] * 3
-        + [low(rows, events), full(2 * rows, 256), full(2 * rows, times), full(8, events)],
+            low(2, max(2 * rows, cand_width), events),
+            full(2 * rows, LANES),
+            low(rows, events),
+            low(2 * rows, events),
+            low(rows, events),
+            low(rows, events),
+            low(events, rows),
+            full(rows, events),
+            full(rows, events),
+            full(rows, events),
+            low(rows, events),
+            full(2 * rows, 384),
+            low(256, 128),
+            full(8, events),
+            pltpu.SemaphoreType.DMA((len(late),)),
+        ],
         compiler_params=pltpu.CompilerParams(vmem_limit_bytes=63 * 2**20),
         name="train",
     )(*args)
@@ -930,9 +980,12 @@
     )(packed)
 
 
-def update_kernel(layout, step_rate, grad_ref, *refs):
-    sources, targets, held, laid = refs[:15], refs[15:30], refs[30:45], refs[45:47]
-    in_sem, out_sem = refs[47:]
+def update_kernel(layout, step_rate, grad_ref, pos_ref, *refs):
+    sources, targets, loss_ref, count_ref = refs[:15], refs[15:30], refs[30], refs[31]
+    held, laid = refs[32:47], refs[47:49]
+    in_sem, out_sem = refs[49:]
+    loss_ref[...] = grad_ref[layout.loss : layout.loss + 1, 0:1]
+    count_ref[...] = pos_ref[0:1, 0:1]
     arrive = [pltpu.make_async_copy(sources[i], held[i], in_sem.at[i]) for i in range(15)]
     leave = [pltpu.make_async_copy(held[i], targets[(i + 5) % 10 if i < 10 else i], out_sem.at[i]) for i in range(15)]
     order = (1, 2, 0, 3, 4)
@@ -967,19 +1020,20 @@
         copy.wait()
 
 
-def update_all(layout, step_rate, packed, params):
+def update_all(layout, step_rate, packed, positives, params):
     vmem = pl.BlockSpec(memory_space=pltpu.VMEM)
     hbm = pl.BlockSpec(memory_space=pl.ANY)
     buffers = [pltpu.VMEM(p.shape, f32) for p in params]
     return pl.pallas_call(
         partial(update_kernel, layout, step_rate),
-        out_shape=tuple(jax.ShapeDtypeStruct(p.shape, f32) for p in params[5:10] + params[:5] + params[10:]),
-        in_specs=[vmem] + [hbm] * 15,
-        out_specs=(hbm,) * 15,
+        out_shape=tuple(jax.ShapeDtypeStruct(p.shape, f32) for p in params[5:10] + params[:5] + params[10:])
+        + (jax.ShapeDtypeStruct((1, 1), f32),) * 2,
+        in_specs=[vmem] * 2 + [hbm] * 15,
+        out_specs=(hbm,) * 15 + (vmem,) * 2,
         scratch_shapes=buffers + buffers[1:3] + [pltpu.SemaphoreType.DMA((15,))] * 2,
         compiler_params=pltpu.CompilerParams(vmem_limit_bytes=63 * 2**20),
         name="update",
-    )(packed, *params)
+    )(packed, positives, *params)
 
 
 def turned(arrays):
@@ -999,32 +1053,32 @@
     nodes, width = memory.shape
     head_dim = width // HEADS
     time_width = w_key_value.shape[0] - width
-    times = pad_to(time_width, 16)
+    columns = time_columns(time_width, 128)
     layout = Layout(
         width, w_msg.shape[0], w_output.shape[0], w_gru.shape[2], *w_key_value.shape, 8 * own * batch
     )
     weights = turned((w_msg, w_gru, w_square, w_key_value, w_output))
     time_row, mask_row, src_row, target_row = (x[None, :] for x in (event_time, event_mask, src_local, target))
-    table, cand_ids, flat_ids, positives, newest, mem3, *low_weights = exchange(
+    table, cand_ids, flat_ids, positives, newest, *handed = exchange(
         own, batch,
         (memory.T, last_update[None, :], dest_local[None, :], time_row, mask_row, src_row,
-         nbr_owner.T, nbr_ids.transpose(2, 1, 0)) + weights,
+         nbr_owner.T, nbr_ids.transpose(2, 1, 0), jnp.asarray(columns)) + weights + (edge_feat.T,),
     )
     packed = main(
         layout, own * nodes <= 16384, width, head_dim, dest_local.shape[0],
-        (flat_ids.reshape(-1), cand_ids.reshape(-1), positives, table, time_row, mask_row, src_row, target_row,
-         nbr_mask.transpose(2, 1, 0), mem3, edge_feat.T, *low_weights, jnp.asarray(time_columns(time_width, times))),
+        (flat_ids.reshape(-1), cand_ids.reshape(-1), positives, table, time_row, mask_row, target_row,
+         nbr_mask.transpose(2, 1, 0), *handed[:5], jnp.asarray(columns.T[:8]), *handed[5:]),
     )
     summed = reduce_all(own, batch, packed)
     step_rate = rate_coef * math.sqrt(events * own * batch)
-    states = update_all(
-        layout, step_rate, summed,
+    *states, loss, count = update_all(
+        layout, step_rate, summed, positives,
         weights
         + turned((mom_msg, mom_gru, mom_square, mom_key_value, mom_output))
         + turned((avg_msg, avg_gru, avg_square, avg_key_value, avg_output)),
     )
     states = [x for i in range(3) for x in turned(states[5 * i : 5 * i + 5])]
-    return (summed[layout.loss, 0], positives[0, 0], newest.reshape(-1), *states)
+    return (loss.reshape(()), count.reshape(()), newest.reshape(-1), *states)
 
 
 def solution(mesh):

time: 175 us -> 165 us (0.943)
  Pallas kernels: 171 us -> 164 us
  local copies, waits for them, and re-layouts: 2.98 us -> 0.6 us
    pallas_call x1, Pallas kernels: 87.9 us -> 82.1 us  [main(): pl.pallas_call(partial(main_kernel, (width, head_dim, keep_kv, cand_width...]
    pallas_call x1, Pallas kernels: 32 us -> 29.6 us  [exchange(): pl.pallas_call(partial(exchange_kernel, own, batch), out_shape=(jax.Shape...]
    slice x2 -> x0, local copies, waits for them, and re-layouts: 2.38 us -> none  [the longest x1 1.19 us: local(): summed[layout.loss, 0]]
where the time goes in v4:
time: 165 us
  Pallas kernels  164 us (99%)
    pallas_call x1, Pallas kernels, main(): pl.pallas_call(partial(main_kernel, (width, head_dim, keep_kv, cand_width...  82.1 us
    pallas_call x1, Pallas kernels, reduce_all(): pl.pallas_call(partial(reduce_kernel, own, batch, streams), out_shape=jax...  44.2 us
    pallas_call x1, Pallas kernels, exchange(): pl.pallas_call(partial(exchange_kernel, own, batch), out_shape=(jax.Shape...  29.6 us
    pallas_call x1, Pallas kernels, update_all(): pl.pallas_call(partial(update_kernel, layout, step_rate), out_shape=tuple...  7.82 us

profile of v4, /device:TPU:0, one launch (start us, length us, event | category | flops | bytes accessed | tf_op | source)
XLA Modules:
  0.0 164.9 jit_solution(15174738561907688974)
XLA Ops:
  0.7 29.6 %exchange.1 = (bf16[8192,2,128]{2,1,0:T(2,128)(2,1)}, s32[32,128]{1,0:T(8,128)}, s32[160,128]{1,0:T(8,128)}, f32[8,128]{1,0:T(8,128)}, s32[1,1024]{1,0:T(1,128)}...) custom-call(f32[172,1024]{1,0:T(8,128)} %bitcast.50, ...), custom_call_target="tpu_custom_call" | custom-call | tf_op jit(solution)/shard_map/exchange/pallas_call | solution.py:406
  30.2 82.1 %train.1.grad_ref = f32[4608,128]{1,0:T(8,128)} custom-call(s32[20480]{0:T(1024)} %bitcast.60, s32[4096]{0:T(1024)} %bitcast.62, f32[8,128]{1,0:T(8,128)} %get-tuple-element.58.pos_ref, bf16[8192,2,128]{2,1,0:T(2,128)(2,1)} %get-tuple-element.59.table_ref, s32[1,1024]{1,0:T(1,128)} %bitcast.64, s32[1,1024]{1,0:T(1,128)} %bitcast.66, s32[1,1024]{1,0:T(1,128)} %bitcast.70, ...), custom_call_target="tpu_custom_call" | custom-call | tf_op jit(solution)/shard_map/train/pallas_call | solution.py:814
  112.3 44.2 %reduce.1.grad_ref = f32[4608,128]{1,0:T(8,128)} custom-call(f32[4608,128]{1,0:T(8,128)} %train.1.grad_ref), custom_call_target="tpu_custom_call" | custom-call | tf_op jit(solution)/shard_map/reduce/pallas_call | solution.py:965
  156.5 0.0 copy-start
  156.5 7.8 %update.1 = (f32[172,444]{1,0:T(8,128)}, f32[172,2,516]{2,1,0:T(2,128)}, f32[172,4,172]{2,1,0:T(4,128)}, f32[272,344]{1,0:T(8,128)}, f32[172,344]{1,0:T(8,128)},...) custom-call(f32[4608,128]{1,0:T(8,128)} %reduce.1.grad_ref, ...), custom_call_target="tpu_custom_call" | custom-call | tf_op jit(solution)/shard_map/update/pallas_call | solution.py:1027
  164.3 0.0 copy-done
  164.3 0.6 copy.47
Async XLA Ops:
  156.5 7.8 %copy-start = (s32[1,1024]{1,0:T(1,128)S(1)}, s32[1,1024]{1,0:T(1,128)}, u32[]{:S(2)}) copy-start(s32[1,1024]{1,0:T(1,128)} %get-tuple-element.78) | copy-start | bytes 12292

commit v5 on v4

--- a/solution.py
+++ b/solution.py
@@ -536,8 +536,9 @@
 
     def gather(buf, read_id, at):
         got = [table_ref[read_id(k)] for k in range(128)]
-        for k in range(128):
-            buf[pl.ds(pl.multiple_of(2 * at, 256) + 2 * k, 2), :] = got[k].astype(f32)
+        for k in range(0, 128, 2):
+            pair = jnp.concatenate([got[k].astype(f32), got[k + 1].astype(f32)], 0)
+            buf[pl.ds(pl.multiple_of(2 * at, 256) + 2 * k, 4), :] = pair
 
     def gathered(buf, start, count):
         base = pl.multiple_of(2 * start, 2 * count)
@@ -848,29 +849,55 @@
     )(*args)
 
 
-def reduce_kernel(own, batch, streams, grad_ref, out_ref, acc, recv, send_sem, recv_sem):
+def reduce_kernel(own, batch, streams, grad_ref, out_ref, acc, recv, local_sem, send_sem, recv_sem):
     place = {"own": lax.axis_index("own"), "batch": lax.axis_index("batch")}
-    rounds = len(streams[0][2])
-
-    def peers(axis, bit):
-        if axis == "own":
-            return [(place["batch"], flip_bit(place["own"], bit))]
-        return [(lax.rem(place["batch"] + d, batch), place["own"]) for d in range(1, batch)]
-
+
+    digits = [lax.div(place["own"], 1 << b) % 2 for b in range(own.bit_length() - 1)]
+
+    def parts(bits):
+        if not bits:
+            return batch, place["batch"]
+        return 1 << len(bits), sum(digits[b] * (1 << i) for i, b in enumerate(bits))
+
+    def peers(bits):
+        if not bits:
+            for d in range(1, batch):
+                there = lax.rem(place["batch"] + d, batch)
+                yield (there, place["own"]), there
+            return
+        for pattern in range(1, 1 << len(bits)):
+            there, at = place["own"], 0
+            for i, b in enumerate(bits):
+                digit = digits[b]
+                if pattern >> i & 1:
+                    there, digit = there + (1 << b) * (1 - 2 * digit), 1 - digit
+                at = at + digit * (1 << i)
+            yield (place["batch"], there), at
+
+    load = pltpu.make_async_copy(grad_ref, acc, local_sem)
+    load.start()
     barrier = pltpu.get_barrier_semaphore()
-    signals = 0
-    for axis, bit in streams[0][2]:
-        for peer in peers(axis, bit):
-            pl.semaphore_signal(barrier, inc=1, device_id=peer, device_id_type=MESH)
-            signals += 1
-    pl.semaphore_wait(barrier, signals)
+    devices = {}
+    for order in [order for start, size, order in streams]:
+        for bits in order:
+            devices.setdefault(tuple(sorted(bits)), [device for device, there in peers(sorted(bits))])
+    greeted = [device for bits in devices if all(set(bits) >= set(other) or not set(bits) & set(other) for other in devices)
+               for device in devices[bits]]
+    for device in greeted:
+        pl.semaphore_signal(barrier, inc=1, device_id=device, device_id_type=MESH)
+    pl.semaphore_wait(barrier, len(greeted))
+    load.wait()
 
     sent = []
+    longest = max(len(order) for start, size, order in streams)
 
     class Stream:
         def __init__(self, index, start, size, order):
             self.index, self.base, self.size, self.inner, self.order = index, start, size, start, order
             self.copies = []
+            self.slots = [0]
+            for bits in order:
+                self.slots.append(self.slots[-1] + parts(bits)[0] - 1)
 
         def copy(self, source, target, peer, slot):
             copy = pltpu.make_async_remote_copy(
@@ -882,31 +909,22 @@
             self.copies.append(copy)
             sent.append(copy)
 
-        def parts(self, axis, bit):
-            if axis == "own":
-                return 2, lax.div(place["own"], 1 << bit) % 2
-            return batch, place["batch"]
-
         def scatter(self, step):
-            axis, bit = self.order[step]
-            count, mine = self.parts(axis, bit)
+            count, mine = parts(self.order[step])
             piece = self.size // count
-            source = grad_ref if step == 0 else acc
-            for d, peer in enumerate(peers(axis, bit), 1):
-                theirs = 1 - mine if axis == "own" else peer[0]
+            for d, (peer, theirs) in enumerate(peers(self.order[step]), 1):
                 away = pl.multiple_of(self.base + theirs * piece, 8)
                 self.copy(
-                    source.at[pl.ds(away, piece), :], recv.at[pl.ds(self.inner + (d - 1) * piece, piece), :],
-                    peer, step * (batch - 1) + d - 1,
+                    acc.at[pl.ds(away, piece), :], recv.at[pl.ds(self.inner + (d - 1) * piece, piece), :],
+                    peer, self.slots[step] + d - 1,
                 )
             self.base = pl.multiple_of(self.base + mine * piece, 8)
             self.size = piece
 
         def add(self, step):
-            source = grad_ref if step == 0 else acc
-            target = out_ref if step == rounds - 1 else acc
+            target = out_ref if step == len(self.order) - 1 else acc
             part = pl.ds(self.base, self.size)
-            total = source[part, :]
+            total = acc[part, :]
             for copy in self.copies:
                 copy.wait_recv()
                 total = total + recv[pl.ds(self.inner, self.size), :]
@@ -915,11 +933,10 @@
             self.copies = []
 
         def gather(self, step):
-            axis, bit = self.order[step]
-            count, mine = self.parts(axis, bit)
+            count, mine = parts(self.order[step])
             part = pl.ds(self.base, self.size)
-            for d, peer in enumerate(peers(axis, bit), 1):
-                self.copy(out_ref.at[part, :], out_ref.at[part, :], peer, (rounds + step) * (batch - 1) + d - 1)
+            for d, (peer, theirs) in enumerate(peers(self.order[step]), 1):
+                self.copy(out_ref.at[part, :], out_ref.at[part, :], peer, self.slots[-1] + self.slots[step] + d - 1)
             self.base = pl.multiple_of(self.base - mine * self.size, 8)
             self.size *= count
 
@@ -929,11 +946,12 @@
             self.copies = []
 
     flows = [Stream(index, *stream) for index, stream in enumerate(streams)]
-    for step in range(2 * rounds + 1):
+    for step in range(2 * longest + 1):
         for flow in flows:
+            rounds = len(flow.order)
             if 0 < step <= rounds:
                 flow.add(step - 1)
-            elif step > rounds:
+            elif rounds < step <= 2 * rounds:
                 flow.gathered()
             if step < rounds:
                 flow.scatter(step)
@@ -947,29 +965,27 @@
     total = packed.shape[0]
     own_bits = own.bit_length() - 1
     fold = 8 * own * batch
-    rest = [("own", b) for b in range(1, own_bits)]
-    cut = len(rest) // 2
-    axes = [rest[:cut], rest[cut:], [("batch", 0)]]
-    blocks = total // fold
-    halves = 1
+    core, xs, ys, zs = (0,), tuple(range(1, (own_bits + 1) // 2)), tuple(range((own_bits + 1) // 2, own_bits)), ()
+    plan = ((6, (core, xs + ys, zs)), (3, (core, zs, xs + ys)), (6, (core, ys + xs, zs)), (3, (core, zs, ys + xs)))
     streams = []
     start = 0
-    for index in range(3 * halves):
-        size = (blocks + 3 * halves - 1 - index) // (3 * halves) * fold
-        turn = index % 3
-        order = [("own", 0)] + [bit for part in axes[turn:] + axes[:turn] for bit in part]
+    blocks = total // fold
+    shares = sum(share for share, order in plan)
+    for index, (share, order) in enumerate(plan):
+        size = total - start if index == len(plan) - 1 else blocks * share // shares * fold
         if size:
             streams.append((start, size, order))
-            start += size
-    count = 2 * len(streams[0][2]) * (batch - 1)
+        start += size
+    count = 2 * (own * batch)
     return pl.pallas_call(
         partial(reduce_kernel, own, batch, streams),
         out_shape=jax.ShapeDtypeStruct(packed.shape, f32),
-        in_specs=[pl.BlockSpec(memory_space=pltpu.VMEM)],
+        in_specs=[pl.BlockSpec(memory_space=pl.ANY)],
         out_specs=pl.BlockSpec(memory_space=pltpu.VMEM),
         scratch_shapes=[
             pltpu.VMEM(packed.shape, f32),
             pltpu.VMEM(packed.shape, f32),
+            pltpu.SemaphoreType.DMA,
             pltpu.SemaphoreType.DMA((len(streams), count)),
             pltpu.SemaphoreType.DMA((len(streams), count)),
         ],

time: 165 us -> 156 us (0.945)
  Pallas kernels: 164 us -> 155 us
    pallas_call x1, Pallas kernels: 44.2 us -> 37.8 us  [reduce_all(): pl.pallas_call(partial(reduce_kernel, own, batch, streams), out_shape=jax...]
    pallas_call x1, Pallas kernels: 82.1 us -> 79.3 us  [main(): pl.pallas_call(partial(main_kernel, (width, head_dim, keep_kv, cand_width...]
where the time goes in v5:
time: 156 us
  Pallas kernels  155 us (99%)
    pallas_call x1, Pallas kernels, main(): pl.pallas_call(partial(main_kernel, (width, head_dim, keep_kv, cand_width...  79.3 us
    pallas_call x1, Pallas kernels, reduce_all(): pl.pallas_call(partial(reduce_kernel, own, batch, streams), out_shape=jax...  37.8 us
    pallas_call x1, Pallas kernels, exchange(): pl.pallas_call(partial(exchange_kernel, own, batch), out_shape=(jax.Shape...  29.6 us
    pallas_call x1, Pallas kernels, update_all(): pl.pallas_call(partial(update_kernel, layout, step_rate), out_shape=tuple...  7.82 us

profile of v5, /device:TPU:0, one launch (start us, length us, event | category | flops | bytes accessed | tf_op | source)
XLA Modules:
  0.0 155.9 jit_solution(9681089754290954930)
XLA Ops:
  0.7 29.6 %exchange.1 = (bf16[8192,2,128]{2,1,0:T(2,128)(2,1)}, s32[32,128]{1,0:T(8,128)}, s32[160,128]{1,0:T(8,128)}, f32[8,128]{1,0:T(8,128)}, s32[1,1024]{1,0:T(1,128)}...) custom-call(f32[172,1024]{1,0:T(8,128)} %bitcast.50, ...), custom_call_target="tpu_custom_call" | custom-call | tf_op jit(solution)/shard_map/exchange/pallas_call | solution.py:406
  30.2 79.3 %train.1.grad_ref = f32[4608,128]{1,0:T(8,128)} custom-call(s32[20480]{0:T(1024)} %bitcast.60, s32[4096]{0:T(1024)} %bitcast.62, f32[8,128]{1,0:T(8,128)} %get-tuple-element.58.pos_ref, bf16[8192,2,128]{2,1,0:T(2,128)(2,1)} %get-tuple-element.59.table_ref, s32[1,1024]{1,0:T(1,128)} %bitcast.64, s32[1,1024]{1,0:T(1,128)} %bitcast.66, s32[1,1024]{1,0:T(1,128)} %bitcast.70, ...), custom_call_target="tpu_custom_call" | custom-call | tf_op jit(solution)/shard_map/train/pallas_call | solution.py:815
  109.6 37.8 %reduce.1.grad_ref = f32[4608,128]{1,0:T(8,128)} custom-call(f32[4608,128]{1,0:T(8,128)} %train.1.grad_ref), custom_call_target="tpu_custom_call" | custom-call | tf_op jit(solution)/shard_map/reduce/pallas_call | solution.py:980
  147.4 0.0 copy-start
  147.4 7.8 %update.1 = (f32[172,444]{1,0:T(8,128)}, f32[172,2,516]{2,1,0:T(2,128)}, f32[172,4,172]{2,1,0:T(4,128)}, f32[272,344]{1,0:T(8,128)}, f32[172,344]{1,0:T(8,128)},...) custom-call(f32[4608,128]{1,0:T(8,128)} %reduce.1.grad_ref, ...), custom_call_target="tpu_custom_call" | custom-call | tf_op jit(solution)/shard_map/update/pallas_call | solution.py:1043
  155.3 0.0 copy-done
  155.3 0.6 copy.47
Async XLA Ops:
  147.4 7.8 %copy-start = (s32[1,1024]{1,0:T(1,128)S(1)}, s32[1,1024]{1,0:T(1,128)}, u32[]{:S(2)}) copy-start(s32[1,1024]{1,0:T(1,128)} %get-tuple-element.78) | copy-start | bytes 12292

commit v6 on v5

--- a/solution.py
+++ b/solution.py
@@ -424,7 +424,7 @@
             pltpu.VMEM((wide, LANES), f32),
             pltpu.VMEM((nodes, 2, 128), bf16),
             pltpu.VMEM((256, nodes), f32),
-            pltpu.VMEM((2 * nodes, 128), f32),
+            pltpu.VMEM((2 * nodes + 64, 128), f32),
             pltpu.VMEM((rows, rows), f32),
             pltpu.VMEM((rows, wide), f32),
             pltpu.VMEM((2 * rows, 384), f32),
@@ -652,7 +652,7 @@
         emb_rows[cs, :] = nt(eye_ref[...], e).astype(bf16)
         return unused
 
-    lax.fori_loop(0, chunks, out_body, 0, unroll=2)
+    lax.fori_loop(0, chunks, out_body, 0, unroll=4)
 
     def row_init(c, unused):
         cs = lanes(c)
@@ -737,7 +737,7 @@
         rows_ref[6:7, cs] = d1
         return unused
 
-    lax.fori_loop(0, chunks, out_back, 0, unroll=2)
+    lax.fori_loop(0, chunks, out_back, 0, unroll=4)
     layout.put(grad_ref, "square2", nt(hid_out[...], slab[r0, :]))
     layout.put(grad_ref, "out", nt(slab[r1, :], x_out[...]))
     layout.put(grad_ref, "square1", nt(att_low[...], slab[r2, :]))
@@ -792,7 +792,7 @@
         att_low[:, cs] = (back * (sig * (1.0 + pre * (1.0 - sig)))).astype(bf16)
         return unused
 
-    lax.fori_loop(0, chunks, gru_back, 0, unroll=2)
+    lax.fori_loop(0, chunks, gru_back, 0, unroll=4)
     layout.put(grad_ref, "square0", nt(fresh_low[...], slab[r0, :]))
     for index, (left, last) in enumerate(((hidden, x_out[0:rows, :]), (mem_low, hid_out[...]))):
         left = left[...]
@@ -819,8 +819,8 @@
         out_specs=vmem,
         scratch_shapes=[pltpu.VMEM(x.shape, x.dtype) for x in late]
         + [
-            full(2 * events, 128),
-            full(2 * events, 128),
+            full(2 * events + 64, 128),
+            full(2 * events + 64, 128),
             low(slots, events, 384),
             full(events, 128),
             low(slots if keep_kv else 1, 2 * rows if keep_kv else 16, events),

time: 156 us -> 154 us (0.987)
  Pallas kernels: 155 us -> 153 us
    pallas_call x1, Pallas kernels: 79.3 us -> 77.7 us  [main(): pl.pallas_call(partial(main_kernel, (width, head_dim, keep_kv, cand_width...]
where the time goes in v6:
time: 154 us
  Pallas kernels  153 us (99%)
    pallas_call x1, Pallas kernels, main(): pl.pallas_call(partial(main_kernel, (width, head_dim, keep_kv, cand_width...  77.7 us
    pallas_call x1, Pallas kernels, reduce_all(): pl.pallas_call(partial(reduce_kernel, own, batch, streams), out_shape=jax...  37.9 us
    pallas_call x1, Pallas kernels, exchange(): pl.pallas_call(partial(exchange_kernel, own, batch), out_shape=(jax.Shape...  29.6 us
    pallas_call x1, Pallas kernels, update_all(): pl.pallas_call(partial(update_kernel, layout, step_rate), out_shape=tuple...  7.82 us

profile of v6, /device:TPU:0, one launch (start us, length us, event | category | flops | bytes accessed | tf_op | source)
XLA Modules:
  0.0 154.3 jit_solution(1942556782315139485)
XLA Ops:
  0.7 29.6 %exchange.1 = (bf16[8192,2,128]{2,1,0:T(2,128)(2,1)}, s32[32,128]{1,0:T(8,128)}, s32[160,128]{1,0:T(8,128)}, f32[8,128]{1,0:T(8,128)}, s32[1,1024]{1,0:T(1,128)}...) custom-call(f32[172,1024]{1,0:T(8,128)} %bitcast.50, ...), custom_call_target="tpu_custom_call" | custom-call | tf_op jit(solution)/shard_map/exchange/pallas_call | solution.py:406
  30.2 77.7 %train.1.grad_ref = f32[4608,128]{1,0:T(8,128)} custom-call(s32[20480]{0:T(1024)} %bitcast.60, s32[4096]{0:T(1024)} %bitcast.62, f32[8,128]{1,0:T(8,128)} %get-tuple-element.58.pos_ref, bf16[8192,2,128]{2,1,0:T(2,128)(2,1)} %get-tuple-element.59.table_ref, s32[1,1024]{1,0:T(1,128)} %bitcast.64, s32[1,1024]{1,0:T(1,128)} %bitcast.66, s32[1,1024]{1,0:T(1,128)} %bitcast.70, ...), custom_call_target="tpu_custom_call" | custom-call | tf_op jit(solution)/shard_map/train/pallas_call | solution.py:815
  107.9 37.9 %reduce.1.grad_ref = f32[4608,128]{1,0:T(8,128)} custom-call(f32[4608,128]{1,0:T(8,128)} %train.1.grad_ref), custom_call_target="tpu_custom_call" | custom-call | tf_op jit(solution)/shard_map/reduce/pallas_call | solution.py:980
  145.8 0.0 copy-start
  145.8 7.8 %update.1 = (f32[172,444]{1,0:T(8,128)}, f32[172,2,516]{2,1,0:T(2,128)}, f32[172,4,172]{2,1,0:T(4,128)}, f32[272,344]{1,0:T(8,128)}, f32[172,344]{1,0:T(8,128)},...) custom-call(f32[4608,128]{1,0:T(8,128)} %reduce.1.grad_ref, ...), custom_call_target="tpu_custom_call" | custom-call | tf_op jit(solution)/shard_map/update/pallas_call | solution.py:1043
  153.7 0.0 copy-done
  153.7 0.6 copy.47
Async XLA Ops:
  145.8 7.8 %copy-start = (s32[1,1024]{1,0:T(1,128)S(1)}, s32[1,1024]{1,0:T(1,128)}, u32[]{:S(2)}) copy-start(s32[1,1024]{1,0:T(1,128)} %get-tuple-element.78) | copy-start | bytes 12292

commit v7 on v6

--- a/solution.py
+++ b/solution.py
@@ -626,8 +626,8 @@
         return nt(wkv_ref[part, :], x_all[j, cs, :]).astype(bf16)
 
     def att_body(c, unused):
-        cs = lanes(c, 128)
-        total = jnp.zeros((rows, 128), f32)
+        cs = lanes(c, 256)
+        total = jnp.zeros((rows, 256), f32)
         for j in range(slots):
             v = kv_of(j, cs, slice(rows, 2 * rows)).astype(f32)
             total = total + heads.scale(v, score[j, 0:1, cs], score[j, 1:2, cs])
@@ -635,7 +635,7 @@
         att_low[:, cs] = total.astype(bf16)
         return unused
 
-    lax.fori_loop(0, events // 128, att_body, 0)
+    lax.fori_loop(0, events // 256, att_body, 0)
 
     def out_body(c, unused):
         cs = lanes(c)
@@ -671,8 +671,8 @@
         for side in range(2):
             o = 2 * i + side
             dest = nn(dest_of(o), wd_ref[...]).astype(bf16)
-            for c in range(chunks):
-                cs = lanes(c)
+            for c in range(events // 512):
+                cs = lanes(c, 512)
                 logits = nn(dest, emb[:, cs])
                 old = rows_ref[0:1, cs]
                 top = jnp.maximum(old, jnp.max(logits, 0, keepdims=True))

time: 154 us -> 154 us (level)
  no operation moved by 1% of the time
where the time goes in v7:
time: 154 us
  Pallas kernels  153 us (99%)
    pallas_call x1, Pallas kernels, main(): pl.pallas_call(partial(main_kernel, (width, head_dim, keep_kv, cand_width...  77.2 us
    pallas_call x1, Pallas kernels, reduce_all(): pl.pallas_call(partial(reduce_kernel, own, batch, streams), out_shape=jax...  38.1 us
    pallas_call x1, Pallas kernels, exchange(): pl.pallas_call(partial(exchange_kernel, own, batch), out_shape=(jax.Shape...  29.6 us
    pallas_call x1, Pallas kernels, update_all(): pl.pallas_call(partial(update_kernel, layout, step_rate), out_shape=tuple...  7.82 us

profile of v7, /device:TPU:0, one launch (start us, length us, event | category | flops | bytes accessed | tf_op | source)
XLA Modules:
  0.0 154.0 jit_solution(17436397107086537941)
XLA Ops:
  0.7 29.6 %exchange.1 = (bf16[8192,2,128]{2,1,0:T(2,128)(2,1)}, s32[32,128]{1,0:T(8,128)}, s32[160,128]{1,0:T(8,128)}, f32[8,128]{1,0:T(8,128)}, s32[1,1024]{1,0:T(1,128)}...) custom-call(f32[172,1024]{1,0:T(8,128)} %bitcast.50, ...), custom_call_target="tpu_custom_call" | custom-call | tf_op jit(solution)/shard_map/exchange/pallas_call | solution.py:406
  30.2 77.2 %train.1.grad_ref = f32[4608,128]{1,0:T(8,128)} custom-call(s32[20480]{0:T(1024)} %bitcast.60, s32[4096]{0:T(1024)} %bitcast.62, f32[8,128]{1,0:T(8,128)} %get-tuple-element.58.pos_ref, bf16[8192,2,128]{2,1,0:T(2,128)(2,1)} %get-tuple-element.59.table_ref, s32[1,1024]{1,0:T(1,128)} %bitcast.64, s32[1,1024]{1,0:T(1,128)} %bitcast.66, s32[1,1024]{1,0:T(1,128)} %bitcast.70, ...), custom_call_target="tpu_custom_call" | custom-call | tf_op jit(solution)/shard_map/train/pallas_call | solution.py:815
  107.5 38.1 %reduce.1.grad_ref = f32[4608,128]{1,0:T(8,128)} custom-call(f32[4608,128]{1,0:T(8,128)} %train.1.grad_ref), custom_call_target="tpu_custom_call" | custom-call | tf_op jit(solution)/shard_map/reduce/pallas_call | solution.py:980
  145.6 0.0 copy-start
  145.6 7.8 %update.1 = (f32[172,444]{1,0:T(8,128)}, f32[172,2,516]{2,1,0:T(2,128)}, f32[172,4,172]{2,1,0:T(4,128)}, f32[272,344]{1,0:T(8,128)}, f32[172,344]{1,0:T(8,128)},...) custom-call(f32[4608,128]{1,0:T(8,128)} %reduce.1.grad_ref, ...), custom_call_target="tpu_custom_call" | custom-call | tf_op jit(solution)/shard_map/update/pallas_call | solution.py:1043
  153.4 0.0 copy-done
  153.4 0.6 copy.47
Async XLA Ops:
  145.6 7.8 %copy-start = (s32[1,1024]{1,0:T(1,128)S(1)}, s32[1,1024]{1,0:T(1,128)}, u32[]{:S(2)}) copy-start(s32[1,1024]{1,0:T(1,128)} %get-tuple-element.78) | copy-start | bytes 12292
